TPU v7x, 32 devices: a whole 2x2x4 slice. The times are simulated.
32 devices in a mesh: grp: 2 (over y), lat: 16 (over z, x, core).
Axes of the slice: x: 2, y: 2, z: 4, core: 2. Of those that a mesh axis runs over, the one named last changes fastest.
Arguments:
- state: bfloat16 [128, 72, 128], P(('grp', 'lat')), parts along dimension 0, may hold values from -6 to 6
- tangent: bfloat16 [128, 72, 128], P(('grp', 'lat')), parts along dimension 0, may hold values from -6 to 6
- cotangent: bfloat16 [128, 72, 128], P(('grp', 'lat')), parts along dimension 0, may hold values from -6 to 6
- cubic: bfloat16 [4, 128, 128], replicated, may hold values from -0.25 to 0.25
- w_in: bfloat16 [512, 72], replicated, may hold values from -0.75 to 0.75
- w_out: bfloat16 [72, 512], replicated, may hold values from -0.25 to 0.25
- slots: int32 [4, 64, 4], P('grp', 'lat'), parts along dimension 0, may hold values from 0 to 15, as said below
- sends: int32 [4, 16, 16, 1], P('grp', 'lat'), parts along dimension 0, may hold values from -1 to 3, as said below
Outputs:
- tangent_final: bfloat16 [128, 72, 128], P(('grp', 'lat')), parts along dimension 0
- adjoint_start: float32 [128, 72, 128], P(('grp', 'lat')), parts along dimension 0
- grad_in: float32 [1024, 72], P('grp'), parts along dimension 0
- grad_out: float32 [144, 512], P('grp'), parts along dimension 0
There are 2 independent parts, one for each index of `grp`. A program takes and returns all parts, laid end to end along the dimension named above; an argument that names none is the same for every part. Nothing has to cross between parts.
Inputs may be any that keep to these rules, and one draw needn't show every extreme that they name: On each device d, the 16 entries of one step name distinct slots, 1 from each sender (d + o) mod 16 for every whole o with -8 <= o < 8, and no other slot. `sends`: entry [s, p, d, lane] is the block of sender p that fills slot p + lane of device d at step s; -1 exactly where device d reads nothing from p.
All inputs are finite; a program needn't handle non-finite values.
Results may differ from a plain program's by a relative error of at most 0.013.
Values may be sent and summed in bfloat16 or wider, within the bound.
No kernel may reach another device: no remote copies, remote signals or barrier semaphores. Data moves between devices by JAX's collectives and lax.ppermute only.
A program may use at most 64 MiB of HBM per device.

v0:
```python
import jax
import jax.numpy as jnp
from jax import lax
from jax.sharding import PartitionSpec as P

STEPS = 2


def silu_slope(preact):
    sigma = jax.nn.sigmoid(preact)
    return sigma * (1.0 + preact * (1.0 - sigma))


def pack_blocks(field, table, own_blocks):
    onehot = (
        table.reshape(-1)[:, None] == jnp.arange(own_blocks, dtype=jnp.int32)[None, :]
    ).astype(jnp.bfloat16)
    packed = jnp.dot(onehot, field.reshape(own_blocks, -1), preferred_element_type=jnp.float32)
    return (
        packed.astype(jnp.bfloat16)
        .reshape((table.shape[0] * table.shape[1],) + field.shape[1:])
        .reshape(table.shape + field.shape[1:])
    )


def interpolate(received, slot_rows, cubic):
    flat = received.reshape(-1, received.shape[2], received.shape[3])
    picked = jnp.take(flat, slot_rows, axis=0)
    return jnp.einsum("bkcn,knm->bcm", picked, cubic, preferred_element_type=jnp.float32).astype(
        jnp.bfloat16
    )


def shards(state, tangent, cotangent, cubic, w_in, w_out, slots, sends):
    own_blocks = state.shape[0]
    channels = state.shape[1]
    columns = state.shape[2]
    peer_count = lax.axis_size("lat")
    slot_cap = sends.shape[-1]
    field, pert = (state, tangent)
    saved = []
    for section in range(STEPS):
        table = sends[section, 0]
        send_field = pack_blocks(field, table, own_blocks)
        send_pert = pack_blocks(pert, table, own_blocks)
        recv_field, recv_pert = (
            lax.all_to_all(send_field, "lat", split_axis=0, concat_axis=0, tiled=True),
            lax.all_to_all(send_pert, "lat", split_axis=0, concat_axis=0, tiled=True),
        )
        advected = interpolate(recv_field, slots[section], cubic)
        tadv = interpolate(recv_pert, slots[section], cubic)
        preact = jnp.einsum("hc,bcn->bhn", w_in, advected, preferred_element_type=jnp.float32)
        hidden = jax.nn.silu(preact).astype(jnp.bfloat16)
        field = (
            advected.astype(jnp.float32)
            + jnp.einsum("ch,bhn->bcn", w_out, hidden, preferred_element_type=jnp.float32)
        ).astype(jnp.bfloat16)
        thid = (
            silu_slope(preact)
            * jnp.einsum("hc,bcn->bhn", w_in, tadv, preferred_element_type=jnp.float32)
        ).astype(jnp.bfloat16)
        pert = (
            tadv.astype(jnp.float32)
            + jnp.einsum("ch,bhn->bcn", w_out, thid, preferred_element_type=jnp.float32)
        ).astype(jnp.bfloat16)
        saved.append(advected)
    adjoint_state = cotangent
    grad_in = jnp.zeros((w_in.shape[0], channels), jnp.float32)
    grad_out = jnp.zeros((channels, w_in.shape[0]), jnp.float32)
    gathered_back = None
    for section in reversed(range(STEPS)):
        advected = saved[section]
        table = sends[section, 0]
        preact = jnp.einsum("hc,bcn->bhn", w_in, advected, preferred_element_type=jnp.float32)
        hidden = jax.nn.silu(preact).astype(jnp.bfloat16)
        ghid = (
            silu_slope(preact)
            * jnp.einsum("ch,bcn->bhn", w_out, adjoint_state, preferred_element_type=jnp.float32)
        ).astype(jnp.bfloat16)
        ladv = (
            adjoint_state.astype(jnp.float32)
            + jnp.einsum("hc,bhn->bcn", w_in, ghid, preferred_element_type=jnp.float32)
        ).astype(jnp.bfloat16)
        terms = jnp.einsum("bcm,knm->bkcn", ladv, cubic, preferred_element_type=jnp.float32).astype(
            jnp.bfloat16
        )
        buffer = jnp.zeros((peer_count * slot_cap, channels, columns), jnp.bfloat16)
        buffer = buffer.at[slots[section].reshape(-1)].add(terms.reshape(-1, channels, columns))
        returned = lax.all_to_all(
            buffer.reshape(peer_count, slot_cap, channels, columns),
            "lat",
            split_axis=0,
            concat_axis=0,
            tiled=True,
        )
        onehot = (
            table.reshape(-1)[None, :] == jnp.arange(own_blocks, dtype=jnp.int32)[:, None]
        ).astype(jnp.bfloat16)
        gathered_back = jnp.dot(
            onehot, returned.reshape(peer_count * slot_cap, -1), preferred_element_type=jnp.float32
        ).reshape(own_blocks, channels, columns)
        step_in = jnp.einsum("bhn,bcn->hc", ghid, advected, preferred_element_type=jnp.float32)
        step_out = jnp.einsum(
            "bcn,bhn->ch", adjoint_state, hidden, preferred_element_type=jnp.float32
        )
        grad_in = grad_in + step_in
        grad_out = grad_out + step_out
        adjoint_state = gathered_back.astype(jnp.bfloat16)
    grad_in, grad_out = lax.psum((grad_in, grad_out), "lat")
    return (pert, gathered_back, grad_in, grad_out)


def solution(mesh):
    in_specs = (
        P(("grp", "lat"), None, None),
        P(("grp", "lat"), None, None),
        P(("grp", "lat"), None, None),
        P(),
        P(),
        P(),
        P("grp", "lat", None),
        P("grp", "lat", None, None),
    )
    out_specs = (
        P(("grp", "lat"), None, None),
        P(("grp", "lat"), None, None),
        P("grp", None),
        P("grp", None),
    )
    return jax.shard_map(shards, mesh=mesh, in_specs=in_specs, out_specs=out_specs, check_vma=False)
```

profile of v0, /device:TPU:0, one launch (start us, length us, event | category | flops | bytes accessed | tf_op | source)
XLA Modules:
  0.0 199.7 jit_solution(14291115993726346600)
XLA Ops:
  7.2 0.7 slice_bitcast_fusion.1
  7.9 1.2 fusion.11
  9.1 0.8 copy.79
  9.8 7.5 %all-to-all-start.1 = ((bf16[16,1,72,128]{3,2,1,0:T(8,128)(2,1)}), bf16[16,1,72,128]{3,2,1,0:T(8,128)(2,1)S(1)}, u32[]{:S(2)}, u32[]{:S(2)}) async-start(bf16[16,1,72,128]{3,2,1,0:T(8,128)(2,1)} %bitcast.10), calls=%async_computation.1 | async-start | bytes 589824 | tf_op jit(solution)/shard_map/all_to_all | solution.py:47
  17.7 0.3 fusion.10
  18.0 0.7 copy.77
  18.8 9.1 %all-to-all-done.1 = bf16[16,1,72,128]{3,2,1,0:T(8,128)(2,1)S(1)} async-done(((bf16[16,1,72,128]{3,2,1,0:T(8,128)(2,1)}), bf16[16,1,72,128]{3,2,1,0:T(8,128)(2,1)S(1)}, u32[]{:S(2)}, u32[]{:S(2)}) %all-to-all-start.1) | async-done | bytes 294944 | tf_op jit(solution)/shard_map/all_to_all | solution.py:47
  27.9 3.5 %all-to-all-start = ((bf16[16,1,72,128]{3,2,1,0:T(8,128)(2,1)}), bf16[16,1,72,128]{3,2,1,0:T(8,128)(2,1)S(1)}, u32[]{:S(2)}, u32[]{:S(2)}) async-start(bf16[16,1,72,128]{3,2,1,0:T(8,128)(2,1)} %bitcast.4), calls=%async_computation | async-start | bytes 589824 | tf_op jit(solution)/shard_map/all_to_all | solution.py:48
  31.4 0.6 gather_fusion.1
  32.1 0.3 fusion.25
  32.4 0.6 copy-done.1
  33.0 0.5 multiply_convert_fusion.1
  33.4 0.4 copy-done.3
  34.1 0.3 fusion.13
  34.4 0.7 copy.83
  35.2 6.8 %all-to-all-done = bf16[16,1,72,128]{3,2,1,0:T(8,128)(2,1)S(1)} async-done(((bf16[16,1,72,128]{3,2,1,0:T(8,128)(2,1)}), bf16[16,1,72,128]{3,2,1,0:T(8,128)(2,1)S(1)}, u32[]{:S(2)}, u32[]{:S(2)}) %all-to-all-start) | async-done | bytes 294944 | tf_op jit(solution)/shard_map/all_to_all | solution.py:48
  42.0 3.5 %all-to-all-start.3 = ((bf16[16,1,72,128]{3,2,1,0:T(8,128)(2,1)}), bf16[16,1,72,128]{3,2,1,0:T(8,128)(2,1)S(1)}, u32[]{:S(2)}, u32[]{:S(2)}) async-start(bf16[16,1,72,128]{3,2,1,0:T(8,128)(2,1)} %bitcast.26), calls=%async_computation.3 | async-start | bytes 589824 | tf_op jit(solution)/shard_map/all_to_all | solution.py:47
  45.5 0.6 gather_fusion
  46.1 0.3 fusion.24
  46.4 0.7 fusion.30
  47.4 0.7 copy.81
  48.1 7.9 %all-to-all-done.3 = bf16[16,1,72,128]{3,2,1,0:T(8,128)(2,1)S(1)} async-done(((bf16[16,1,72,128]{3,2,1,0:T(8,128)(2,1)}), bf16[16,1,72,128]{3,2,1,0:T(8,128)(2,1)S(1)}, u32[]{:S(2)}, u32[]{:S(2)}) %all-to-all-start.3) | async-done | bytes 294944 | tf_op jit(solution)/shard_map/all_to_all | solution.py:47
  56.0 3.5 %all-to-all-start.2 = ((bf16[16,1,72,128]{3,2,1,0:T(8,128)(2,1)}), bf16[16,1,72,128]{3,2,1,0:T(8,128)(2,1)S(1)}, u32[]{:S(2)}, u32[]{:S(2)}) async-start(bf16[16,1,72,128]{3,2,1,0:T(8,128)(2,1)} %bitcast.20), calls=%async_computation.2 | async-start | bytes 589824 | tf_op jit(solution)/shard_map/all_to_all | solution.py:48
  59.6 0.6 gather_fusion.3
  60.2 0.3 fusion.28
  60.5 0.3 convolution_bitcast_fusion.3
  60.8 0.6 copy-done.4
  61.4 0.5 fusion.6
  61.9 0.5 convolution_convert_fusion.5
  62.4 0.7 broadcast.58.clone
  63.1 2.8 %scatter_fusion = bf16[16,72,128]{2,1,0:T(8,128)(2,1)} fusion(bf16[16,72,128]{2,1,0:T(8,128)(2,1)} %broadcast.58.clone, s32[16]{0:T(128)S(1)} %fusion.96, bf16[16,72,128]{2,1,0:T(8,128)(2,1)S(1)} %bitcast.302), kind=kCustom, calls=%fused_computation.4 | custom fusion | flops 147456 | bytes 884800 | tf_op jit(solution)/shard_map/scatter-add | solution.py:88
  66.0 4.1 %all-to-all-done.2 = bf16[16,1,72,128]{3,2,1,0:T(8,128)(2,1)S(1)} async-done(((bf16[16,1,72,128]{3,2,1,0:T(8,128)(2,1)}), bf16[16,1,72,128]{3,2,1,0:T(8,128)(2,1)S(1)}, u32[]{:S(2)}, u32[]{:S(2)}) %all-to-all-start.2) | async-done | bytes 294944 | tf_op jit(solution)/shard_map/all_to_all | solution.py:48
  70.1 3.5 %all-to-all-start.4 = ((bf16[16,1,72,128]{3,2,1,0:T(8,128)(2,1)}), bf16[16,1,72,128]{3,2,1,0:T(8,128)(2,1)S(1)}, u32[]{:S(2)}, u32[]{:S(2)}) async-start(bf16[16,1,72,128]{3,2,1,0:T(8,128)(2,1)} %bitcast.44), calls=%async_computation.4 | async-start | bytes 589824 | tf_op jit(solution)/shard_map/all_to_all | solution.py:89
  73.7 0.6 gather_fusion.2
  74.3 0.3 fusion.26
  74.6 1.3 fusion.23
  75.9 8.3 %all-to-all-done.4 = bf16[16,1,72,128]{3,2,1,0:T(8,128)(2,1)S(1)} async-done(((bf16[16,1,72,128]{3,2,1,0:T(8,128)(2,1)}), bf16[16,1,72,128]{3,2,1,0:T(8,128)(2,1)S(1)}, u32[]{:S(2)}, u32[]{:S(2)}) %all-to-all-start.4) | async-done | bytes 294944 | tf_op jit(solution)/shard_map/all_to_all | solution.py:89
  84.4 1.8 fusion.7
  87.0 0.8 broadcast.58
  87.7 2.8 %scatter_fusion.1 = bf16[16,72,128]{2,1,0:T(8,128)(2,1)} fusion(bf16[16,72,128]{2,1,0:T(8,128)(2,1)} %broadcast.58, s32[16]{0:T(128)S(1)} %fusion.95, bf16[16,72,128]{2,1,0:T(8,128)(2,1)S(1)} %bitcast.296), kind=kCustom, calls=%fused_computation.5 | custom fusion | flops 147456 | bytes 884800 | tf_op jit(solution)/shard_map/scatter-add | solution.py:88
  90.6 3.5 %all-to-all-start.5 = ((bf16[16,1,72,128]{3,2,1,0:T(8,128)(2,1)}), bf16[16,1,72,128]{3,2,1,0:T(8,128)(2,1)S(1)}, u32[]{:S(2)}, u32[]{:S(2)}) async-start(bf16[16,1,72,128]{3,2,1,0:T(8,128)(2,1)} %bitcast.52), calls=%async_computation.5 | async-start | bytes 589824 | tf_op jit(solution)/shard_map/all_to_all | solution.py:89
  94.4 0.9 fusion.20
  95.2 1.1 fusion.21
  96.4 8.3 %all-to-all-done.5 = bf16[16,1,72,128]{3,2,1,0:T(8,128)(2,1)S(1)} async-done(((bf16[16,1,72,128]{3,2,1,0:T(8,128)(2,1)}), bf16[16,1,72,128]{3,2,1,0:T(8,128)(2,1)S(1)}, u32[]{:S(2)}, u32[]{:S(2)}) %all-to-all-start.5) | async-done | bytes 294944 | tf_op jit(solution)/shard_map/all_to_all | solution.py:89
  104.8 0.7 copy.56
  105.5 85.1 %all-reduce.3.cloned.1.call-done = (f32[512,72]{0,1:T(8,128)}, f32[72,512]{1,0:T(8,128)}) async-done(((f32[512,72]{0,1:T(8,128)}, f32[72,512]{1,0:T(8,128)}), (f32[512,72]{0,1:T(8,128)}, f32[72,512]{1,0:T(8,128)})) %all-reduce.3.cloned.1.call-update) | async-done | bytes 294928 | tf_op jit(solution)/shard_map/psum | solution.py:109
  190.6 1.6 copy.129
  192.2 0.7 copy.130
  (35 shorter events, 2.4 us)
Async XLA Ops:
  7.2 24.9 %copy-start = (bf16[4,128,128]{2,1,0:T(8,128)(2,1)S(1)}, bf16[4,128,128]{2,1,0:T(8,128)(2,1)}, u32[]{:S(2)}) copy-start(bf16[4,128,128]{2,1,0:T(8,128)(2,1)} %param.13) | copy-start | bytes 393220
  9.8 7.5 %copy-start.6 = (s32[2,4,4]{2,1,0:T(4,128)S(1)}, s32[2,4,4]{2,1,0:T(4,128)}, u32[]{:S(2)}) copy-start(s32[2,4,4]{2,1,0:T(4,128)} %param.16) | copy-start | bytes 388
  9.8 7.9 %copy-start.5 = (bf16[4,72,128]{2,1,0:T(8,128)(2,1)S(1)}, bf16[4,72,128]{2,1,0:T(8,128)(2,1)}, u32[]{:S(2)}) copy-start(bf16[4,72,128]{2,1,0:T(8,128)(2,1)} %param.11) | copy-start | bytes 221188
  9.8 18.1 %all-to-all-start.1 = ((bf16[16,1,72,128]{3,2,1,0:T(8,128)(2,1)}), bf16[16,1,72,128]{3,2,1,0:T(8,128)(2,1)S(1)}, u32[]{:S(2)}, u32[]{:S(2)}) async-start(bf16[16,1,72,128]{3,2,1,0:T(8,128)(2,1)} %bitcast.10), calls=%async_computation.1 | async-start | bytes 589824 | tf_op jit(solution)/shard_map/all_to_all | solution.py:47
  27.9 14.1 %all-to-all-start = ((bf16[16,1,72,128]{3,2,1,0:T(8,128)(2,1)}), bf16[16,1,72,128]{3,2,1,0:T(8,128)(2,1)S(1)}, u32[]{:S(2)}, u32[]{:S(2)}) async-start(bf16[16,1,72,128]{3,2,1,0:T(8,128)(2,1)} %bitcast.4), calls=%async_computation | async-start | bytes 589824 | tf_op jit(solution)/shard_map/all_to_all | solution.py:48
  32.1 0.9 copy-start.1
  32.9 0.9 copy-start.3
  33.4 13.7 %copy-start.7 = (f32[4,512,128]{1,2,0:T(8,128)}, f32[4,512,128]{1,2,0:T(8,128)S(1)}, u32[]{:S(2)}) copy-start(f32[4,512,128]{1,2,0:T(8,128)S(1)} %get-tuple-element.28) | copy-start | bytes 3145732
  42.0 14.1 %all-to-all-start.3 = ((bf16[16,1,72,128]{3,2,1,0:T(8,128)(2,1)}), bf16[16,1,72,128]{3,2,1,0:T(8,128)(2,1)S(1)}, u32[]{:S(2)}, u32[]{:S(2)}) async-start(bf16[16,1,72,128]{3,2,1,0:T(8,128)(2,1)} %bitcast.26), calls=%async_computation.3 | async-start | bytes 589824 | tf_op jit(solution)/shard_map/all_to_all | solution.py:47
  56.0 14.1 %all-to-all-start.2 = ((bf16[16,1,72,128]{3,2,1,0:T(8,128)(2,1)}), bf16[16,1,72,128]{3,2,1,0:T(8,128)(2,1)S(1)}, u32[]{:S(2)}, u32[]{:S(2)}) async-start(bf16[16,1,72,128]{3,2,1,0:T(8,128)(2,1)} %bitcast.20), calls=%async_computation.2 | async-start | bytes 589824 | tf_op jit(solution)/shard_map/all_to_all | solution.py:48
  60.5 0.9 copy-start.4
  70.1 14.1 %all-to-all-start.4 = ((bf16[16,1,72,128]{3,2,1,0:T(8,128)(2,1)}), bf16[16,1,72,128]{3,2,1,0:T(8,128)(2,1)S(1)}, u32[]{:S(2)}, u32[]{:S(2)}) async-start(bf16[16,1,72,128]{3,2,1,0:T(8,128)(2,1)} %bitcast.44), calls=%async_computation.4 | async-start | bytes 589824 | tf_op jit(solution)/shard_map/all_to_all | solution.py:89
  90.6 14.1 %all-to-all-start.5 = ((bf16[16,1,72,128]{3,2,1,0:T(8,128)(2,1)}), bf16[16,1,72,128]{3,2,1,0:T(8,128)(2,1)S(1)}, u32[]{:S(2)}, u32[]{:S(2)}) async-start(bf16[16,1,72,128]{3,2,1,0:T(8,128)(2,1)} %bitcast.52), calls=%async_computation.5 | async-start | bytes 589824 | tf_op jit(solution)/shard_map/all_to_all | solution.py:89
  94.1 96.5 %all-reduce.3.cloned.1.call-start = ((), (), s32[]{:S(2)}) async-start(), calls=%async_computation.6 | async-start | bytes 589824 | tf_op jit(solution)/shard_map/psum | solution.py:109
  190.6 1.6 copy-start.2
Sparse Core Ops, SparseCore 0:
  98.9 91.5 all-reduce.2
where the time goes:
time: 201 us; the launch traced here: 200 us
  waiting for transfers between devices  130 us (65%)
  starting transfers between devices  25.2 us (13%)
  between operations  14.3 us (7%)
  local copies, waits for them, and re-layouts  12.5 us (6%)
  matrix products  12.2 us (6%)
  other arithmetic  5.76 us (3%)
    psum x1, waiting for transfers between devices, shards(): grad_in, grad_out = lax.psum((grad_in, grad_out), 'lat')  85.1 us
    all_to_all x2, waiting for transfers between devices, shards(): lax.all_to_all(send_field, 'lat', split_axis=0, concat_axis=0, tiled=True)  17 us
    all_to_all x2, waiting for transfers between devices, shards(): lax.all_to_all(buffer.reshape(peer_count, slot_cap, channels, columns), '...  16.6 us
    all_to_all x2, starting transfers between devices, shards(): lax.all_to_all(send_field, 'lat', split_axis=0, concat_axis=0, tiled=True)  11 us
    all_to_all x2, waiting for transfers between devices, shards(): lax.all_to_all(send_pert, 'lat', split_axis=0, concat_axis=0, tiled=True)  11 us
    unnamed x23, local copies, waits for them, and re-layouts  7.52 us
    all_to_all x2, starting transfers between devices, shards(): lax.all_to_all(send_pert, 'lat', split_axis=0, concat_axis=0, tiled=True)  7.07 us
    all_to_all x2, starting transfers between devices, shards(): lax.all_to_all(buffer.reshape(peer_count, slot_cap, channels, columns), '...  7.07 us
  transfers between devices with their start and end apart: 7, of which 7 were waited for; matrix products, arithmetic and copies ran while one was open for 9% of the time, Pallas kernels for 0%

commit v1 on v0

v1 whole, which is shorter than its diff:
```python
import functools

import jax
import jax.numpy as jnp
from jax import lax
from jax.experimental import pallas as pl
from jax.experimental.pallas import tpu as pltpu
from jax.sharding import PartitionSpec as P

BF = jnp.bfloat16
F32 = jnp.float32


def call(kernel, outs, tables, arrays, flops):
    moved = sum(a.size * a.dtype.itemsize for a in arrays)
    moved += sum(o.size * o.dtype.itemsize for o in outs)
    return pl.pallas_call(
        kernel,
        out_shape=tuple(outs),
        in_specs=[pl.BlockSpec(memory_space=pltpu.SMEM)] * len(tables)
        + [pl.BlockSpec(memory_space=pltpu.VMEM)] * len(arrays),
        out_specs=tuple(pl.BlockSpec(memory_space=pltpu.VMEM) for _ in outs),
        compiler_params=pltpu.CompilerParams(vmem_limit_bytes=32 * 1024 * 1024),
        cost_estimate=pl.CostEstimate(flops=flops, bytes_accessed=moved, transcendentals=0),
    )(*tables, *arrays)


def shape(dims, dtype=BF):
    return jax.ShapeDtypeStruct(tuple(dims), dtype)


def dot(a, b):
    return jnp.dot(a, b, preferred_element_type=F32)


def dot_nt(a, b):
    return lax.dot_general(a, b, (((1,), (1,)), ((), ())), preferred_element_type=F32)


def to_rows(wide, count):
    width = wide.shape[1] // count
    return jnp.concatenate([wide[:, j * width : (j + 1) * width] for j in range(count)], axis=0)


def to_lanes(tall, count):
    height = tall.shape[0] // count
    return jnp.concatenate([tall[j * height : (j + 1) * height] for j in range(count)], axis=1)


def gates(preact):
    sigma = 0.5 + 0.5 * jnp.tanh(0.5 * preact)
    hidden = preact * sigma
    return hidden, sigma + hidden * (1.0 - sigma)


def advect(read, slots_ref, section, count, stencil, cubic_ref):
    parts = []
    for k in range(stencil):
        rows = [read(slots_ref[(section * count + j) * stencil + k]).astype(F32) for j in range(count)]
        parts.append(jnp.concatenate(rows, axis=0).astype(BF))
    return to_lanes(dot(jnp.concatenate(parts, axis=1), cubic_ref[...]), count)


def scatter_terms(ladv, count, stencil, section, slots_ref, cubic_t_ref, write):
    width = ladv.shape[1] // count
    height = ladv.shape[0]
    terms = dot(to_rows(ladv, count).astype(BF), cubic_t_ref[...])
    for j in range(count):
        for k in range(stencil):
            block = terms[j * height : (j + 1) * height, k * width : (k + 1) * width]
            write(slots_ref[(section * count + j) * stencil + k], block.astype(BF))


def pack(sends_ref, section, slots, read, write):
    def one(q):
        write(q, read(jnp.maximum(sends_ref[section * slots + q], 0)))

    if slots <= 16:
        for q in range(slots):
            one(q)
    else:
        pl.loop(0, slots)(one)


def collect(sends_ref, section, slots, read, total_ref):
    total_ref[...] = jnp.zeros(total_ref.shape, F32)

    def one(q):
        entry = sends_ref[section * slots + q]

        @pl.when(entry >= 0)
        def _():
            total_ref[entry] += read(q).astype(F32)

    if slots <= 16:
        for q in range(slots):
            one(q)
    else:
        pl.loop(0, slots)(one)


def pack_kernel(slots, sends_ref, state_ref, tangent_ref, out_ref):
    def write_state(q, block):
        out_ref[q, 0] = block

    def write_tangent(q, block):
        out_ref[q, 1] = block

    pack(sends_ref, 0, slots, lambda e: state_ref[e], write_state)
    pack(sends_ref, 0, slots, lambda e: tangent_ref[e], write_tangent)


def prepare_kernel(w_in_ref, w_out_ref, cubic_ref, cot_ref, w_in_t_ref, w_out_t_ref, cubic_t_ref, lam_ref, pull_ref):
    count = cot_ref.shape[0]
    columns = cubic_ref.shape[1]
    w_in_t_ref[...] = w_in_ref[...].astype(F32).T.astype(BF)
    w_out_t = w_out_ref[...].astype(F32).T.astype(BF)
    w_out_t_ref[...] = w_out_t
    for k in range(cubic_ref.shape[0] // columns):
        tile = cubic_ref[k * columns : (k + 1) * columns, :].astype(F32)
        cubic_t_ref[:, k * columns : (k + 1) * columns] = tile.T.astype(BF)
    lam = jnp.concatenate([cot_ref[j] for j in range(count)], axis=1)
    lam_ref[...] = lam
    pull_ref[...] = dot(w_out_t, lam)


def first_kernel(count, stencil, slots, slots_ref, sends_ref, recv_ref, cubic_ref, w_in_ref, w_out_ref,
                 send_ref, adv_ref, hidden_ref, slope_ref, field_ref):
    adv = advect(lambda q: recv_ref[q, 0], slots_ref, 0, count, stencil, cubic_ref).astype(BF)
    adv_ref[...] = adv
    hidden, slope = gates(dot(w_in_ref[...], adv))
    hidden = hidden.astype(BF)
    field = adv.astype(F32) + dot(w_out_ref[...], hidden)
    width = field.shape[1] // count
    for j in range(count):
        field_ref[j] = field[:, j * width : (j + 1) * width].astype(BF)

    def write(q, block):
        send_ref[q] = block

    pack(sends_ref, 1, slots, lambda e: field_ref[e], write)
    hidden_ref[...] = hidden
    slope_ref[...] = slope


def tangent_kernel(section, count, stencil, slots_ref, recv_ref, cubic_ref, w_in_ref, w_out_ref, slope_ref, out_ref):
    tadv = advect(lambda q: recv_ref[q, 1], slots_ref, section, count, stencil, cubic_ref).astype(BF)
    thid = (slope_ref[...] * dot(w_in_ref[...], tadv)).astype(BF)
    pert = tadv.astype(F32) + dot(w_out_ref[...], thid)
    width = pert.shape[1] // count
    for j in range(count):
        out_ref[j] = pert[:, j * width : (j + 1) * width].astype(BF)


def second_kernel(count, stencil, slots, slots_ref, recv_ref, cubic_ref, cubic_t_ref, w_in_ref, w_in_t_ref, lam_ref, pull_ref,
                  send_ref, adv_ref, hidden_ref, slope_ref, ghid_ref):
    adv = advect(lambda q: recv_ref[q], slots_ref, 1, count, stencil, cubic_ref).astype(BF)
    adv_ref[...] = adv
    hidden, slope = gates(dot(w_in_ref[...], adv))
    hidden_ref[...] = hidden.astype(BF)
    slope_ref[...] = slope
    ghid = (slope * pull_ref[...]).astype(BF)
    ghid_ref[...] = ghid
    ladv = lam_ref[...].astype(F32) + dot(w_in_t_ref[...], ghid)
    if slots != count * stencil:
        send_ref[...] = jnp.zeros(send_ref.shape, BF)

    def write(q, block):
        send_ref[q] = block

    scatter_terms(ladv, count, stencil, 1, slots_ref, cubic_t_ref, write)


def grad_kernel(lam_ref, hidden_ref, ghid_ref, adv_ref, in_ref, out_ref):
    in_ref[...] = dot_nt(adv_ref[...], ghid_ref[...])
    out_ref[...] = dot_nt(lam_ref[...], hidden_ref[...])


def third_kernel(count, stencil, slots, slots_ref, sends_ref, recv_ref, cubic_t_ref, w_in_t_ref, w_out_t_ref, slope_ref, pert_ref,
                 send_ref, lam_ref, ghid_ref, total_ref):
    collect(sends_ref, 1, slots, lambda q: recv_ref[q], total_ref)
    lam = jnp.concatenate([total_ref[j] for j in range(count)], axis=1).astype(BF)
    lam_ref[...] = lam
    ghid = (slope_ref[...] * dot(w_out_t_ref[...], lam)).astype(BF)
    ghid_ref[...] = ghid
    ladv = lam.astype(F32) + dot(w_in_t_ref[...], ghid)
    if slots != count * stencil:
        send_ref[...] = jnp.zeros(send_ref.shape, BF)

    def write_term(q, block):
        send_ref[q, 0] = block

    def write_pert(q, block):
        send_ref[q, 1] = block

    scatter_terms(ladv, count, stencil, 0, slots_ref, cubic_t_ref, write_term)
    pack(sends_ref, 1, slots, lambda e: pert_ref[e], write_pert)


def grad_pair_kernel(side_ref, lam_ref, hidden_ref, ghid_ref, adv_ref, in_ref, out_ref, keep_ref, give_ref):
    grad_in = (in_ref[...] + dot_nt(adv_ref[...], ghid_ref[...])).astype(BF)
    grad_out = (out_ref[...] + dot_nt(lam_ref[...], hidden_ref[...])).astype(BF)

    @pl.when(side_ref[0] == 0)
    def _():
        keep_ref[...] = grad_in
        give_ref[...] = grad_out

    @pl.when(side_ref[0] != 0)
    def _():
        keep_ref[...] = grad_out
        give_ref[...] = grad_in


def last_kernel(count, stencil, slots, slots_ref, sends_ref, recv_ref, cubic_ref, w_in_ref, w_out_ref, slope_ref, back_ref, pert_ref):
    collect(sends_ref, 0, slots, lambda q: recv_ref[q, 0], back_ref)
    tangent_kernel(1, count, stencil, slots_ref, recv_ref, cubic_ref, w_in_ref, w_out_ref, slope_ref, pert_ref)


def grad_end_kernel(side_ref, mine_ref, other_ref, in_ref, out_ref):
    mine = mine_ref[...].astype(F32)
    other = other_ref[...].astype(F32)

    @pl.when(side_ref[0] == 0)
    def _():
        in_ref[...] = mine.T
        out_ref[...] = other

    @pl.when(side_ref[0] != 0)
    def _():
        in_ref[...] = other.T
        out_ref[...] = mine


def shards(state, tangent, cotangent, cubic, w_in, w_out, slots, sends):
    count, channels, columns = state.shape
    stencil = cubic.shape[0]
    hid = w_in.shape[0]
    peers = lax.axis_size("lat")
    slot_count = peers * sends.shape[-1]
    wide = count * columns
    blocks = (count, channels, columns)
    me = lax.axis_index("lat")
    side = (me % 2).astype(jnp.int32).reshape(1)
    slots = slots.reshape(-1)
    sends = sends.reshape(-1)
    cubic = cubic.reshape(stencil * columns, columns)
    mix = 2 * wide * channels * stencil * columns
    net = 2 * wide * channels * hid
    sizes = (count, stencil, slot_count)

    def exchange(packed):
        return lax.all_to_all(packed, "lat", split_axis=0, concat_axis=0, tiled=True)

    def swap(values, step):
        return lax.ppermute(values, "lat", [(i, i ^ step) for i in range(peers)])

    (send,) = call(
        functools.partial(pack_kernel, slot_count),
        [shape((slot_count, 2, channels, columns))], [sends], [state, tangent], 0,
    )
    recv_one = exchange(send)
    w_in_t, w_out_t, cubic_t, lam_two, pull_two = call(
        prepare_kernel,
        [shape((channels, hid)), shape((hid, channels)), shape((columns, stencil * columns)),
         shape((channels, wide)), shape((hid, wide), F32)],
        [], [w_in, w_out, cubic, cotangent], net,
    )
    send, adv_one, hidden_one, slope_one, _ = call(
        functools.partial(first_kernel, *sizes),
        [shape((slot_count, channels, columns)), shape((channels, wide)), shape((hid, wide)), shape((hid, wide), F32), shape(blocks)],
        [slots, sends], [recv_one, cubic, w_in, w_out], mix + 2 * net,
    )
    recv_two = exchange(send)
    (pert_one,) = call(
        functools.partial(tangent_kernel, 0, count, stencil),
        [shape(blocks)], [slots], [recv_one, cubic, w_in, w_out, slope_one], mix + 2 * net,
    )
    send, adv_two, hidden_two, slope_two, ghid_two = call(
        functools.partial(second_kernel, *sizes),
        [shape((slot_count, channels, columns)), shape((channels, wide)), shape((hid, wide)), shape((hid, wide), F32), shape((hid, wide))],
        [slots], [recv_two, cubic, cubic_t, w_in, w_in_t, lam_two, pull_two], 2 * mix + 2 * net,
    )
    recv_three = exchange(send)
    part_in, part_out = call(
        grad_kernel,
        [shape((channels, hid), F32)] * 2, [], [lam_two, hidden_two, ghid_two, adv_two], 2 * net,
    )
    send, lam_one, ghid_one, _ = call(
        functools.partial(third_kernel, *sizes),
        [shape((slot_count, 2, channels, columns)), shape((channels, wide)), shape((hid, wide)), shape(blocks, F32)],
        [slots, sends], [recv_three, cubic_t, w_in_t, w_out_t, slope_one, pert_one], mix + 2 * net,
    )
    recv_four = exchange(send)
    mine, give = call(
        grad_pair_kernel,
        [shape((channels, hid))] * 2, [side], [lam_one, hidden_one, ghid_one, adv_one, part_in, part_out], 2 * net,
    )
    mine = (mine.astype(F32) + swap(give, 1).astype(F32)).astype(BF)
    step = 2
    while step < peers:
        mine = (mine.astype(F32) + swap(mine, step).astype(F32)).astype(BF)
        step *= 2
    grad_in, grad_out = call(
        grad_end_kernel,
        [shape((hid, channels), F32), shape((channels, hid), F32)], [side], [mine, swap(mine, 1)], 0,
    )
    back, pert = call(
        functools.partial(last_kernel, *sizes),
        [shape(blocks, F32), shape(blocks)],
        [slots, sends], [recv_four, cubic, w_in, w_out, slope_two], mix + 2 * net,
    )
    return (pert, back, grad_in, grad_out)


def solution(mesh):
    in_specs = (
        P(("grp", "lat"), None, None),
        P(("grp", "lat"), None, None),
        P(("grp", "lat"), None, None),
        P(),
        P(),
        P(),
        P("grp", "lat", None),
        P("grp", "lat", None, None),
    )
    out_specs = (
        P(("grp", "lat"), None, None),
        P(("grp", "lat"), None, None),
        P("grp", None),
        P("grp", None),
    )
    return jax.shard_map(shards, mesh=mesh, in_specs=in_specs, out_specs=out_specs, check_vma=False)
```

time: 201 us -> 99.6 us (0.50)
  waiting for transfers between devices: 130 us -> 45.7 us
  between operations: 14.3 us -> 0.9 us
  Pallas kernels: 0 us -> 12.9 us
  matrix products: 12.2 us -> 0 us
  other arithmetic: 5.76 us -> 0.75 us
    psum x1 -> x0, waiting for transfers between devices: 85.1 us -> none  [shards(): grad_in, grad_out = lax.psum((grad_in, grad_out), 'lat')]
    ppermute x0 -> x5, waiting for transfers between devices: none -> 14.4 us  [swap(): return lax.ppermute(values, 'lat', [(i, i ^ step) for i in range(peers)])]
    all_to_all x6 -> x4, waiting for transfers between devices: 44.6 us -> 31.2 us  [exchange(): lax.all_to_all(packed, 'lat', split_axis=0, concat_axis=0, tiled=True)]
    pallas_call x0 -> x10, Pallas kernels: none -> 12.9 us  [call(): pl.pallas_call(kernel, out_shape=tuple(outs), in_specs=[pl.BlockSpec(memo...]
    dot_general x24 -> x0, matrix products: 12.2 us -> none  [the longest x2 2.27 us: shards(): jnp.einsum('ch,bcn->bhn', w_out, adjoint_state, preferred_element_type=jn...]
    ppermute x0 -> x5, starting transfers between devices: none -> 6.45 us  [swap(): return lax.ppermute(values, 'lat', [(i, i ^ step) for i in range(peers)])]
    all_to_all x6 -> x4, starting transfers between devices: 25.2 us -> 19.2 us  [exchange(): lax.all_to_all(packed, 'lat', split_axis=0, concat_axis=0, tiled=True)]
    scatter-add x2 -> x0, other arithmetic: 5.67 us -> none  [shards(): buffer.at[slots[section].reshape(-1)]]
  transfers between devices with their start and end apart: 7 -> 9, of which waited for: 7 -> 7; matrix products, arithmetic and copies ran while one was open for 9% -> 1% of each run, Pallas kernels for 0% -> 3%
where the time goes in v1:
time: 99.6 us; the launch traced here: 98.8 us
  waiting for transfers between devices  45.7 us (46%)
  starting transfers between devices  25.6 us (26%)
  local copies, waits for them, and re-layouts  13 us (13%)
  Pallas kernels  12.9 us (13%)
    all_to_all x4, waiting for transfers between devices, exchange(): lax.all_to_all(packed, 'lat', split_axis=0, concat_axis=0, tiled=True)  31.2 us
    all_to_all x4, starting transfers between devices, exchange(): lax.all_to_all(packed, 'lat', split_axis=0, concat_axis=0, tiled=True)  19.2 us
    ppermute x5, waiting for transfers between devices, swap(): return lax.ppermute(values, 'lat', [(i, i ^ step) for i in range(peers)])  14.4 us
    pallas_call x10, Pallas kernels, call(): pl.pallas_call(kernel, out_shape=tuple(outs), in_specs=[pl.BlockSpec(memo...  12.9 us
    unnamed x59, local copies, waits for them, and re-layouts  12.8 us
    ppermute x5, starting transfers between devices, swap(): return lax.ppermute(values, 'lat', [(i, i ^ step) for i in range(peers)])  6.45 us
  transfers between devices with their start and end apart: 9, of which 7 were waited for; matrix products, arithmetic and copies ran while one was open for 1% of the time, Pallas kernels for 3%

profile of v1, /device:TPU:0, one launch (start us, length us, event | category | flops | bytes accessed | tf_op | source)
XLA Modules:
  0.0 98.8 jit_solution(17843399915834128666)
XLA Ops:
  0.6 0.5 broadcast.4
  1.2 0.2 copy-done.27
  1.3 0.7 reduce.3
  2.0 0.1 reshape.21.sends_ref
  2.1 0.9 copy-done.18
  2.9 0.9 copy-done.19
  3.8 1.4 %shard_map.111 = bf16[16,2,72,128]{3,2,1,0:T(8,128)(2,1)} custom-call(s32[32]{0:T(128)S(1)} %reshape.21.sends_ref, bf16[4,72,128]{2,1,0:T(8,128)(2,1)S(1)} %copy-done.18, bf16[4,72,128]{2,1,0:T(8,128)(2,1)S(1)} %copy-done.19), custom_call_target="tpu_custom_call" | custom-call | bytes 737280 | tf_op jit(solution)/shard_map/pallas_call | solution.py:17
  5.2 7.5 %all-to-all-start = ((bf16[16,2,72,128]{3,2,1,0:T(8,128)(2,1)}), bf16[16,2,72,128]{3,2,1,0:T(8,128)(2,1)S(1)}, u32[]{:S(2)}, u32[]{:S(2)}) async-start(bf16[16,2,72,128]{3,2,1,0:T(8,128)(2,1)} %shard_map.111), calls=%async_computation | async-start | bytes 1179648 | tf_op jit(solution)/shard_map/all_to_all | solution.py:253
  12.8 0.0 copy-start
  12.8 0.1 reshape.20.slots_ref
  12.9 0.1 copy.12.w_in_ref
  13.0 15.3 %all-to-all-done.recv_ref = bf16[16,2,72,128]{3,2,1,0:T(8,128)(2,1)S(1)} async-done(((bf16[16,2,72,128]{3,2,1,0:T(8,128)(2,1)}), bf16[16,2,72,128]{3,2,1,0:T(8,128)(2,1)S(1)}, u32[]{:S(2)}, u32[]{:S(2)}) %all-to-all-start) | async-done | bytes 589856 | tf_op jit(solution)/shard_map/all_to_all | solution.py:253
  28.3 2.2 %shard_map.112 = (bf16[16,72,128]{2,1,0:T(8,128)(2,1)}, bf16[72,512]{1,0:T(8,128)(2,1)S(1)}, bf16[512,512]{1,0:T(8,128)(2,1)S(1)}, f32[512,512]{1,0:T(8,128)S(1)}, bf16[4,72,128]{2,1,0:T(8,128)(2,1)}) custom-call(s32[32]{0:T(128)S(1)} %reshape.20.slots_ref, s32[32]{0:T(128)S(1)} %reshape.21.sends_ref, bf16[16,2,72,128]{3,2,1,0:T(8,128)(2,1)S(1)} %all-to-all-done.recv_ref, ...), custom_call_target="tpu_custom_call" | custom-call | flops 113246208 | bytes 2883584 | tf_op jit(solution)/shard_map/pallas_call | solution.py:17
  30.5 0.8 copy-done.8
  31.3 0.6 copy-done.23
  31.9 4.6 %all-to-all-start.1 = ((bf16[16,72,128]{2,1,0:T(8,128)(2,1)}), bf16[16,72,128]{2,1,0:T(8,128)(2,1)S(1)}, u32[]{:S(2)}, u32[]{:S(2)}) async-start(bf16[16,72,128]{2,1,0:T(8,128)(2,1)} %get-tuple-element.29), calls=%async_computation.1 | async-start | bytes 589824 | tf_op jit(solution)/shard_map/all_to_all | solution.py:253
  36.5 0.4 shard_map.113
  36.8 1.0 %copy-done.2 = f32[512,512]{1,0:T(8,128)} copy-done((f32[512,512]{1,0:T(8,128)}, f32[512,512]{1,0:T(8,128)S(1)}, u32[]{:S(2)}) %copy-start.2) | copy-done | bytes 1048600
  37.8 0.6 copy-done.10
  38.5 0.7 copy-done.16
  39.1 7.9 %all-to-all-done.1.recv_ref = bf16[16,72,128]{2,1,0:T(8,128)(2,1)S(1)} async-done(((bf16[16,72,128]{2,1,0:T(8,128)(2,1)}), bf16[16,72,128]{2,1,0:T(8,128)(2,1)S(1)}, u32[]{:S(2)}, u32[]{:S(2)}) %all-to-all-start.1) | async-done | bytes 294944 | tf_op jit(solution)/shard_map/all_to_all | solution.py:253
  47.0 1.2 %copy-done.3 = f32[512,512]{1,0:T(8,128)S(1)} copy-done((f32[512,512]{1,0:T(8,128)S(1)}, f32[512,512]{1,0:T(8,128)}, u32[]{:S(2)}) %copy-start.3) | copy-done | bytes 1048600
  48.3 0.9 copy-done.11
  49.1 1.6 %shard_map.114 = (bf16[16,72,128]{2,1,0:T(8,128)(2,1)S(1)}, bf16[72,512]{1,0:T(8,128)(2,1)S(1)}, bf16[512,512]{1,0:T(8,128)(2,1)S(1)}, f32[512,512]{1,0:T(8,128)S(1)}, bf16[512,512]{1,0:T(8,128)(2,1)S(1)}) custom-call(s32[32]{0:T(128)S(1)} %reshape.20.slots_ref, bf16[16,72,128]{2,1,0:T(8,128)(2,1)S(1)} %all-to-all-done.1.recv_ref, ...), custom_call_target="tpu_custom_call" | custom-call | flops 150994944 | bytes 4292608 | tf_op jit(solution)/shard_map/pallas_call | solution.py:17
  50.8 0.8 copy-done.4
  51.6 0.8 copy-done.6
  52.4 0.7 copy-done.15
  53.1 0.6 copy-done.20
  53.8 3.5 %all-to-all-start.2 = ((bf16[16,72,128]{2,1,0:T(8,128)(2,1)}), bf16[16,72,128]{2,1,0:T(8,128)(2,1)S(1)}, u32[]{:S(2)}, u32[]{:S(2)}) async-start(bf16[16,72,128]{2,1,0:T(8,128)(2,1)} %copy-done.15), calls=%async_computation.2 | async-start | bytes 589824 | tf_op jit(solution)/shard_map/all_to_all | solution.py:253
  57.4 1.3 %shard_map.115.pert_ref = bf16[4,72,128]{2,1,0:T(8,128)(2,1)S(1)} custom-call(s32[32]{0:T(128)S(1)} %reshape.20.slots_ref, bf16[16,2,72,128]{3,2,1,0:T(8,128)(2,1)S(1)} %all-to-all-done.recv_ref, bf16[512,128]{1,0:T(8,128)(2,1)S(1)} %bitcast.6, bf16[512,72]{1,0:T(8,128)(2,1)S(1)} %copy.12.w_in_ref, bf16[72,512]{1,0:T(8,128)(2,1)S(1)} %copy-done.1, ...), custom_call_target="tpu_custom_call" | custom-call | flops 113246208 | bytes 1990656 | tf_op jit(solution)/shard_map/pallas_call | solution.py:17
  58.7 0.6 copy-done.13
  59.4 0.4 shard_map.118
  59.8 8.0 %all-to-all-done.2.recv_ref = bf16[16,72,128]{2,1,0:T(8,128)(2,1)S(1)} async-done(((bf16[16,72,128]{2,1,0:T(8,128)(2,1)}), bf16[16,72,128]{2,1,0:T(8,128)(2,1)S(1)}, u32[]{:S(2)}, u32[]{:S(2)}) %all-to-all-start.2) | async-done | bytes 294944 | tf_op jit(solution)/shard_map/all_to_all | solution.py:253
  67.8 2.2 %shard_map.116 = (bf16[16,2,72,128]{3,2,1,0:T(8,128)(2,1)}, bf16[72,512]{1,0:T(8,128)(2,1)S(1)}, bf16[512,512]{1,0:T(8,128)(2,1)S(1)}, f32[4,72,128]{2,1,0:T(8,128)}) custom-call(s32[32]{0:T(128)S(1)} %reshape.20.slots_ref, s32[32]{0:T(128)S(1)} %reshape.21.sends_ref, bf16[16,72,128]{2,1,0:T(8,128)(2,1)S(1)} %all-to-all-done.2.recv_ref, ...), custom_call_target="tpu_custom_call" | custom-call | flops 113246208 | bytes 3031040 | tf_op jit(solution)/shard_map/pallas_call | solution.py:17
  70.0 0.5 shard_map.119
  70.5 0.1 collective-permute-start
  70.6 3.6 %all-to-all-start.3 = ((bf16[16,2,72,128]{3,2,1,0:T(8,128)(2,1)}), bf16[16,2,72,128]{3,2,1,0:T(8,128)(2,1)S(1)}, u32[]{:S(2)}, u32[]{:S(2)}) async-start(bf16[16,2,72,128]{3,2,1,0:T(8,128)(2,1)} %get-tuple-element.37), calls=%async_computation.3 | async-start | bytes 1179648 | tf_op jit(solution)/shard_map/all_to_all | solution.py:253
  74.2 1.9 %collective-permute-start.1 = (bf16[72,512]{1,0:T(8,128)(2,1)S(1)}, bf16[72,512]{1,0:T(8,128)(2,1)S(1)}, u32[]{:S(2)}, u32[]{:S(2)}) collective-permute-start(bf16[72,512]{1,0:T(8,128)(2,1)S(1)} %add_convert_fusion.3), channel_id=1, source_target_pairs={{0,2},{1,3},{2,0},{3,1},{4,6},{5,7},{6,4},{7,5},{8,10},{9,11},{10,... | collective-permute-start | bytes 221192 | tf_op jit(solution)/shard_map/ppermute | solution.py:256
  76.1 6.4 %collective-permute-done.1 = bf16[72,512]{1,0:T(8,128)(2,1)S(1)} collective-permute-done((bf16[72,512]{1,0:T(8,128)(2,1)S(1)}, bf16[72,512]{1,0:T(8,128)(2,1)S(1)}, u32[]{:S(2)}, u32[]{:S(2)}) %collective-permute-start.1) | collective-permute-done | bytes 73760 | tf_op jit(solution)/shard_map/ppermute | solution.py:256
  82.5 0.7 collective-permute-start.2
  83.2 4.0 %collective-permute-done.2 = bf16[72,512]{1,0:T(8,128)(2,1)S(1)} collective-permute-done((bf16[72,512]{1,0:T(8,128)(2,1)S(1)}, bf16[72,512]{1,0:T(8,128)(2,1)S(1)}, u32[]{:S(2)}, u32[]{:S(2)}) %collective-permute-start.2) | collective-permute-done | bytes 73760 | tf_op jit(solution)/shard_map/ppermute | solution.py:256
  87.2 3.7 %collective-permute-start.3 = (bf16[72,512]{1,0:T(8,128)(2,1)S(1)}, bf16[72,512]{1,0:T(8,128)(2,1)S(1)}, u32[]{:S(2)}, u32[]{:S(2)}) collective-permute-start(bf16[72,512]{1,0:T(8,128)(2,1)S(1)} %add_convert_fusion.1), channel_id=1, source_target_pairs={{0,8},{1,9},{2,10},{3,11},{4,12},{5,13},{6,14},{7,15},{8,0},{9,1},... | collective-permute-start | bytes 221192 | tf_op jit(solution)/shard_map/ppermute | solution.py:256
  90.9 2.8 %collective-permute-done.3 = bf16[72,512]{1,0:T(8,128)(2,1)S(1)} collective-permute-done((bf16[72,512]{1,0:T(8,128)(2,1)S(1)}, bf16[72,512]{1,0:T(8,128)(2,1)S(1)}, u32[]{:S(2)}, u32[]{:S(2)}) %collective-permute-start.3) | collective-permute-done | bytes 73760 | tf_op jit(solution)/shard_map/ppermute | solution.py:256
  93.8 0.1 collective-permute-start.4
  93.9 1.3 %collective-permute-done.4.other_ref = bf16[72,512]{1,0:T(8,128)(2,1)S(1)} collective-permute-done((bf16[72,512]{1,0:T(8,128)(2,1)S(1)}, bf16[72,512]{1,0:T(8,128)(2,1)S(1)}, u32[]{:S(2)}, u32[]{:S(2)}) %collective-permute-start.4) | collective-permute-done | bytes 73760 | tf_op jit(solution)/shard_map/ppermute | solution.py:256
  95.1 0.8 shard_map.120
  95.9 0.8 copy.17
  96.7 2.1 %shard_map.117 = (f32[4,72,128]{2,1,0:T(8,128)}, bf16[4,72,128]{2,1,0:T(8,128)(2,1)}) custom-call(s32[32]{0:T(128)S(1)} %reshape.20.slots_ref, s32[32]{0:T(128)S(1)} %reshape.21.sends_ref, bf16[16,2,72,128]{3,2,1,0:T(8,128)(2,1)S(1)} %all-to-all-done.3.recv_ref, bf16[512,128]{1,0:T(8,128)(2,1)S(1)} %bitcast.7, bf16[512,72]{1,0:T(8,128)(2,1)S(1)} %copy.12.w_in_ref, ...), custom_call_target="tpu_custom_call" | custom-call | flops 113246208 | bytes 2138112 | tf_op jit(solution)/shard_map/pallas_call | solution.py:17
  (46 shorter events, 0.2 us)
Async XLA Ops:
  0.6 0.7 copy-start.27
  2.1 0.9 copy-start.18
  2.9 0.9 copy-start.19
  5.2 7.5 %copy-start.26 = (s32[2,4,4]{2,1,0:T(4,128)S(1)}, s32[2,4,4]{2,1,0:T(4,128)}, u32[]{:S(2)}) copy-start(s32[2,4,4]{2,1,0:T(4,128)} %param.14) | copy-start | bytes 388
  5.2 7.6 %copy-start.25 = (bf16[512,72]{0,1:T(8,128)(2,1)S(1)}, bf16[512,72]{0,1:T(8,128)(2,1)}, u32[]{:S(2)}) copy-start(bf16[512,72]{0,1:T(8,128)(2,1)} %param.12) | copy-start | bytes 221188
  5.2 23.0 %all-to-all-start = ((bf16[16,2,72,128]{3,2,1,0:T(8,128)(2,1)}), bf16[16,2,72,128]{3,2,1,0:T(8,128)(2,1)S(1)}, u32[]{:S(2)}, u32[]{:S(2)}) async-start(bf16[16,2,72,128]{3,2,1,0:T(8,128)(2,1)} %shard_map.111), calls=%async_computation | async-start | bytes 1179648 | tf_op jit(solution)/shard_map/all_to_all | solution.py:253
  12.8 15.5 %copy-start = (bf16[4,128,128]{2,1,0:T(8,128)(2,1)S(1)}, bf16[4,128,128]{2,1,0:T(8,128)(2,1)}, u32[]{:S(2)}) copy-start(bf16[4,128,128]{2,1,0:T(8,128)(2,1)} %param.11) | copy-start | bytes 393220
  12.9 15.4 %copy-start.1 = (bf16[72,512]{1,0:T(8,128)(2,1)S(1)}, bf16[72,512]{1,0:T(8,128)(2,1)}, u32[]{:S(2)}) copy-start(bf16[72,512]{1,0:T(8,128)(2,1)} %w_out_ref.7) | copy-start | bytes 221188
  30.5 0.8 copy-start.8
  31.3 0.6 copy-start.23
  31.9 4.6 %copy-start.22 = (bf16[4,72,128]{2,1,0:T(8,128)(2,1)S(1)}, bf16[4,72,128]{2,1,0:T(8,128)(2,1)}, u32[]{:S(2)}) copy-start(bf16[4,72,128]{2,1,0:T(8,128)(2,1)} %cot_ref.1) | copy-start | bytes 221188
  31.9 15.1 %all-to-all-start.1 = ((bf16[16,72,128]{2,1,0:T(8,128)(2,1)}), bf16[16,72,128]{2,1,0:T(8,128)(2,1)S(1)}, u32[]{:S(2)}, u32[]{:S(2)}) async-start(bf16[16,72,128]{2,1,0:T(8,128)(2,1)} %get-tuple-element.29), calls=%async_computation.1 | async-start | bytes 589824 | tf_op jit(solution)/shard_map/all_to_all | solution.py:253
  36.8 1.0 %copy-start.2 = (f32[512,512]{1,0:T(8,128)}, f32[512,512]{1,0:T(8,128)S(1)}, u32[]{:S(2)}) copy-start(f32[512,512]{1,0:T(8,128)S(1)} %get-tuple-element.33.pull_ref) | copy-start | bytes 3145732
  37.8 0.6 copy-start.10
  38.5 0.7 copy-start.16
  47.0 1.2 %copy-start.3 = (f32[512,512]{1,0:T(8,128)S(1)}, f32[512,512]{1,0:T(8,128)}, u32[]{:S(2)}) copy-start(f32[512,512]{1,0:T(8,128)} %copy-done.2) | copy-start | bytes 3145732
  48.3 0.9 copy-start.11
  50.8 0.8 copy-start.4
  51.6 0.8 copy-start.6
  52.4 0.7 copy-start.15
  53.1 0.6 copy-start.20
  53.8 14.1 %all-to-all-start.2 = ((bf16[16,72,128]{2,1,0:T(8,128)(2,1)}), bf16[16,72,128]{2,1,0:T(8,128)(2,1)S(1)}, u32[]{:S(2)}, u32[]{:S(2)}) async-start(bf16[16,72,128]{2,1,0:T(8,128)(2,1)} %copy-done.15), calls=%async_computation.2 | async-start | bytes 589824 | tf_op jit(solution)/shard_map/all_to_all | solution.py:253
  57.3 2.0 %copy-start.5 = (bf16[512,512]{1,0:T(8,128)(2,1)S(1)}, bf16[512,512]{1,0:T(8,128)(2,1)}, u32[]{:S(2)}) copy-start(bf16[512,512]{1,0:T(8,128)(2,1)} %copy-done.4) | copy-start | bytes 1572868
  57.3 2.0 %copy-start.7 = (bf16[512,512]{1,0:T(8,128)(2,1)S(1)}, bf16[512,512]{1,0:T(8,128)(2,1)}, u32[]{:S(2)}) copy-start(bf16[512,512]{1,0:T(8,128)(2,1)} %copy-done.6) | copy-start | bytes 1572868
  57.3 2.0 %copy-start.12 = (bf16[72,512]{1,0:T(8,128)(2,1)S(1)}, bf16[72,512]{1,0:T(8,128)(2,1)}, u32[]{:S(2)}) copy-start(bf16[72,512]{1,0:T(8,128)(2,1)} %copy-done.10) | copy-start | bytes 221188
  57.3 2.0 %copy-start.21 = (bf16[72,512]{1,0:T(8,128)(2,1)S(1)}, bf16[72,512]{1,0:T(8,128)(2,1)}, u32[]{:S(2)}) copy-start(bf16[72,512]{1,0:T(8,128)(2,1)} %copy-done.20) | copy-start | bytes 221188
  58.7 0.6 copy-start.13
  59.3 8.5 %copy-start.14 = (bf16[4,72,128]{2,1,0:T(8,128)(2,1)S(1)}, bf16[4,72,128]{2,1,0:T(8,128)(2,1)}, u32[]{:S(2)}) copy-start(bf16[4,72,128]{2,1,0:T(8,128)(2,1)} %copy-done.13) | copy-start | bytes 221188
  59.4 8.5 %copy-start.17 = (bf16[512,72]{1,0:T(8,128)(2,1)S(1)}, bf16[512,72]{1,0:T(8,128)(2,1)}, u32[]{:S(2)}) copy-start(bf16[512,72]{1,0:T(8,128)(2,1)} %copy-done.16) | copy-start | bytes 221188
  67.8 2.2 %copy-start.9 = (bf16[512,512]{1,0:T(8,128)(2,1)S(1)}, bf16[512,512]{1,0:T(8,128)(2,1)}, u32[]{:S(2)}) copy-start(bf16[512,512]{1,0:T(8,128)(2,1)} %copy-done.8) | copy-start | bytes 1572868
  67.8 2.2 %copy-start.24 = (bf16[72,512]{1,0:T(8,128)(2,1)S(1)}, bf16[72,512]{1,0:T(8,128)(2,1)}, u32[]{:S(2)}) copy-start(bf16[72,512]{1,0:T(8,128)(2,1)} %copy-done.23) | copy-start | bytes 221188
  70.5 3.7 %collective-permute-start = (bf16[72,512]{1,0:T(8,128)(2,1)S(1)}, bf16[72,512]{1,0:T(8,128)(2,1)S(1)}, u32[]{:S(2)}, u32[]{:S(2)}) collective-permute-start(bf16[72,512]{1,0:T(8,128)(2,1)S(1)} %get-tuple-element.51), channel_id=1, source_target_pairs={{0,1},{1,0},{2,3},{3,2},{4,5},{5,4},{6,7},{7,6},{8,9},{9,8},{10,11... | collective-permute-start | bytes 221192 | tf_op jit(solution)/shard_map/ppermute | solution.py:256
  70.6 26.1 %all-to-all-start.3 = ((bf16[16,2,72,128]{3,2,1,0:T(8,128)(2,1)}), bf16[16,2,72,128]{3,2,1,0:T(8,128)(2,1)S(1)}, u32[]{:S(2)}, u32[]{:S(2)}) async-start(bf16[16,2,72,128]{3,2,1,0:T(8,128)(2,1)} %get-tuple-element.37), calls=%async_computation.3 | async-start | bytes 1179648 | tf_op jit(solution)/shard_map/all_to_all | solution.py:253
  74.2 8.3 %collective-permute-start.1 = (bf16[72,512]{1,0:T(8,128)(2,1)S(1)}, bf16[72,512]{1,0:T(8,128)(2,1)S(1)}, u32[]{:S(2)}, u32[]{:S(2)}) collective-permute-start(bf16[72,512]{1,0:T(8,128)(2,1)S(1)} %add_convert_fusion.3), channel_id=1, source_target_pairs={{0,2},{1,3},{2,0},{3,1},{4,6},{5,7},{6,4},{7,5},{8,10},{9,11},{10,... | collective-permute-start | bytes 221192 | tf_op jit(solution)/shard_map/ppermute | solution.py:256
  82.5 4.7 %collective-permute-start.2 = (bf16[72,512]{1,0:T(8,128)(2,1)S(1)}, bf16[72,512]{1,0:T(8,128)(2,1)S(1)}, u32[]{:S(2)}, u32[]{:S(2)}) collective-permute-start(bf16[72,512]{1,0:T(8,128)(2,1)S(1)} %add_convert_fusion.2), channel_id=1, source_target_pairs={{0,4},{1,5},{2,6},{3,7},{4,0},{5,1},{6,2},{7,3},{8,12},{9,13},{10,... | collective-permute-start | bytes 221192 | tf_op jit(solution)/shard_map/ppermute | solution.py:256
  87.2 6.5 %collective-permute-start.3 = (bf16[72,512]{1,0:T(8,128)(2,1)S(1)}, bf16[72,512]{1,0:T(8,128)(2,1)S(1)}, u32[]{:S(2)}, u32[]{:S(2)}) collective-permute-start(bf16[72,512]{1,0:T(8,128)(2,1)S(1)} %add_convert_fusion.1), channel_id=1, source_target_pairs={{0,8},{1,9},{2,10},{3,11},{4,12},{5,13},{6,14},{7,15},{8,0},{9,1},... | collective-permute-start | bytes 221192 | tf_op jit(solution)/shard_map/ppermute | solution.py:256
  93.8 1.3 %collective-permute-start.4 = (bf16[72,512]{1,0:T(8,128)(2,1)S(1)}, bf16[72,512]{1,0:T(8,128)(2,1)S(1)}, u32[]{:S(2)}, u32[]{:S(2)}) collective-permute-start(bf16[72,512]{1,0:T(8,128)(2,1)S(1)} %add_convert_fusion.mine_ref), channel_id=1, source_target_pairs={{0,1},{1,0},{2,3},{3,2},{4,5},{5,4},{6,7},{7,6},{8,9},{9,8},{10,11... | collective-permute-start | bytes 221192 | tf_op jit(solution)/shard_map/ppermute | solution.py:256

commit v2 on v1

v2 whole, which is shorter than its diff:
```python
import functools

import jax
import jax.numpy as jnp
from jax import lax
from jax.experimental import pallas as pl
from jax.experimental.pallas import tpu as pltpu
from jax.sharding import PartitionSpec as P

BF = jnp.bfloat16
F32 = jnp.float32
VMEM = pltpu.VMEM
HBM = pltpu.HBM


def shape(dims, dtype=BF):
    return jax.ShapeDtypeStruct(tuple(dims), dtype)


class Placed:
    def __init__(self, memory_space, dims, dtype=BF):
        self.memory_space, self.shape, self.dtype = memory_space, tuple(dims), jnp.dtype(dtype)
        self.size = functools.reduce(lambda a, b: a * b, self.shape, 1)


SMEM = pltpu.SMEM


def call(kernel, outs, tables, arrays, flops, scratch=()):
    moved = sum(a.size * a.dtype.itemsize for a in arrays) + sum(o.size * o.dtype.itemsize for o in outs)
    places = [o.memory_space if isinstance(o, Placed) else VMEM for o in outs]
    return pl.pallas_call(
        kernel,
        out_shape=tuple(o.memory_space(o.shape, o.dtype) if isinstance(o, Placed) else o for o in outs),
        in_specs=[pl.BlockSpec(memory_space=SMEM)] * len(tables) + [pl.BlockSpec(memory_space=VMEM)] * len(arrays),
        out_specs=tuple(pl.BlockSpec(memory_space=place) for place in places),
        scratch_shapes=list(scratch),
        compiler_params=pltpu.CompilerParams(vmem_limit_bytes=32 * 1024 * 1024),
        cost_estimate=pl.CostEstimate(flops=flops, bytes_accessed=moved, transcendentals=0),
    )(*tables, *arrays)


def dot(a, b):
    return jnp.dot(a, b, preferred_element_type=F32)


def dot_nt(a, b):
    return lax.dot_general(a, b, (((1,), (1,)), ((), ())), preferred_element_type=F32)


def to_rows(wide, count):
    width = wide.shape[1] // count
    return jnp.concatenate([wide[:, j * width : (j + 1) * width] for j in range(count)], axis=0)


def to_lanes(tall, count):
    height = tall.shape[0] // count
    return jnp.concatenate([tall[j * height : (j + 1) * height] for j in range(count)], axis=1)


def gates(preact):
    sigma = 0.5 + 0.5 * jnp.tanh(0.5 * preact)
    hidden = preact * sigma
    return hidden, sigma + hidden * (1.0 - sigma)


def repeat(slots, one):
    if slots <= 16:
        for q in range(slots):
            one(q)
    else:
        pl.loop(0, slots)(one)


def advect(read, slots_ref, section, count, stencil, cubic_ref):
    parts = []
    for k in range(stencil):
        rows = [read(slots_ref[section, j, k]).astype(F32) for j in range(count)]
        parts.append(jnp.concatenate(rows, axis=0).astype(BF))
    return to_lanes(dot(jnp.concatenate(parts, axis=1), cubic_ref[...]), count)


def entry_of(sends_ref, section, q):
    cap = sends_ref.shape[2]
    return sends_ref[section, 0, q % cap, q // cap]


def send_blocks(sends_ref, section, slots, source_ref, target, sem):
    def one(q):
        entry = jnp.maximum(entry_of(sends_ref, section, q), 0)
        pltpu.make_async_copy(source_ref.at[entry], target(q), sem).start()

    repeat(slots, one)


def send_terms(ladv, count, stencil, section, slots_ref, cubic_ref, terms_ref, target, sem):
    width = ladv.shape[1] // count
    height = ladv.shape[0]
    terms = dot_nt(to_rows(ladv, count).astype(BF), cubic_ref[...])
    for j in range(count):
        for k in range(stencil):
            block = terms[j * height : (j + 1) * height, k * width : (k + 1) * width]
            terms_ref[j * stencil + k] = block.astype(BF)
            pltpu.make_async_copy(terms_ref.at[j * stencil + k], target(slots_ref[section, j, k]), sem).start()


def collect(sends_ref, section, slots, read, total_ref):
    total_ref[...] = jnp.zeros(total_ref.shape, F32)

    def one(q):
        entry = entry_of(sends_ref, section, q)

        @pl.when(entry >= 0)
        def _():
            total_ref[entry] += read(q).astype(F32)

    repeat(slots, one)


def pack_kernel(slots, slots_in_ref, sends_in_ref, state_in_ref, tangent_in_ref, out_ref, slots_ref, sends_ref,
                state_ref, tangent_ref, in_sems, sem):
    pairs = ((sends_in_ref, sends_ref), (state_in_ref, state_ref), (tangent_in_ref, tangent_ref), (slots_in_ref, slots_ref))
    loads = [pltpu.make_async_copy(a, b, in_sems.at[i]) for i, (a, b) in enumerate(pairs)]
    for load in loads:
        load.start()
    loads[0].wait()
    loads[1].wait()
    send_blocks(sends_ref, 0, slots, state_ref, lambda q: out_ref.at[q, 0], sem)
    loads[2].wait()
    send_blocks(sends_ref, 0, slots, tangent_ref, lambda q: out_ref.at[q, 1], sem)
    loads[3].wait()
    pltpu.make_async_copy(out_ref, out_ref, sem).wait()


def prepare_kernel(w_in_t_ref, w_out_ref, w_in_ref, w_out_t_ref):
    w_in_ref[...] = w_in_t_ref[...].astype(F32).T.astype(BF)
    w_out_t_ref[...] = w_out_ref[...].astype(F32).T.astype(BF)


def first_kernel(count, stencil, slots, slots_ref, sends_ref, recv_ref, cubic_ref, w_in_ref, w_out_ref,
                 send_ref, adv_ref, field_ref, sem):
    adv = advect(lambda q: recv_ref[q, 0], slots_ref, 0, count, stencil, cubic_ref).astype(BF)
    adv_ref[...] = adv
    hidden = gates(dot(w_in_ref[...], adv))[0].astype(BF)
    field = adv.astype(F32) + dot(w_out_ref[...], hidden)
    width = field.shape[1] // count
    for j in range(count):
        field_ref[j] = field[:, j * width : (j + 1) * width].astype(BF)
    send_blocks(sends_ref, 1, slots, field_ref, lambda q: send_ref.at[q], sem)
    pltpu.make_async_copy(send_ref, send_ref, sem).wait()


def tangent_kernel(section, count, stencil, slots_ref, recv_ref, cubic_ref, w_in_ref, w_out_ref, adv_ref, out_ref):
    slope = gates(dot(w_in_ref[...], adv_ref[...]))[1]
    tadv = advect(lambda q: recv_ref[q, 1], slots_ref, section, count, stencil, cubic_ref).astype(BF)
    thid = (slope * dot(w_in_ref[...], tadv)).astype(BF)
    pert = tadv.astype(F32) + dot(w_out_ref[...], thid)
    width = pert.shape[1] // count
    for j in range(count):
        out_ref[j] = pert[:, j * width : (j + 1) * width].astype(BF)


def side_by_side(ref):
    return jnp.concatenate([ref[j] for j in range(ref.shape[0])], axis=1)


def second_kernel(count, stencil, slots, slots_ref, recv_ref, cubic_ref, w_in_ref, w_in_t_ref, w_out_t_ref, cot_ref,
                  send_ref, adv_ref, terms_ref, sem):
    lam = side_by_side(cot_ref)
    adv = advect(lambda q: recv_ref[q], slots_ref, 1, count, stencil, cubic_ref).astype(BF)
    adv_ref[...] = adv
    slope = gates(dot(w_in_ref[...], adv))[1]
    ghid = (slope * dot(w_out_t_ref[...], lam)).astype(BF)
    ladv = lam.astype(F32) + dot(w_in_t_ref[...], ghid)
    send_terms(ladv, count, stencil, 1, slots_ref, cubic_ref, terms_ref, lambda q: send_ref.at[q], sem)
    pltpu.make_async_copy(terms_ref, terms_ref, sem).wait()


def between_kernel(cot_ref, w_in_ref, w_out_t_ref, adv_two_ref, adv_one_ref, in_ref, out_ref, hidden_ref, slope_ref):
    lam = side_by_side(cot_ref)
    adv = adv_two_ref[...]
    hidden, slope = gates(dot(w_in_ref[...], adv))
    ghid = (slope * dot(w_out_t_ref[...], lam)).astype(BF)
    in_ref[...] = dot_nt(adv, ghid)
    out_ref[...] = dot_nt(lam, hidden.astype(BF))
    hidden, slope = gates(dot(w_in_ref[...], adv_one_ref[...]))
    hidden_ref[...] = hidden.astype(BF)
    slope_ref[...] = slope.astype(BF)


def third_kernel(count, stencil, slots, slots_ref, sends_ref, recv_ref, cubic_ref, w_in_t_ref, w_out_t_ref, slope_ref, pert_ref,
                 send_ref, lam_ref, ghid_ref, total_ref, terms_ref, sems):
    send_blocks(sends_ref, 1, slots, pert_ref, lambda q: send_ref.at[q, 1], sems.at[1])
    collect(sends_ref, 1, slots, lambda q: recv_ref[q], total_ref)
    lam = side_by_side(total_ref).astype(BF)
    lam_ref[...] = lam
    ghid = (slope_ref[...].astype(F32) * dot(w_out_t_ref[...], lam)).astype(BF)
    ghid_ref[...] = ghid
    ladv = lam.astype(F32) + dot(w_in_t_ref[...], ghid)
    send_terms(ladv, count, stencil, 0, slots_ref, cubic_ref, terms_ref, lambda q: send_ref.at[q, 0], sems.at[0])
    pltpu.make_async_copy(terms_ref, terms_ref, sems.at[0]).wait()
    half = send_ref.at[pl.ds(0, slots // 2)]
    pltpu.make_async_copy(half, half, sems.at[1]).wait()


def grad_pair_kernel(side_ref, lam_ref, hidden_ref, ghid_ref, adv_ref, in_ref, out_ref, keep_ref, give_ref):
    grad_in = (in_ref[...] + dot_nt(adv_ref[...], ghid_ref[...])).astype(BF)
    grad_out = (out_ref[...] + dot_nt(lam_ref[...], hidden_ref[...])).astype(BF)

    @pl.when(side_ref[0] == 0)
    def _():
        keep_ref[...] = grad_in
        give_ref[...] = grad_out

    @pl.when(side_ref[0] != 0)
    def _():
        keep_ref[...] = grad_out
        give_ref[...] = grad_in


def last_kernel(count, stencil, slots, slots_ref, sends_ref, recv_ref, cubic_ref, w_in_ref, w_out_ref, adv_ref, back_ref, pert_ref):
    collect(sends_ref, 0, slots, lambda q: recv_ref[q, 0], back_ref)
    tangent_kernel(1, count, stencil, slots_ref, recv_ref, cubic_ref, w_in_ref, w_out_ref, adv_ref, pert_ref)


def shards(state, tangent, cotangent, cubic, w_in, w_out, slots, sends):
    count, channels, columns = state.shape
    stencil = cubic.shape[0]
    hid = w_in.shape[0]
    peers = lax.axis_size("lat")
    slot_count = peers * sends.shape[-1]
    wide = count * columns
    block = (channels, columns)
    blocks = (count, *block)
    side = lax.axis_index("lat") % 2
    sends = jnp.transpose(sends, (0, 1, 3, 2))
    cubic = cubic.reshape(stencil * columns, columns)
    w_in_t = w_in.T
    mix = 2 * wide * channels * stencil * columns
    net = 2 * wide * channels * hid
    sizes = (count, stencil, slot_count)
    sem = pltpu.SemaphoreType.DMA

    def exchange(packed):
        return lax.all_to_all(packed, "lat", split_axis=0, concat_axis=0, tiled=True)

    def swap(values, step):
        return lax.ppermute(values, "lat", [(i, i ^ step) for i in range(peers)])

    def add(a, b):
        return (a.astype(F32) + b.astype(F32)).astype(BF)

    send, slots, sends = pl.pallas_call(
        functools.partial(pack_kernel, slot_count),
        out_shape=(HBM((slot_count, 2, *block), BF), SMEM(slots.shape, slots.dtype), SMEM(sends.shape, sends.dtype)),
        in_specs=[pl.BlockSpec(memory_space=HBM)] * 4,
        out_specs=(pl.BlockSpec(memory_space=HBM), pl.BlockSpec(memory_space=SMEM), pl.BlockSpec(memory_space=SMEM)),
        scratch_shapes=[VMEM(blocks, BF), VMEM(blocks, BF), sem((4,)), sem],
    )(*(pltpu.with_memory_space_constraint(a, HBM) for a in (slots, sends, state, tangent)))
    recv_one = exchange(send)
    w_in, w_out_t = call(prepare_kernel, [shape((hid, channels)), shape((hid, channels))], [], [w_in_t, w_out], 0)
    send, adv_one = call(
        functools.partial(first_kernel, *sizes),
        [Placed(HBM, (slot_count, *block)), shape((channels, wide))],
        [slots, sends], [recv_one, cubic, w_in, w_out], mix + 2 * net, [VMEM(blocks, BF), sem],
    )
    recv_two = exchange(send)
    (pert_one,) = call(
        functools.partial(tangent_kernel, 0, count, stencil),
        [shape(blocks)], [slots], [recv_one, cubic, w_in, w_out, adv_one], mix + 3 * net,
    )
    recv_two, pert_one = lax.optimization_barrier((recv_two, pert_one))
    send, adv_two = call(
        functools.partial(second_kernel, *sizes),
        [Placed(HBM, (slot_count, *block)), shape((channels, wide))],
        [slots], [recv_two, cubic, w_in, w_in_t, w_out_t, cotangent], 2 * mix + 3 * net,
        [VMEM((count * stencil, *block), BF), sem],
    )
    recv_three = exchange(send)
    part_in, part_out, hidden_one, slope_one = call(
        between_kernel,
        [shape((channels, hid), F32)] * 2 + [shape((hid, wide))] * 2,
        [], [cotangent, w_in, w_out_t, adv_two, adv_one], 5 * net,
    )
    send, lam_one, ghid_one = call(
        functools.partial(third_kernel, *sizes),
        [Placed(HBM, (slot_count, 2, *block)), shape((channels, wide)), shape((hid, wide))],
        [slots, sends], [recv_three, cubic, w_in_t, w_out_t, slope_one, pert_one], mix + 2 * net,
        [VMEM(blocks, F32), VMEM((count * stencil, *block), BF), sem((2,))],
    )
    recv_four = exchange(send)
    mine, give = call(
        grad_pair_kernel,
        [shape((channels, hid))] * 2, [side.astype(jnp.int32).reshape(1)],
        [lam_one, hidden_one, ghid_one, adv_one, part_in, part_out], 2 * net,
    )
    mine = add(mine, swap(give, 1))
    step = 2
    while step < peers:
        mine = add(mine, swap(mine, step))
        step *= 2
    mine, recv_four = lax.optimization_barrier((mine, recv_four))
    back, pert = call(
        functools.partial(last_kernel, *sizes),
        [shape(blocks, F32), shape(blocks)],
        [slots, sends], [recv_four, cubic, w_in, w_out, adv_two], mix + 3 * net,
    )
    other = swap(mine, 1)
    grad_in = jnp.where(side == 0, mine, other).astype(F32).T
    grad_out = jnp.where(side == 0, other, mine).astype(F32)
    return (pert, back, grad_in, grad_out)


def solution(mesh):
    in_specs = (
        P(("grp", "lat"), None, None),
        P(("grp", "lat"), None, None),
        P(("grp", "lat"), None, None),
        P(),
        P(),
        P(),
        P("grp", "lat", None),
        P("grp", "lat", None, None),
    )
    out_specs = (
        P(("grp", "lat"), None, None),
        P(("grp", "lat"), None, None),
        P("grp", None),
        P("grp", None),
    )
    return jax.shard_map(shards, mesh=mesh, in_specs=in_specs, out_specs=out_specs, check_vma=False)
```

time: 99.6 us -> 86.4 us (0.87)
  local copies, waits for them, and re-layouts: 13 us -> 0.03 us
  Pallas kernels: 12.9 us -> 11 us
  waiting for transfers between devices: 45.7 us -> 47.5 us
    unnamed x59 -> x8, local copies, waits for them, and re-layouts: 12.8 us -> 0.03 us
    all_to_all x4, waiting for transfers between devices: 31.2 us -> 34.3 us  [exchange(): lax.all_to_all(packed, 'lat', split_axis=0, concat_axis=0, tiled=True)]
    pallas_call x10 -> x9, Pallas kernels: 12.9 us -> 11 us  [the longest x8 9.2 us: call(): pl.pallas_call(kernel, out_shape=tuple((o.memory_space(o.shape, o.dtype)...]
    ppermute x5, waiting for transfers between devices: 14.4 us -> 13.2 us  [swap(): return lax.ppermute(values, 'lat', [(i, i ^ step) for i in range(peers)])]
  transfers between devices with their start and end apart: 9 -> 9, of which waited for: 7 -> 6; matrix products, arithmetic and copies ran while one was open for 1% -> 0% of each run, Pallas kernels for 3% -> 5%
where the time goes in v2:
time: 86.4 us; the launch traced here: 85.7 us
  waiting for transfers between devices  47.5 us (55%)
  starting transfers between devices  25.5 us (30%)
  Pallas kernels  11 us (13%)
    all_to_all x4, waiting for transfers between devices, exchange(): lax.all_to_all(packed, 'lat', split_axis=0, concat_axis=0, tiled=True)  34.3 us
    all_to_all x4, starting transfers between devices, exchange(): lax.all_to_all(packed, 'lat', split_axis=0, concat_axis=0, tiled=True)  19.1 us
    ppermute x5, waiting for transfers between devices, swap(): return lax.ppermute(values, 'lat', [(i, i ^ step) for i in range(peers)])  13.2 us
    pallas_call x8, Pallas kernels, call(): pl.pallas_call(kernel, out_shape=tuple((o.memory_space(o.shape, o.dtype)...  9.2 us
    ppermute x5, starting transfers between devices, swap(): return lax.ppermute(values, 'lat', [(i, i ^ step) for i in range(peers)])  6.45 us
    pallas_call x1, Pallas kernels, shards(): pl.pallas_call(functools.partial(pack_kernel, slot_count), out_shape=(HBM...  1.76 us
  transfers between devices with their start and end apart: 9, of which 6 were waited for; matrix products, arithmetic and copies ran while one was open for 0% of the time, Pallas kernels for 5%

profile of v2, /device:TPU:0, one launch (start us, length us, event | category | flops | bytes accessed | tf_op | source)
XLA Modules:
  0.0 85.7 jit_solution(16492280135444241047)
XLA Ops:
  0.6 1.8 %shard_map.111 = (bf16[16,2,72,128]{3,2,1,0:T(8,128)(2,1)}, s32[2,4,4]{2,1,0:T(4,128)S(4)}, s32[2,1,1,16]{3,2,1,0:T(1,128)S(4)}) custom-call(s32[2,4,4]{2,1,0:T(4,128)} %slots_in_ref.1, s32[2,1,1,16]{3,2,1,0:T(1,128)} %bitcast.16, bf16[4,72,128]{2,1,0:T(8,128)(2,1)} %state_in_ref.1, bf16[4,72,128]{2,1,0:T(8,128)(2,1)} %tangent_in_ref.1), custom_call_target="tpu_custom_call" | custom-call | tf_op jit(solution)/shard_map/pallas_call | solution.py:253
  2.4 0.0 copy-start.1
  2.4 0.0 copy-start.2
  2.4 7.5 %all-to-all-start = ((bf16[16,2,72,128]{3,2,1,0:T(8,128)(2,1)}), bf16[16,2,72,128]{3,2,1,0:T(8,128)(2,1)S(1)}, u32[]{:S(2)}, u32[]{:S(2)}) async-start(bf16[16,2,72,128]{3,2,1,0:T(8,128)(2,1)} %get-tuple-element.30), calls=%async_computation | async-start | bytes 1179648 | tf_op jit(solution)/shard_map/all_to_all | solution.py:245
  9.9 0.0 copy-start
  9.9 0.0 copy-done.1
  10.0 0.0 copy-done.2
  10.0 0.1 shard_map.112
  10.1 15.4 %all-to-all-done.recv_ref = bf16[16,2,72,128]{3,2,1,0:T(8,128)(2,1)S(1)} async-done(((bf16[16,2,72,128]{3,2,1,0:T(8,128)(2,1)}), bf16[16,2,72,128]{3,2,1,0:T(8,128)(2,1)S(1)}, u32[]{:S(2)}, u32[]{:S(2)}) %all-to-all-start) | async-done | bytes 589856 | tf_op jit(solution)/shard_map/all_to_all | solution.py:245
  25.5 0.0 copy-done
  25.5 1.5 %shard_map.113 = (bf16[16,72,128]{2,1,0:T(8,128)(2,1)}, bf16[72,512]{1,0:T(8,128)(2,1)S(1)}) custom-call(s32[2,4,4]{2,1,0:T(4,128)S(4)} %get-tuple-element.28.slots_ref, s32[2,1,1,16]{3,2,1,0:T(1,128)S(4)} %get-tuple-element.29.sends_ref, bf16[16,2,72,128]{3,2,1,0:T(8,128)(2,1)S(1)} %all-to-all-done.recv_ref, bf16[512,128]{1,0:T(8,128)(2,1)S(1)} %bitcast.8, ...), custom_call_target="tpu_custom_call" | custom-call | flops 113246208 | bytes 1236992 | tf_op jit(solution)/shard_map/pallas_call | solution.py:32
  27.0 4.4 %all-to-all-start.1 = ((bf16[16,72,128]{2,1,0:T(8,128)(2,1)}), bf16[16,72,128]{2,1,0:T(8,128)(2,1)S(1)}, u32[]{:S(2)}, u32[]{:S(2)}) async-start(bf16[16,72,128]{2,1,0:T(8,128)(2,1)} %get-tuple-element.32), calls=%async_computation.1 | async-start | bytes 589824 | tf_op jit(solution)/shard_map/all_to_all | solution.py:245
  31.5 0.0 copy-start.3
  31.5 0.9 %shard_map.114.pert_ref = bf16[4,72,128]{2,1,0:T(8,128)(2,1)S(1)} custom-call(s32[2,4,4]{2,1,0:T(4,128)S(4)} %get-tuple-element.28.slots_ref, bf16[16,2,72,128]{3,2,1,0:T(8,128)(2,1)S(1)} %all-to-all-done.recv_ref, bf16[512,128]{1,0:T(8,128)(2,1)S(1)} %bitcast.9, bf16[512,72]{1,0:T(8,128)(2,1)S(1)} %get-tuple-element.31.w_in_ref, ...), custom_call_target="tpu_custom_call" | custom-call | flops 150994944 | bytes 1015808 | tf_op jit(solution)/shard_map/pallas_call | solution.py:32
  32.4 9.6 %all-to-all-done.1.recv_ref = bf16[16,72,128]{2,1,0:T(8,128)(2,1)S(1)} async-done(((bf16[16,72,128]{2,1,0:T(8,128)(2,1)}), bf16[16,72,128]{2,1,0:T(8,128)(2,1)S(1)}, u32[]{:S(2)}, u32[]{:S(2)}) %all-to-all-start.1) | async-done | bytes 294944 | tf_op jit(solution)/shard_map/all_to_all | solution.py:245
  42.0 0.0 copy-done.3
  42.0 1.8 %shard_map.115 = (bf16[16,72,128]{2,1,0:T(8,128)(2,1)}, bf16[72,512]{1,0:T(8,128)(2,1)S(1)}) custom-call(s32[2,4,4]{2,1,0:T(4,128)S(4)} %get-tuple-element.28.slots_ref, bf16[16,72,128]{2,1,0:T(8,128)(2,1)S(1)} %all-to-all-done.1.recv_ref, bf16[512,128]{1,0:T(8,128)(2,1)S(1)} %bitcast.10, bf16[512,72]{1,0:T(8,128)(2,1)S(1)} %get-tuple-element.31.w_in_ref, ...), custom_call_target="tpu_custom_call" | custom-call | flops 188743680 | bytes 1089536 | tf_op jit(solution)/shard_map/pallas_call | solution.py:32
  43.8 3.5 %all-to-all-start.2 = ((bf16[16,72,128]{2,1,0:T(8,128)(2,1)}), bf16[16,72,128]{2,1,0:T(8,128)(2,1)S(1)}, u32[]{:S(2)}, u32[]{:S(2)}) async-start(bf16[16,72,128]{2,1,0:T(8,128)(2,1)} %get-tuple-element.36), calls=%async_computation.2 | async-start | bytes 589824 | tf_op jit(solution)/shard_map/all_to_all | solution.py:245
  47.4 1.2 %shard_map.116 = (f32[72,512]{1,0:T(8,128)S(1)}, f32[72,512]{1,0:T(8,128)S(1)}, bf16[512,512]{1,0:T(8,128)(2,1)S(1)}, bf16[512,512]{1,0:T(8,128)(2,1)S(1)}) custom-call(bf16[4,72,128]{2,1,0:T(8,128)(2,1)S(1)} %copy-done.3, bf16[512,72]{1,0:T(8,128)(2,1)S(1)} %get-tuple-element.31.w_in_ref, bf16[512,72]{1,0:T(8,128)(2,1)S(1)} %get-tuple-element.35.w_out_t_ref, ...), custom_call_target="tpu_custom_call" | custom-call | flops 188743680 | bytes 1712128 | tf_op jit(solution)/shard_map/pallas_call | solution.py:32
  48.5 9.3 %all-to-all-done.2.recv_ref = bf16[16,72,128]{2,1,0:T(8,128)(2,1)S(1)} async-done(((bf16[16,72,128]{2,1,0:T(8,128)(2,1)}), bf16[16,72,128]{2,1,0:T(8,128)(2,1)S(1)}, u32[]{:S(2)}, u32[]{:S(2)}) %all-to-all-start.2) | async-done | bytes 294944 | tf_op jit(solution)/shard_map/all_to_all | solution.py:245
  57.9 1.5 %shard_map.117 = (bf16[16,2,72,128]{3,2,1,0:T(8,128)(2,1)}, bf16[72,512]{1,0:T(8,128)(2,1)S(1)}, bf16[512,512]{1,0:T(8,128)(2,1)S(1)}) custom-call(s32[2,4,4]{2,1,0:T(4,128)S(4)} %get-tuple-element.28.slots_ref, s32[2,1,1,16]{3,2,1,0:T(1,128)S(4)} %get-tuple-element.29.sends_ref, bf16[16,72,128]{2,1,0:T(8,128)(2,1)S(1)} %all-to-all-done.2.recv_ref, ...), custom_call_target="tpu_custom_call" | custom-call | flops 113246208 | bytes 2359296 | tf_op jit(solution)/shard_map/pallas_call | solution.py:32
  59.4 0.5 shard_map.118
  59.9 0.1 collective-permute-start
  60.0 3.6 %all-to-all-start.3 = ((bf16[16,2,72,128]{3,2,1,0:T(8,128)(2,1)}), bf16[16,2,72,128]{3,2,1,0:T(8,128)(2,1)S(1)}, u32[]{:S(2)}, u32[]{:S(2)}) async-start(bf16[16,2,72,128]{3,2,1,0:T(8,128)(2,1)} %get-tuple-element.47), calls=%async_computation.3 | async-start | bytes 1179648 | tf_op jit(solution)/shard_map/all_to_all | solution.py:245
  63.6 0.0 collective-permute-done
  63.6 1.9 %collective-permute-start.1 = (bf16[72,512]{1,0:T(8,128)(2,1)S(1)}, bf16[72,512]{1,0:T(8,128)(2,1)S(1)}, u32[]{:S(2)}, u32[]{:S(2)}) collective-permute-start(bf16[72,512]{1,0:T(8,128)(2,1)S(1)} %add_convert_fusion.3), channel_id=1, source_target_pairs={{0,2},{1,3},{2,0},{3,1},{4,6},{5,7},{6,4},{7,5},{8,10},{9,11},{10,... | collective-permute-start | bytes 221192 | tf_op jit(solution)/shard_map/ppermute | solution.py:248
  65.5 6.4 %collective-permute-done.1 = bf16[72,512]{1,0:T(8,128)(2,1)S(1)} collective-permute-done((bf16[72,512]{1,0:T(8,128)(2,1)S(1)}, bf16[72,512]{1,0:T(8,128)(2,1)S(1)}, u32[]{:S(2)}, u32[]{:S(2)}) %collective-permute-start.1) | collective-permute-done | bytes 73760 | tf_op jit(solution)/shard_map/ppermute | solution.py:248
  71.9 0.7 collective-permute-start.2
  72.6 4.0 %collective-permute-done.2 = bf16[72,512]{1,0:T(8,128)(2,1)S(1)} collective-permute-done((bf16[72,512]{1,0:T(8,128)(2,1)S(1)}, bf16[72,512]{1,0:T(8,128)(2,1)S(1)}, u32[]{:S(2)}, u32[]{:S(2)}) %collective-permute-start.2) | collective-permute-done | bytes 73760 | tf_op jit(solution)/shard_map/ppermute | solution.py:248
  76.6 3.7 %collective-permute-start.3 = (bf16[72,512]{1,0:T(8,128)(2,1)S(1)}, bf16[72,512]{1,0:T(8,128)(2,1)S(1)}, u32[]{:S(2)}, u32[]{:S(2)}) collective-permute-start(bf16[72,512]{1,0:T(8,128)(2,1)S(1)} %add_convert_fusion.1), channel_id=1, source_target_pairs={{0,8},{1,9},{2,10},{3,11},{4,12},{5,13},{6,14},{7,15},{8,0},{9,1},... | collective-permute-start | bytes 221192 | tf_op jit(solution)/shard_map/ppermute | solution.py:248
  80.3 2.8 %collective-permute-done.3 = bf16[72,512]{1,0:T(8,128)(2,1)S(1)} collective-permute-done((bf16[72,512]{1,0:T(8,128)(2,1)S(1)}, bf16[72,512]{1,0:T(8,128)(2,1)S(1)}, u32[]{:S(2)}, u32[]{:S(2)}) %collective-permute-start.3) | collective-permute-done | bytes 73760 | tf_op jit(solution)/shard_map/ppermute | solution.py:248
  83.2 0.0 all-to-all-done.3.recv_ref
  83.2 0.1 collective-permute-start.4
  83.3 1.7 %shard_map.119 = (f32[4,72,128]{2,1,0:T(8,128)}, bf16[4,72,128]{2,1,0:T(8,128)(2,1)}) custom-call(s32[2,4,4]{2,1,0:T(4,128)S(4)} %get-tuple-element.28.slots_ref, s32[2,1,1,16]{3,2,1,0:T(1,128)S(4)} %get-tuple-element.29.sends_ref, bf16[16,2,72,128]{3,2,1,0:T(8,128)(2,1)S(1)} %all-to-all-done.3.recv_ref, bf16[512,128]{1,0:T(8,128)(2,1)S(1)} %bitcast.12, ...), custom_call_target="tpu_custom_call" | custom-call | flops 150994944 | bytes 1163264 | tf_op jit(solution)/shard_map/pallas_call | solution.py:32
  85.0 0.0 collective-permute-done.4
  85.0 0.7 select_convert_fusion
  (4 shorter events, 0.1 us)
Async XLA Ops:
  2.4 7.5 %copy-start.1 = (bf16[72,512]{1,0:T(8,128)(2,1)S(1)}, bf16[72,512]{1,0:T(8,128)(2,1)}, u32[]{:S(2)}) copy-start(bf16[72,512]{1,0:T(8,128)(2,1)} %w_out_ref.7) | copy-start | bytes 221188
  2.4 7.5 %copy-start.2 = (bf16[512,72]{0,1:T(8,128)(2,1)S(1)}, bf16[512,72]{0,1:T(8,128)(2,1)}, u32[]{:S(2)}) copy-start(bf16[512,72]{0,1:T(8,128)(2,1)} %param.12) | copy-start | bytes 221188
  2.4 23.1 %all-to-all-start = ((bf16[16,2,72,128]{3,2,1,0:T(8,128)(2,1)}), bf16[16,2,72,128]{3,2,1,0:T(8,128)(2,1)S(1)}, u32[]{:S(2)}, u32[]{:S(2)}) async-start(bf16[16,2,72,128]{3,2,1,0:T(8,128)(2,1)} %get-tuple-element.30), calls=%async_computation | async-start | bytes 1179648 | tf_op jit(solution)/shard_map/all_to_all | solution.py:245
  9.9 15.6 %copy-start = (bf16[4,128,128]{2,1,0:T(8,128)(2,1)S(1)}, bf16[4,128,128]{2,1,0:T(8,128)(2,1)}, u32[]{:S(2)}) copy-start(bf16[4,128,128]{2,1,0:T(8,128)(2,1)} %param.11) | copy-start | bytes 393220
  27.0 15.0 %all-to-all-start.1 = ((bf16[16,72,128]{2,1,0:T(8,128)(2,1)}), bf16[16,72,128]{2,1,0:T(8,128)(2,1)S(1)}, u32[]{:S(2)}, u32[]{:S(2)}) async-start(bf16[16,72,128]{2,1,0:T(8,128)(2,1)} %get-tuple-element.32), calls=%async_computation.1 | async-start | bytes 589824 | tf_op jit(solution)/shard_map/all_to_all | solution.py:245
  31.5 10.6 %copy-start.3 = (bf16[4,72,128]{2,1,0:T(8,128)(2,1)S(1)}, bf16[4,72,128]{2,1,0:T(8,128)(2,1)}, u32[]{:S(2)}) copy-start(bf16[4,72,128]{2,1,0:T(8,128)(2,1)} %cot_ref.3) | copy-start | bytes 221188
  43.8 14.1 %all-to-all-start.2 = ((bf16[16,72,128]{2,1,0:T(8,128)(2,1)}), bf16[16,72,128]{2,1,0:T(8,128)(2,1)S(1)}, u32[]{:S(2)}, u32[]{:S(2)}) async-start(bf16[16,72,128]{2,1,0:T(8,128)(2,1)} %get-tuple-element.36), calls=%async_computation.2 | async-start | bytes 589824 | tf_op jit(solution)/shard_map/all_to_all | solution.py:245
  59.9 3.7 %collective-permute-start = (bf16[72,512]{1,0:T(8,128)(2,1)S(1)}, bf16[72,512]{1,0:T(8,128)(2,1)S(1)}, u32[]{:S(2)}, u32[]{:S(2)}) collective-permute-start(bf16[72,512]{1,0:T(8,128)(2,1)S(1)} %get-tuple-element.46), channel_id=1, source_target_pairs={{0,1},{1,0},{2,3},{3,2},{4,5},{5,4},{6,7},{7,6},{8,9},{9,8},{10,11... | collective-permute-start | bytes 221192 | tf_op jit(solution)/shard_map/ppermute | solution.py:248
  60.0 23.2 %all-to-all-start.3 = ((bf16[16,2,72,128]{3,2,1,0:T(8,128)(2,1)}), bf16[16,2,72,128]{3,2,1,0:T(8,128)(2,1)S(1)}, u32[]{:S(2)}, u32[]{:S(2)}) async-start(bf16[16,2,72,128]{3,2,1,0:T(8,128)(2,1)} %get-tuple-element.47), calls=%async_computation.3 | async-start | bytes 1179648 | tf_op jit(solution)/shard_map/all_to_all | solution.py:245
  63.6 8.3 %collective-permute-start.1 = (bf16[72,512]{1,0:T(8,128)(2,1)S(1)}, bf16[72,512]{1,0:T(8,128)(2,1)S(1)}, u32[]{:S(2)}, u32[]{:S(2)}) collective-permute-start(bf16[72,512]{1,0:T(8,128)(2,1)S(1)} %add_convert_fusion.3), channel_id=1, source_target_pairs={{0,2},{1,3},{2,0},{3,1},{4,6},{5,7},{6,4},{7,5},{8,10},{9,11},{10,... | collective-permute-start | bytes 221192 | tf_op jit(solution)/shard_map/ppermute | solution.py:248
  71.9 4.7 %collective-permute-start.2 = (bf16[72,512]{1,0:T(8,128)(2,1)S(1)}, bf16[72,512]{1,0:T(8,128)(2,1)S(1)}, u32[]{:S(2)}, u32[]{:S(2)}) collective-permute-start(bf16[72,512]{1,0:T(8,128)(2,1)S(1)} %add_convert_fusion.2), channel_id=1, source_target_pairs={{0,4},{1,5},{2,6},{3,7},{4,0},{5,1},{6,2},{7,3},{8,12},{9,13},{10,... | collective-permute-start | bytes 221192 | tf_op jit(solution)/shard_map/ppermute | solution.py:248
  76.6 6.5 %collective-permute-start.3 = (bf16[72,512]{1,0:T(8,128)(2,1)S(1)}, bf16[72,512]{1,0:T(8,128)(2,1)S(1)}, u32[]{:S(2)}, u32[]{:S(2)}) collective-permute-start(bf16[72,512]{1,0:T(8,128)(2,1)S(1)} %add_convert_fusion.1), channel_id=1, source_target_pairs={{0,8},{1,9},{2,10},{3,11},{4,12},{5,13},{6,14},{7,15},{8,0},{9,1},... | collective-permute-start | bytes 221192 | tf_op jit(solution)/shard_map/ppermute | solution.py:248
  83.2 1.8 %collective-permute-start.4 = (bf16[72,512]{1,0:T(8,128)(2,1)S(1)}, bf16[72,512]{1,0:T(8,128)(2,1)S(1)}, u32[]{:S(2)}, u32[]{:S(2)}) collective-permute-start(bf16[72,512]{1,0:T(8,128)(2,1)S(1)} %add_convert_fusion), channel_id=1, source_target_pairs={{0,1},{1,0},{2,3},{3,2},{4,5},{5,4},{6,7},{7,6},{8,9},{9,8},{10,11... | collective-permute-start | bytes 221192 | tf_op jit(solution)/shard_map/ppermute | solution.py:248

commit v3 on v2

v3 whole, which is shorter than its diff:
```python
import functools

import jax
import jax.numpy as jnp
from jax import lax
from jax.experimental import pallas as pl
from jax.experimental.pallas import tpu as pltpu
from jax.sharding import PartitionSpec as P

BF = jnp.bfloat16
F32 = jnp.float32
VMEM = pltpu.VMEM
HBM = pltpu.HBM


def shape(dims, dtype=BF):
    return jax.ShapeDtypeStruct(tuple(dims), dtype)


class Placed:
    def __init__(self, memory_space, dims, dtype=BF):
        self.memory_space, self.shape, self.dtype = memory_space, tuple(dims), jnp.dtype(dtype)
        self.size = functools.reduce(lambda a, b: a * b, self.shape, 1)


SMEM = pltpu.SMEM


def call(kernel, outs, tables, arrays, flops, scratch=()):
    moved = sum(a.size * a.dtype.itemsize for a in arrays) + sum(o.size * o.dtype.itemsize for o in outs)
    places = [o.memory_space if isinstance(o, Placed) else VMEM for o in outs]
    return pl.pallas_call(
        kernel,
        out_shape=tuple(o.memory_space(o.shape, o.dtype) if isinstance(o, Placed) else o for o in outs),
        in_specs=[pl.BlockSpec(memory_space=SMEM)] * len(tables) + [pl.BlockSpec(memory_space=VMEM)] * len(arrays),
        out_specs=tuple(pl.BlockSpec(memory_space=place) for place in places),
        scratch_shapes=list(scratch),
        compiler_params=pltpu.CompilerParams(vmem_limit_bytes=32 * 1024 * 1024),
        cost_estimate=pl.CostEstimate(flops=flops, bytes_accessed=moved, transcendentals=0),
    )(*tables, *arrays)


def dot(a, b):
    return jnp.dot(a, b, preferred_element_type=F32)


def dot_nt(a, b):
    return lax.dot_general(a, b, (((1,), (1,)), ((), ())), preferred_element_type=F32)


def to_rows(wide, count):
    width = wide.shape[1] // count
    return jnp.concatenate([wide[:, j * width : (j + 1) * width] for j in range(count)], axis=0)


def to_lanes(tall, count):
    height = tall.shape[0] // count
    return jnp.concatenate([tall[j * height : (j + 1) * height] for j in range(count)], axis=1)


def gates(preact):
    sigma = 0.5 + 0.5 * jnp.tanh(0.5 * preact)
    hidden = preact * sigma
    return hidden, sigma + hidden * (1.0 - sigma)


def repeat(slots, one):
    if slots <= 16:
        for q in range(slots):
            one(q)
    else:
        pl.loop(0, slots)(one)


def advect(read, count, stencil, cubic_ref):
    parts = [jnp.concatenate([read(t, k) for t in range(count)], axis=0) for k in range(stencil)]
    return to_lanes(dot(jnp.concatenate(parts, axis=1), cubic_ref[...]), count)


def entry_of(sends_ref, section, q):
    cap = sends_ref.shape[2]
    return sends_ref[section, 0, q % cap, q // cap]


def send_terms(ladv, count, stencil, section, slots_ref, cubic_ref, terms_ref, target, sem):
    width = ladv.shape[1] // count
    height = ladv.shape[0]
    terms = dot_nt(to_rows(ladv, count).astype(BF), cubic_ref[...])
    for j in range(count):
        for k in range(stencil):
            block = terms[j * height : (j + 1) * height, k * width : (k + 1) * width]
            terms_ref[j * stencil + k] = block.astype(BF)
            pltpu.make_async_copy(terms_ref.at[j * stencil + k], target(slots_ref[section, j, k]), sem).start()


def collect(sends_ref, section, slots, read, total_ref):
    total_ref[...] = jnp.zeros(total_ref.shape, F32)

    def one(q):
        entry = entry_of(sends_ref, section, q)

        @pl.when(entry >= 0)
        def _():
            total_ref[entry] += read(q).astype(F32)

    repeat(slots, one)


def padded(block, rows):
    block = block.astype(F32)
    return jnp.concatenate([block, jnp.zeros((rows - block.shape[0], block.shape[1]), F32)], axis=0)


def own_kernel(slots_in_ref, sends_in_ref, state_in_ref, out_ref, slots_ref, sends_ref, state_ref, note_ref, sems):
    pairs = ((sends_in_ref, sends_ref), (slots_in_ref, slots_ref), (state_in_ref, state_ref))
    loads = [pltpu.make_async_copy(a, b, sems.at[i]) for i, (a, b) in enumerate(pairs)]
    for load in loads:
        load.start()
    for load in loads:
        load.wait()
    count, channels, _ = state_ref.shape
    rows = out_ref.shape[1]
    note_ref[...] = jnp.zeros(note_ref.shape, F32)
    for section in range(sends_ref.shape[0]):
        note_ref[section : section + 1, : sends_ref.shape[3]] = sends_ref[section, 0].astype(F32)
    note_ref[4 : 4 + count, : slots_ref.shape[2]] = slots_ref[0].astype(F32)
    for j in range(1, count):
        out_ref[j] = padded(state_ref[j], rows).astype(BF)
    out_ref[0] = jnp.concatenate([state_ref[0].astype(F32), note_ref[...]], axis=0).astype(BF)


def own_tangent_kernel(slots_in_ref, sends_in_ref, tangent_in_ref, out_ref, slots_ref, sends_ref, tangent_ref, sems):
    pairs = ((sends_in_ref, sends_ref), (slots_in_ref, slots_ref), (tangent_in_ref, tangent_ref))
    loads = [pltpu.make_async_copy(a, b, sems.at[i]) for i, (a, b) in enumerate(pairs)]
    for load in loads:
        load.start()
    for load in loads:
        load.wait()
    for j in range(tangent_ref.shape[0]):
        out_ref[j] = padded(tangent_ref[j], out_ref.shape[1]).astype(BF)


def prepare_kernel(w_in_t_ref, w_out_ref, cubic_in_ref, cot_ref, w_in_ref, w_out_pad_ref, w_out_t_ref, cubic_ref, lam_ref):
    cubic_ref[...] = cubic_in_ref[...]
    lam_ref[...] = side_by_side(cot_ref)
    rows = w_out_pad_ref.shape[0]
    w_in_ref[...] = padded(w_in_t_ref[...], rows).T.astype(BF)
    w_out_pad_ref[...] = padded(w_out_ref[...], rows).astype(BF)
    w_out_t_ref[...] = w_out_ref[...].astype(F32).T.astype(BF)


def routes(peers, count, stencil, slots_ref, blocks_ref, notes_ref, tables_ref, route_ref, sem):
    me = lax.axis_index("lat")

    def place(device):
        differs = device ^ me
        return (differs & 1) * (peers // 2) + (differs >> 1)

    def read_note(r):
        block = blocks_ref[r * count].astype(F32)
        notes_ref[r] = block[block.shape[0] - notes_ref.shape[1] :].astype(jnp.int32)

    repeat(peers, read_note)
    pltpu.make_async_copy(notes_ref, tables_ref, sem).start()
    pltpu.make_async_copy(notes_ref, tables_ref, sem).wait()

    def fill(t, device, block):
        for k in range(stencil):
            owner = tables_ref[place(device), 4 + block, k]
            entry = jnp.maximum(tables_ref[place(owner), 0, device], 0)
            route_ref[t, k] = place(owner) * count + entry

    for k in range(stencil):
        for j in range(count):
            device = slots_ref[1, j, k]
            fill(k * count + j, device, jnp.maximum(tables_ref[place(device), 1, me], 0))
    for j in range(count):
        fill(stencil * count + j, me, j)


def forward_kernel(peers, count, stencil, slots_ref, blocks_ref, cubic_ref, w_in_ref, w_out_ref, w_in_t_ref, w_out_t_ref, lam_two_ref,
                   send_ref, adv_one_ref, adv_ref, route_ref, notes_ref, tables_ref, terms_ref, sem, note_sem):
    routes(peers, count, stencil, slots_ref, blocks_ref, notes_ref, tables_ref, route_ref, note_sem)
    everyone = (stencil + 1) * count
    adv = advect(lambda t, k: blocks_ref[route_ref[t, k]], everyone, stencil, cubic_ref)
    wide = adv.shape[1] // (stencil + 1)
    columns = wide // count
    adv_one_ref[...] = adv.astype(BF)
    fields = []
    for k in range(stencil):
        part = adv_one_ref[:, k * wide : (k + 1) * wide]
        hidden = gates(dot(w_in_ref[...], part))[0].astype(BF)
        fields.append((part.astype(F32) + dot(w_out_ref[...], hidden)).astype(BF))
    adv = advect(lambda j, k: fields[k][:, j * columns : (j + 1) * columns], count, stencil, cubic_ref).astype(BF)
    adv_ref[...] = adv
    lam = lam_two_ref[...]
    slope = gates(dot(w_in_ref[...], adv))[1]
    ghid = (slope * dot(w_out_t_ref[...], lam)).astype(BF)
    ladv = lam.astype(F32) + dot(w_in_t_ref[...], ghid)
    send_terms(ladv, count, stencil, 1, slots_ref, cubic_ref, terms_ref, lambda q: send_ref.at[q], sem)
    pltpu.make_async_copy(terms_ref, terms_ref, sem).wait()


def tangent_kernel(count, stencil, route_ref, blocks_ref, cubic_ref, w_in_ref, w_out_ref, adv_one_ref, adv_two_ref, out_ref):
    def step(adv, tadv):
        slope = gates(dot(w_in_ref[...], adv))[1]
        thid = (slope * dot(w_in_ref[...], tadv)).astype(BF)
        return tadv.astype(F32) + dot(w_out_ref[...], thid)

    tadv = advect(lambda t, k: blocks_ref[route_ref[t, k]], stencil * count, stencil, cubic_ref).astype(BF)
    wide = tadv.shape[1] // stencil
    columns = wide // count
    fields = []
    for k in range(stencil):
        fields.append(step(adv_one_ref[:, k * wide : (k + 1) * wide], tadv[:, k * wide : (k + 1) * wide]).astype(BF))
    tadv = advect(lambda j, k: fields[k][:, j * columns : (j + 1) * columns], count, stencil, cubic_ref).astype(BF)
    pert = step(adv_two_ref[...], tadv)
    channels = out_ref.shape[1]
    for j in range(count):
        out_ref[j] = pert[:channels, j * columns : (j + 1) * columns].astype(BF)


def side_by_side(ref):
    return jnp.concatenate([ref[j] for j in range(ref.shape[0])], axis=1)


def between_kernel(lam_two_ref, w_in_ref, w_out_t_ref, adv_two_ref, adv_all_ref, in_ref, out_ref, adv_one_ref, hidden_ref, slope_ref):
    lam = lam_two_ref[...]
    channels, wide = lam.shape
    adv = adv_two_ref[...]
    hidden, slope = gates(dot(w_in_ref[...], adv))
    ghid = (slope * dot(w_out_t_ref[...], lam)).astype(BF)
    in_ref[...] = dot_nt(adv, ghid)[:channels]
    out_ref[...] = dot_nt(lam, hidden.astype(BF))
    adv = adv_all_ref[:, adv_all_ref.shape[1] - wide :]
    adv_one_ref[...] = adv
    hidden, slope = gates(dot(w_in_ref[...], adv))
    hidden_ref[...] = hidden.astype(BF)
    slope_ref[...] = slope.astype(BF)


def third_kernel(count, stencil, slots, slots_ref, sends_ref, recv_ref, cubic_ref, w_in_t_ref, w_out_t_ref, slope_ref,
                 send_ref, lam_ref, ghid_ref, total_ref, terms_ref, sem):
    collect(sends_ref, 1, slots, lambda q: recv_ref[q], total_ref)
    lam = side_by_side(total_ref).astype(BF)
    lam_ref[...] = lam
    ghid = (slope_ref[...].astype(F32) * dot(w_out_t_ref[...], lam)).astype(BF)
    ghid_ref[...] = ghid
    ladv = lam.astype(F32) + dot(w_in_t_ref[...], ghid)
    send_terms(ladv, count, stencil, 0, slots_ref, cubic_ref, terms_ref, lambda q: send_ref.at[q], sem)
    pltpu.make_async_copy(terms_ref, terms_ref, sem).wait()


def grad_pair_kernel(side_ref, lam_ref, hidden_ref, ghid_ref, adv_ref, in_ref, out_ref, keep_ref, give_ref):
    grad_in = dot_nt(adv_ref[...], ghid_ref[...])
    grad_in = (in_ref[...] + grad_in[: in_ref.shape[0]]).astype(BF)
    grad_out = (out_ref[...] + dot_nt(lam_ref[...], hidden_ref[...])).astype(BF)

    @pl.when(side_ref[0] == 0)
    def _():
        keep_ref[...] = grad_in
        give_ref[...] = grad_out

    @pl.when(side_ref[0] != 0)
    def _():
        keep_ref[...] = grad_out
        give_ref[...] = grad_in


def last_kernel(slots, sends_ref, recv_ref, back_ref):
    collect(sends_ref, 0, slots, lambda q: recv_ref[q], back_ref)


def shards(state, tangent, cotangent, cubic, w_in, w_out, slots, sends):
    count, channels, columns = state.shape
    stencil = cubic.shape[0]
    hid = w_in.shape[0]
    peers = lax.axis_size("lat")
    slot_count = peers * sends.shape[-1]
    wide = count * columns
    block = (channels, columns)
    blocks = (count, *block)
    side = lax.axis_index("lat") % 2
    sends = jnp.transpose(sends, (0, 1, 3, 2))
    cubic = cubic.reshape(stencil * columns, columns)
    w_in_t = w_in.T
    mix = 2 * wide * channels * stencil * columns
    net = 2 * wide * channels * hid
    sizes = (count, stencil, slot_count)
    sem = pltpu.SemaphoreType.DMA

    def exchange(packed):
        return lax.all_to_all(packed, "lat", split_axis=0, concat_axis=0, tiled=True)

    def swap(values, step):
        return lax.ppermute(values, "lat", [(i, i ^ step) for i in range(peers)])

    def add(a, b):
        return (a.astype(F32) + b.astype(F32)).astype(BF)

    def widen(held, step):
        other = swap(held, step)
        if step == 1:
            return jnp.concatenate([held, other], axis=0)
        return jnp.stack([held, other], axis=1).reshape(-1, *held.shape[1:])

    tie = lax.optimization_barrier

    def load(kernel, arrays, out_shape, scratch):
        return pl.pallas_call(
            kernel,
            out_shape=out_shape,
            in_specs=[pl.BlockSpec(memory_space=HBM)] * len(arrays),
            out_specs=tuple(pl.BlockSpec(memory_space=place) for place in (VMEM, SMEM, SMEM)[: len(out_shape)]),
            scratch_shapes=scratch,
        )(*(pltpu.with_memory_space_constraint(a, HBM) for a in arrays))

    tall = -(-(channels + 4 + count) // 16) * 16
    rest = tall - channels
    (own,) = load(
        own_kernel, (slots, sends, state), (VMEM((count, tall, columns), BF),),
        [VMEM(slots.shape, slots.dtype), VMEM(sends.shape, sends.dtype), VMEM(blocks, BF), VMEM((rest, columns), F32), sem((3,))],
    )
    steps = []
    while 2 ** len(steps) < peers:
        steps.insert(0, 2 ** len(steps))
    states = widen(own[None], steps[0])
    own, slots, sends = load(
        own_tangent_kernel, (slots, sends, tangent),
        (VMEM((count, tall, columns), BF), SMEM(slots.shape, slots.dtype), SMEM(sends.shape, sends.dtype)),
        [VMEM(blocks, BF), sem((3,))],
    )
    w_in, w_out_pad, w_out_t, cubic, lam_two = call(
        prepare_kernel,
        [shape((hid, tall)), shape((tall, hid)), shape((hid, channels)),
         Placed(VMEM, cubic.shape), Placed(VMEM, (channels, wide))],
        [], [w_in_t, w_out, cubic, cotangent], 0,
    )
    tangents = widen(own[None], steps[0])
    states = widen(states, steps[1])
    for i in range(2, len(steps)):
        if i < len(steps) - 1:
            states, tangents = tie((states, tangents))
        else:
            states, tangents, w_in, cubic, lam_two = tie((states, tangents, w_in, cubic, lam_two))
        states = widen(states, steps[i])
        if i < len(steps) - 1:
            tangents = widen(tangents, steps[i - 1])
    states, tangents = tie((states, tangents))
    tangents = widen(tangents, steps[-2])
    states = states.reshape(-1, tall, columns)
    everyone = (stencil + 1) * count
    send, adv_all, adv_two, route = call(
        functools.partial(forward_kernel, peers, count, stencil),
        [Placed(HBM, (slot_count, *block)), shape((tall, everyone * columns)), shape((tall, wide)),
         Placed(SMEM, (everyone, stencil), jnp.int32)],
        [slots], [states, cubic, w_in, w_out_pad, w_in_t, w_out_t, lam_two], 7 * mix + 11 * net,
        [VMEM((peers, rest, columns), jnp.int32), SMEM((peers, rest, columns), jnp.int32),
         VMEM((count * stencil, *block), BF), sem, sem],
    )
    recv_three = exchange(send)
    _, tangents = tie((send, tangents))
    tangents = widen(tangents, 1).reshape(-1, tall, columns)
    part_in, part_out, adv_one, hidden_one, slope_one = call(
        between_kernel,
        [shape((channels, hid), F32)] * 2 + [shape((tall, wide))] + [shape((hid, wide))] * 2,
        [], [lam_two, w_in, w_out_t, adv_two, adv_all], 5 * net,
    )
    (pert,) = call(
        functools.partial(tangent_kernel, count, stencil),
        [shape(blocks)], [route], [tangents, cubic, w_in, w_out_pad, adv_all, adv_two], 5 * mix + 15 * net,
    )
    recv_three, pert = tie((recv_three, pert))
    send, lam_one, ghid_one = call(
        functools.partial(third_kernel, *sizes),
        [Placed(HBM, (slot_count, *block)), shape((channels, wide)), shape((hid, wide))],
        [slots, sends], [recv_three, cubic, w_in_t, w_out_t, slope_one], mix + 2 * net,
        [VMEM(blocks, F32), VMEM((count * stencil, *block), BF), sem],
    )
    recv_four = exchange(send)
    mine, give = call(
        grad_pair_kernel,
        [shape((channels, hid))] * 2, [side.astype(jnp.int32).reshape(1)],
        [lam_one, hidden_one, ghid_one, adv_one, part_in, part_out], 2 * net,
    )
    mine = add(mine, swap(give, 1))
    step = 2
    while step < peers:
        if 2 * step < peers:
            near, far, both = swap(mine, step), swap(mine, 2 * step), swap(mine, 3 * step)
            mine = ((mine.astype(F32) + near.astype(F32)) + (far.astype(F32) + both.astype(F32))).astype(BF)
            step *= 4
        else:
            mine, recv_four, pert = tie((mine, recv_four, pert))
            mine = add(mine, swap(mine, step))
            step *= 2
    (back,) = call(functools.partial(last_kernel, slot_count), [shape(blocks, F32)], [sends], [recv_four], net)
    other = swap(mine, 1)
    grad_in = jnp.where(side == 0, mine, other).astype(F32).T
    grad_out = jnp.where(side == 0, other, mine).astype(F32)
    return (pert, back, grad_in, grad_out)


def solution(mesh):
    in_specs = (
        P(("grp", "lat"), None, None),
        P(("grp", "lat"), None, None),
        P(("grp", "lat"), None, None),
        P(),
        P(),
        P(),
        P("grp", "lat", None),
        P("grp", "lat", None, None),
    )
    out_specs = (
        P(("grp", "lat"), None, None),
        P(("grp", "lat"), None, None),
        P("grp", None),
        P("grp", None),
    )
    return jax.shard_map(shards, mesh=mesh, in_specs=in_specs, out_specs=out_specs, check_vma=False)
```

time: 86.4 us -> 80.9 us (0.936)
  waiting for transfers between devices: 47.5 us -> 33.6 us
  Pallas kernels: 11 us -> 15.6 us
  starting transfers between devices: 25.5 us -> 27.9 us
  other arithmetic: 0.82 us -> 2.37 us
    all_to_all x4 -> x2, waiting for transfers between devices: 34.3 us -> 4.48 us  [exchange(): lax.all_to_all(packed, 'lat', split_axis=0, concat_axis=0, tiled=True)]
    ppermute x5 -> x14, waiting for transfers between devices: 13.2 us -> 29.1 us  [swap(): return lax.ppermute(values, 'lat', [(i, i ^ step) for i in range(peers)])]
    ppermute x5 -> x14, starting transfers between devices: 6.45 us -> 18.1 us  [swap(): return lax.ppermute(values, 'lat', [(i, i ^ step) for i in range(peers)])]
    all_to_all x4 -> x2, starting transfers between devices: 19.1 us -> 9.78 us  [exchange(): lax.all_to_all(packed, 'lat', split_axis=0, concat_axis=0, tiled=True)]
    pallas_call x8 -> x7, Pallas kernels: 9.2 us -> 13.6 us  [call(): pl.pallas_call(kernel, out_shape=tuple((o.memory_space(o.shape, o.dtype)...]
    concatenate x0 -> x2, other arithmetic: none -> 1.32 us  [widen(): return jnp.concatenate([held, other], axis=0)]
    pallas_call x1 -> x2, Pallas kernels: 1.76 us -> 1.94 us  [load(): pl.pallas_call(kernel, out_shape=out_shape, in_specs=[pl.BlockSpec(memory...]
  transfers between devices with their start and end apart: 9 -> 16, of which waited for: 6 -> 12; matrix products, arithmetic and copies ran while one was open for 0% -> 2% of each run, Pallas kernels for 5% -> 16%
where the time goes in v3:
time: 80.9 us; the launch traced here: 80.5 us
  waiting for transfers between devices  33.6 us (42%)
  starting transfers between devices  27.9 us (34%)
  Pallas kernels  15.6 us (19%)
  other arithmetic  2.37 us (3%)
  between operations  0.89 us (1%)
    ppermute x14, waiting for transfers between devices, swap(): return lax.ppermute(values, 'lat', [(i, i ^ step) for i in range(peers)])  29.1 us
    ppermute x14, starting transfers between devices, swap(): return lax.ppermute(values, 'lat', [(i, i ^ step) for i in range(peers)])  18.1 us
    pallas_call x7, Pallas kernels, call(): pl.pallas_call(kernel, out_shape=tuple((o.memory_space(o.shape, o.dtype)...  13.6 us
    all_to_all x2, starting transfers between devices, exchange(): lax.all_to_all(packed, 'lat', split_axis=0, concat_axis=0, tiled=True)  9.78 us
    all_to_all x2, waiting for transfers between devices, exchange(): lax.all_to_all(packed, 'lat', split_axis=0, concat_axis=0, tiled=True)  4.48 us
    pallas_call x2, Pallas kernels, load(): pl.pallas_call(kernel, out_shape=out_shape, in_specs=[pl.BlockSpec(memory...  1.94 us
  transfers between devices with their start and end apart: 16, of which 12 were waited for; matrix products, arithmetic and copies ran while one was open for 2% of the time, Pallas kernels for 16%

profile of v3, /device:TPU:0, one launch (start us, length us, event | category | flops | bytes accessed | tf_op | source)
XLA Modules:
  0.0 80.5 jit_solution(5581253801763653201)
XLA Ops:
  0.7 1.0 %shard_map.112 = bf16[4,80,128]{2,1,0:T(8,128)(2,1)S(1)} custom-call(s32[2,4,4]{2,1,0:T(4,128)} %slots_in_ref.3, s32[2,1,1,16]{3,2,1,0:T(1,128)} %bitcast.58, bf16[4,72,128]{2,1,0:T(8,128)(2,1)} %state_in_ref.1), custom_call_target="tpu_custom_call" | custom-call | tf_op jit(solution)/shard_map/pallas_call | solution.py:310
  1.7 4.1 %collective-permute-start = (bf16[1,4,80,128]{3,2,1,0:T(8,128)(2,1)S(1)}, bf16[1,4,80,128]{3,2,1,0:T(8,128)(2,1)S(1)}, u32[]{:S(2)}, u32[]{:S(2)}) collective-permute-start(bf16[1,4,80,128]{3,2,1,0:T(8,128)(2,1)S(1)} %bitcast.35), channel_id=1, source_target_pairs={{0,8},{1,9},{2,10},{3,11},{4,12},{5,13},{6,14},{7,15},{8,0},{9,1},... | collective-permute-start | bytes 245768 | tf_op jit(solution)/shard_map/ppermute | solution.py:296
  5.8 0.9 %shard_map.111 = (bf16[4,80,128]{2,1,0:T(8,128)(2,1)S(1)}, s32[2,4,4]{2,1,0:T(4,128)S(4)}, s32[2,1,1,16]{3,2,1,0:T(1,128)S(4)}) custom-call(s32[2,4,4]{2,1,0:T(4,128)} %slots_in_ref.3, s32[2,1,1,16]{3,2,1,0:T(1,128)} %bitcast.59, bf16[4,72,128]{2,1,0:T(8,128)(2,1)} %tangent_in_ref.1), custom_call_target="tpu_custom_call" | custom-call | tf_op jit(solution)/shard_map/pallas_call | solution.py:310
  6.7 0.1 collective-permute-start.2
  6.8 3.3 %collective-permute-done = bf16[1,4,80,128]{3,2,1,0:T(8,128)(2,1)S(1)} collective-permute-done((bf16[1,4,80,128]{3,2,1,0:T(8,128)(2,1)S(1)}, bf16[1,4,80,128]{3,2,1,0:T(8,128)(2,1)S(1)}, u32[]{:S(2)}, u32[]{:S(2)}) %collective-permute-start) | collective-permute-done | bytes 81952 | tf_op jit(solution)/shard_map/ppermute | solution.py:296
  10.1 2.6 %collective-permute-start.1 = (bf16[2,4,80,128]{3,2,1,0:T(8,128)(2,1)S(1)}, bf16[2,4,80,128]{3,2,1,0:T(8,128)(2,1)S(1)}, u32[]{:S(2)}, u32[]{:S(2)}) collective-permute-start(bf16[2,4,80,128]{3,2,1,0:T(8,128)(2,1)S(1)} %get-tuple-element.79), channel_id=1, source_target_pairs={{0,4},{1,5},{2,6},{3,7},{4,0},{5,1},{6,2},{7,3},{8,12},{9,13},{10,... | collective-permute-start | bytes 491528 | tf_op jit(solution)/shard_map/ppermute | solution.py:296
  12.7 0.8 %collective-permute-done.2 = bf16[1,4,80,128]{3,2,1,0:T(8,128)(2,1)S(1)} collective-permute-done((bf16[1,4,80,128]{3,2,1,0:T(8,128)(2,1)S(1)}, bf16[1,4,80,128]{3,2,1,0:T(8,128)(2,1)S(1)}, u32[]{:S(2)}, u32[]{:S(2)}) %collective-permute-start.2) | collective-permute-done | bytes 81952 | tf_op jit(solution)/shard_map/ppermute | solution.py:296
  13.5 3.5 %collective-permute-done.1 = bf16[2,4,80,128]{3,2,1,0:T(8,128)(2,1)S(1)} collective-permute-done((bf16[2,4,80,128]{3,2,1,0:T(8,128)(2,1)S(1)}, bf16[2,4,80,128]{3,2,1,0:T(8,128)(2,1)S(1)}, u32[]{:S(2)}, u32[]{:S(2)}) %collective-permute-start.1) | collective-permute-done | bytes 163872 | tf_op jit(solution)/shard_map/ppermute | solution.py:296
  17.1 1.7 %collective-permute-start.3 = (bf16[4,4,80,128]{3,2,1,0:T(8,128)(2,1)S(1)}, bf16[4,4,80,128]{3,2,1,0:T(8,128)(2,1)S(1)}, u32[]{:S(2)}, u32[]{:S(2)}) collective-permute-start(bf16[4,4,80,128]{3,2,1,0:T(8,128)(2,1)S(1)} %bitcast.49), channel_id=1, source_target_pairs={{0,2},{1,3},{2,0},{3,1},{4,6},{5,7},{6,4},{7,5},{8,10},{9,11},{10,... | collective-permute-start | bytes 983048 | tf_op jit(solution)/shard_map/ppermute | solution.py:296
  18.8 1.4 %collective-permute-start.4 = (bf16[2,4,80,128]{3,2,1,0:T(8,128)(2,1)S(1)}, bf16[2,4,80,128]{3,2,1,0:T(8,128)(2,1)S(1)}, u32[]{:S(2)}, u32[]{:S(2)}) collective-permute-start(bf16[2,4,80,128]{3,2,1,0:T(8,128)(2,1)S(1)} %maximum_bitcast_fusion), channel_id=1, source_target_pairs={{0,4},{1,5},{2,6},{3,7},{4,0},{5,1},{6,2},{7,3},{8,12},{9,13},{10,... | collective-permute-start | bytes 491528 | tf_op jit(solution)/shard_map/ppermute | solution.py:296
  20.2 0.0 copy-done.2
  20.2 0.0 copy-done.3
  20.3 0.1 shard_map.113
  20.4 3.8 %collective-permute-done.4 = bf16[2,4,80,128]{3,2,1,0:T(8,128)(2,1)S(1)} collective-permute-done((bf16[2,4,80,128]{3,2,1,0:T(8,128)(2,1)S(1)}, bf16[2,4,80,128]{3,2,1,0:T(8,128)(2,1)S(1)}, u32[]{:S(2)}, u32[]{:S(2)}) %collective-permute-start.4) | collective-permute-done | bytes 163872 | tf_op jit(solution)/shard_map/ppermute | solution.py:296
  24.3 2.0 %collective-permute-done.3 = bf16[4,4,80,128]{3,2,1,0:T(8,128)(2,1)S(1)} collective-permute-done((bf16[4,4,80,128]{3,2,1,0:T(8,128)(2,1)S(1)}, bf16[4,4,80,128]{3,2,1,0:T(8,128)(2,1)S(1)}, u32[]{:S(2)}, u32[]{:S(2)}) %collective-permute-start.3) | collective-permute-done | bytes 327712 | tf_op jit(solution)/shard_map/ppermute | solution.py:296
  26.2 0.1 pad_maximum_fusion.2
  26.4 0.1 collective-permute-start.5
  26.4 2.1 %collective-permute-done.5 = bf16[8,4,80,128]{3,2,1,0:T(8,128)(2,1)S(1)} collective-permute-done((bf16[8,4,80,128]{3,2,1,0:T(8,128)(2,1)S(1)}, bf16[8,4,80,128]{3,2,1,0:T(8,128)(2,1)S(1)}, u32[]{:S(2)}, u32[]{:S(2)}) %collective-permute-start.5) | collective-permute-done | bytes 655392 | tf_op jit(solution)/shard_map/ppermute | solution.py:296
  28.5 0.1 pad_maximum_fusion
  28.6 1.8 %collective-permute-start.6 = (bf16[4,4,80,128]{3,2,1,0:T(8,128)(2,1)S(1)}, bf16[4,4,80,128]{3,2,1,0:T(8,128)(2,1)S(1)}, u32[]{:S(2)}, u32[]{:S(2)}) collective-permute-start(bf16[4,4,80,128]{3,2,1,0:T(8,128)(2,1)S(1)} %bitcast.47), channel_id=1, source_target_pairs={{0,2},{1,3},{2,0},{3,1},{4,6},{5,7},{6,4},{7,5},{8,10},{9,11},{10,... | collective-permute-start | bytes 983048 | tf_op jit(solution)/shard_map/ppermute | solution.py:296
  30.5 5.9 %shard_map.114 = (bf16[16,72,128]{2,1,0:T(8,128)(2,1)}, bf16[80,2560]{1,0:T(8,128)(2,1)S(1)}, bf16[80,512]{1,0:T(8,128)(2,1)S(1)}, s32[20,4]{1,0:T(8,128)S(4)}) custom-call(s32[2,4,4]{2,1,0:T(4,128)S(4)} %get-tuple-element.41.slots_ref, bf16[64,80,128]{2,1,0:T(8,128)(2,1)S(1)} %bitcast.33, bf16[512,128]{1,0:T(8,128)(2,1)S(1)} %get-tuple-element.52.cubic_ref, ...), custom_call_target="tpu_custom_call" | custom-call | flops 679477248 | bytes 2613568 | tf_op jit(solution)/shard_map/pallas_call | solution.py:32
  36.3 2.1 %collective-permute-done.6 = bf16[4,4,80,128]{3,2,1,0:T(8,128)(2,1)S(1)} collective-permute-done((bf16[4,4,80,128]{3,2,1,0:T(8,128)(2,1)S(1)}, bf16[4,4,80,128]{3,2,1,0:T(8,128)(2,1)S(1)}, u32[]{:S(2)}, u32[]{:S(2)}) %collective-permute-start.6) | collective-permute-done | bytes 327712 | tf_op jit(solution)/shard_map/ppermute | solution.py:296
  38.5 0.1 pad_maximum_fusion.3
  38.6 0.1 collective-permute-start.7
  38.7 6.2 %all-to-all-start = ((bf16[16,72,128]{2,1,0:T(8,128)(2,1)}), bf16[16,72,128]{2,1,0:T(8,128)(2,1)S(1)}, u32[]{:S(2)}, u32[]{:S(2)}) async-start(bf16[16,72,128]{2,1,0:T(8,128)(2,1)} %get-tuple-element.57), calls=%async_computation | async-start | bytes 589824 | tf_op jit(solution)/shard_map/all_to_all | solution.py:293
  44.9 1.2 %shard_map.116 = (f32[72,512]{1,0:T(8,128)S(1)}, f32[72,512]{1,0:T(8,128)S(1)}, bf16[80,512]{1,0:T(8,128)(2,1)S(1)}, bf16[512,512]{1,0:T(8,128)(2,1)S(1)}, bf16[512,512]{1,0:T(8,128)(2,1)S(1)}) custom-call(bf16[72,512]{1,0:T(8,128)(2,1)S(1)} %get-tuple-element.56.lam_two_ref, bf16[512,80]{1,0:T(8,128)(2,1)S(1)} %get-tuple-element.53.w_in_ref, ...), custom_call_target="tpu_custom_call" | custom-call | flops 188743680 | bytes 2146304 | tf_op jit(solution)/shard_map/pallas_call | solution.py:32
  46.1 0.0 collective-permute-done.7
  46.1 1.2 %pad_maximum_fusion.1 = bf16[16,4,80,128]{3,2,1,0:T(8,128)(2,1)S(1)} fusion(bf16[8,4,80,128]{3,2,1,0:T(8,128)(2,1)} %collective-permute-done.7, bf16[8,4,80,128]{3,2,1,0:T(8,128)(2,1)S(1)} %bitcast.44), kind=kLoop, calls=%fused_computation.1 | loop fusion | flops 655360 | bytes 2621440 | tf_op jit(solution)/shard_map/concatenate | solution.py:304
  47.3 3.7 %shard_map.115 = bf16[4,72,128]{2,1,0:T(8,128)(2,1)} custom-call(s32[20,4]{1,0:T(8,128)S(4)} %get-tuple-element.58.route_ref, bf16[64,80,128]{2,1,0:T(8,128)(2,1)S(1)} %bitcast.34, bf16[512,128]{1,0:T(8,128)(2,1)S(1)} %get-tuple-element.52.cubic_ref, bf16[512,80]{1,0:T(8,128)(2,1)S(1)} %get-tuple-element.53.w_in_ref, ...), custom_call_target="tpu_custom_call" | custom-call | flops 754974720 | bytes 2170880 | tf_op jit(solution)/shard_map/pallas_call | solution.py:32
  51.0 4.4 %all-to-all-done.recv_ref = bf16[16,72,128]{2,1,0:T(8,128)(2,1)S(1)} async-done(((bf16[16,72,128]{2,1,0:T(8,128)(2,1)}), bf16[16,72,128]{2,1,0:T(8,128)(2,1)S(1)}, u32[]{:S(2)}, u32[]{:S(2)}) %all-to-all-start) | async-done | bytes 294944 | tf_op jit(solution)/shard_map/all_to_all | solution.py:293
  55.5 1.4 %shard_map.117 = (bf16[16,72,128]{2,1,0:T(8,128)(2,1)}, bf16[72,512]{1,0:T(8,128)(2,1)S(1)}, bf16[512,512]{1,0:T(8,128)(2,1)S(1)}) custom-call(s32[2,4,4]{2,1,0:T(4,128)S(4)} %get-tuple-element.41.slots_ref, s32[2,1,1,16]{3,2,1,0:T(1,128)S(4)} %get-tuple-element.42.sends_ref, bf16[16,72,128]{2,1,0:T(8,128)(2,1)S(1)} %all-to-all-done.recv_ref, ...), custom_call_target="tpu_custom_call" | custom-call | flops 113246208 | bytes 1990656 | tf_op jit(solution)/shard_map/pallas_call | solution.py:32
  56.9 0.5 shard_map.118
  57.4 0.1 collective-permute-start.8
  57.5 3.5 %all-to-all-start.1 = ((bf16[16,72,128]{2,1,0:T(8,128)(2,1)}), bf16[16,72,128]{2,1,0:T(8,128)(2,1)S(1)}, u32[]{:S(2)}, u32[]{:S(2)}) async-start(bf16[16,72,128]{2,1,0:T(8,128)(2,1)} %get-tuple-element.73), calls=%async_computation.1 | async-start | bytes 589824 | tf_op jit(solution)/shard_map/all_to_all | solution.py:293
  61.0 0.0 collective-permute-done.8
  61.1 2.8 %collective-permute-start.11 = (bf16[72,512]{1,0:T(8,128)(2,1)S(1)}, bf16[72,512]{1,0:T(8,128)(2,1)S(1)}, u32[]{:S(2)}, u32[]{:S(2)}) collective-permute-start(bf16[72,512]{1,0:T(8,128)(2,1)S(1)} %add_convert_fusion.2), channel_id=1, source_target_pairs={{0,6},{1,7},{2,4},{3,5},{4,2},{5,3},{6,0},{7,1},{8,14},{9,15},{10,... | collective-permute-start | bytes 221192 | tf_op jit(solution)/shard_map/ppermute | solution.py:296
  63.9 0.5 collective-permute-start.10
  64.4 0.2 collective-permute-start.9
  64.6 6.8 %collective-permute-done.11 = bf16[72,512]{1,0:T(8,128)(2,1)S(1)} collective-permute-done((bf16[72,512]{1,0:T(8,128)(2,1)S(1)}, bf16[72,512]{1,0:T(8,128)(2,1)S(1)}, u32[]{:S(2)}, u32[]{:S(2)}) %collective-permute-start.11) | collective-permute-done | bytes 73760 | tf_op jit(solution)/shard_map/ppermute | solution.py:296
  71.4 0.5 collective-permute-done.10
  72.0 0.0 collective-permute-done.9
  72.0 0.0 all-to-all-done.1.recv_ref
  72.0 2.5 %collective-permute-start.12 = (bf16[72,512]{1,0:T(8,128)(2,1)S(1)}, bf16[72,512]{1,0:T(8,128)(2,1)S(1)}, u32[]{:S(2)}, u32[]{:S(2)}) collective-permute-start(bf16[72,512]{1,0:T(8,128)(2,1)S(1)} %add_convert_fusion.1), channel_id=1, source_target_pairs={{0,8},{1,9},{2,10},{3,11},{4,12},{5,13},{6,14},{7,15},{8,0},{9,1},... | collective-permute-start | bytes 221192 | tf_op jit(solution)/shard_map/ppermute | solution.py:296
  74.5 3.8 %collective-permute-done.12 = bf16[72,512]{1,0:T(8,128)(2,1)S(1)} collective-permute-done((bf16[72,512]{1,0:T(8,128)(2,1)S(1)}, bf16[72,512]{1,0:T(8,128)(2,1)S(1)}, u32[]{:S(2)}, u32[]{:S(2)}) %collective-permute-start.12) | collective-permute-done | bytes 73760 | tf_op jit(solution)/shard_map/ppermute | solution.py:296
  78.4 0.1 collective-permute-start.13
  78.5 0.8 %shard_map.119 = f32[4,72,128]{2,1,0:T(8,128)} custom-call(s32[2,1,1,16]{3,2,1,0:T(1,128)S(4)} %get-tuple-element.42.sends_ref, bf16[16,72,128]{2,1,0:T(8,128)(2,1)S(1)} %all-to-all-done.1.recv_ref), custom_call_target="tpu_custom_call" | custom-call | flops 37748736 | bytes 442368 | tf_op jit(solution)/shard_map/pallas_call | solution.py:32
  79.3 0.4 collective-permute-done.13
  79.7 0.7 select_convert_fusion
  (17 shorter events, 0.3 us)
Async XLA Ops:
  0.6 19.6 %copy-start = (bf16[512,72]{0,1:T(8,128)(2,1)S(1)}, bf16[512,72]{0,1:T(8,128)(2,1)}, u32[]{:S(2)}) copy-start(bf16[512,72]{0,1:T(8,128)(2,1)} %param.12) | copy-start | bytes 221188
  0.6 19.6 %copy-start.2 = (bf16[72,512]{1,0:T(8,128)(2,1)S(1)}, bf16[72,512]{1,0:T(8,128)(2,1)}, u32[]{:S(2)}) copy-start(bf16[72,512]{1,0:T(8,128)(2,1)} %w_out_ref.1) | copy-start | bytes 221188
  0.7 19.6 %copy-start.1 = (bf16[4,128,128]{2,1,0:T(8,128)(2,1)S(1)}, bf16[4,128,128]{2,1,0:T(8,128)(2,1)}, u32[]{:S(2)}) copy-start(bf16[4,128,128]{2,1,0:T(8,128)(2,1)} %param.11) | copy-start | bytes 393220
  0.7 19.6 %copy-start.3 = (bf16[4,72,128]{2,1,0:T(8,128)(2,1)S(1)}, bf16[4,72,128]{2,1,0:T(8,128)(2,1)}, u32[]{:S(2)}) copy-start(bf16[4,72,128]{2,1,0:T(8,128)(2,1)} %cot_ref.1) | copy-start | bytes 221188
  1.7 8.4 %collective-permute-start = (bf16[1,4,80,128]{3,2,1,0:T(8,128)(2,1)S(1)}, bf16[1,4,80,128]{3,2,1,0:T(8,128)(2,1)S(1)}, u32[]{:S(2)}, u32[]{:S(2)}) collective-permute-start(bf16[1,4,80,128]{3,2,1,0:T(8,128)(2,1)S(1)} %bitcast.35), channel_id=1, source_target_pairs={{0,8},{1,9},{2,10},{3,11},{4,12},{5,13},{6,14},{7,15},{8,0},{9,1},... | collective-permute-start | bytes 245768 | tf_op jit(solution)/shard_map/ppermute | solution.py:296
  6.7 6.8 %collective-permute-start.2 = (bf16[1,4,80,128]{3,2,1,0:T(8,128)(2,1)S(1)}, bf16[1,4,80,128]{3,2,1,0:T(8,128)(2,1)S(1)}, u32[]{:S(2)}, u32[]{:S(2)}) collective-permute-start(bf16[1,4,80,128]{3,2,1,0:T(8,128)(2,1)S(1)} %bitcast.41), channel_id=1, source_target_pairs={{0,8},{1,9},{2,10},{3,11},{4,12},{5,13},{6,14},{7,15},{8,0},{9,1},... | collective-permute-start | bytes 245768 | tf_op jit(solution)/shard_map/ppermute | solution.py:296
  10.1 6.9 %collective-permute-start.1 = (bf16[2,4,80,128]{3,2,1,0:T(8,128)(2,1)S(1)}, bf16[2,4,80,128]{3,2,1,0:T(8,128)(2,1)S(1)}, u32[]{:S(2)}, u32[]{:S(2)}) collective-permute-start(bf16[2,4,80,128]{3,2,1,0:T(8,128)(2,1)S(1)} %get-tuple-element.79), channel_id=1, source_target_pairs={{0,4},{1,5},{2,6},{3,7},{4,0},{5,1},{6,2},{7,3},{8,12},{9,13},{10,... | collective-permute-start | bytes 491528 | tf_op jit(solution)/shard_map/ppermute | solution.py:296
  17.1 9.2 %collective-permute-start.3 = (bf16[4,4,80,128]{3,2,1,0:T(8,128)(2,1)S(1)}, bf16[4,4,80,128]{3,2,1,0:T(8,128)(2,1)S(1)}, u32[]{:S(2)}, u32[]{:S(2)}) collective-permute-start(bf16[4,4,80,128]{3,2,1,0:T(8,128)(2,1)S(1)} %bitcast.49), channel_id=1, source_target_pairs={{0,2},{1,3},{2,0},{3,1},{4,6},{5,7},{6,4},{7,5},{8,10},{9,11},{10,... | collective-permute-start | bytes 983048 | tf_op jit(solution)/shard_map/ppermute | solution.py:296
  18.8 5.4 %collective-permute-start.4 = (bf16[2,4,80,128]{3,2,1,0:T(8,128)(2,1)S(1)}, bf16[2,4,80,128]{3,2,1,0:T(8,128)(2,1)S(1)}, u32[]{:S(2)}, u32[]{:S(2)}) collective-permute-start(bf16[2,4,80,128]{3,2,1,0:T(8,128)(2,1)S(1)} %maximum_bitcast_fusion), channel_id=1, source_target_pairs={{0,4},{1,5},{2,6},{3,7},{4,0},{5,1},{6,2},{7,3},{8,12},{9,13},{10,... | collective-permute-start | bytes 491528 | tf_op jit(solution)/shard_map/ppermute | solution.py:296
  26.4 2.2 %collective-permute-start.5 = (bf16[8,4,80,128]{3,2,1,0:T(8,128)(2,1)S(1)}, bf16[8,4,80,128]{3,2,1,0:T(8,128)(2,1)S(1)}, u32[]{:S(2)}, u32[]{:S(2)}) collective-permute-start(bf16[8,4,80,128]{3,2,1,0:T(8,128)(2,1)S(1)} %bitcast.45), channel_id=1, source_target_pairs={{0,1},{1,0},{2,3},{3,2},{4,5},{5,4},{6,7},{7,6},{8,9},{9,8},{10,11... | collective-permute-start | bytes 1966088 | tf_op jit(solution)/shard_map/ppermute | solution.py:296
  28.6 9.8 %collective-permute-start.6 = (bf16[4,4,80,128]{3,2,1,0:T(8,128)(2,1)S(1)}, bf16[4,4,80,128]{3,2,1,0:T(8,128)(2,1)S(1)}, u32[]{:S(2)}, u32[]{:S(2)}) collective-permute-start(bf16[4,4,80,128]{3,2,1,0:T(8,128)(2,1)S(1)} %bitcast.47), channel_id=1, source_target_pairs={{0,2},{1,3},{2,0},{3,1},{4,6},{5,7},{6,4},{7,5},{8,10},{9,11},{10,... | collective-permute-start | bytes 983048 | tf_op jit(solution)/shard_map/ppermute | solution.py:296
  38.6 7.5 %collective-permute-start.7 = (bf16[8,4,80,128]{3,2,1,0:T(8,128)(2,1)S(1)}, bf16[8,4,80,128]{3,2,1,0:T(8,128)(2,1)}, u32[]{:S(2)}, u32[]{:S(2)}) collective-permute-start(bf16[8,4,80,128]{3,2,1,0:T(8,128)(2,1)S(1)} %bitcast.43), channel_id=1, source_target_pairs={{0,1},{1,0},{2,3},{3,2},{4,5},{5,4},{6,7},{7,6},{8,9},{9,8},{10,11... | collective-permute-start | bytes 1966088 | tf_op jit(solution)/shard_map/ppermute | solution.py:296
  38.7 16.8 %all-to-all-start = ((bf16[16,72,128]{2,1,0:T(8,128)(2,1)}), bf16[16,72,128]{2,1,0:T(8,128)(2,1)S(1)}, u32[]{:S(2)}, u32[]{:S(2)}) async-start(bf16[16,72,128]{2,1,0:T(8,128)(2,1)} %get-tuple-element.57), calls=%async_computation | async-start | bytes 589824 | tf_op jit(solution)/shard_map/all_to_all | solution.py:293
  57.4 3.6 %collective-permute-start.8 = (bf16[72,512]{1,0:T(8,128)(2,1)S(1)}, bf16[72,512]{1,0:T(8,128)(2,1)S(1)}, u32[]{:S(2)}, u32[]{:S(2)}) collective-permute-start(bf16[72,512]{1,0:T(8,128)(2,1)S(1)} %get-tuple-element.72), channel_id=1, source_target_pairs={{0,1},{1,0},{2,3},{3,2},{4,5},{5,4},{6,7},{7,6},{8,9},{9,8},{10,11... | collective-permute-start | bytes 221192 | tf_op jit(solution)/shard_map/ppermute | solution.py:296
  57.5 14.6 %all-to-all-start.1 = ((bf16[16,72,128]{2,1,0:T(8,128)(2,1)}), bf16[16,72,128]{2,1,0:T(8,128)(2,1)S(1)}, u32[]{:S(2)}, u32[]{:S(2)}) async-start(bf16[16,72,128]{2,1,0:T(8,128)(2,1)} %get-tuple-element.73), calls=%async_computation.1 | async-start | bytes 589824 | tf_op jit(solution)/shard_map/all_to_all | solution.py:293
  61.1 10.4 %collective-permute-start.11 = (bf16[72,512]{1,0:T(8,128)(2,1)S(1)}, bf16[72,512]{1,0:T(8,128)(2,1)S(1)}, u32[]{:S(2)}, u32[]{:S(2)}) collective-permute-start(bf16[72,512]{1,0:T(8,128)(2,1)S(1)} %add_convert_fusion.2), channel_id=1, source_target_pairs={{0,6},{1,7},{2,4},{3,5},{4,2},{5,3},{6,0},{7,1},{8,14},{9,15},{10,... | collective-permute-start | bytes 221192 | tf_op jit(solution)/shard_map/ppermute | solution.py:296
  63.9 8.1 %collective-permute-start.10 = (bf16[72,512]{1,0:T(8,128)(2,1)S(1)}, bf16[72,512]{1,0:T(8,128)(2,1)S(1)}, u32[]{:S(2)}, u32[]{:S(2)}) collective-permute-start(bf16[72,512]{1,0:T(8,128)(2,1)S(1)} %add_convert_fusion.2), channel_id=1, source_target_pairs={{0,4},{1,5},{2,6},{3,7},{4,0},{5,1},{6,2},{7,3},{8,12},{9,13},{10,... | collective-permute-start | bytes 221192 | tf_op jit(solution)/shard_map/ppermute | solution.py:296
  64.4 7.6 %collective-permute-start.9 = (bf16[72,512]{1,0:T(8,128)(2,1)S(1)}, bf16[72,512]{1,0:T(8,128)(2,1)S(1)}, u32[]{:S(2)}, u32[]{:S(2)}) collective-permute-start(bf16[72,512]{1,0:T(8,128)(2,1)S(1)} %add_convert_fusion.2), channel_id=1, source_target_pairs={{0,2},{1,3},{2,0},{3,1},{4,6},{5,7},{6,4},{7,5},{8,10},{9,11},{10,... | collective-permute-start | bytes 221192 | tf_op jit(solution)/shard_map/ppermute | solution.py:296
  72.0 6.3 %collective-permute-start.12 = (bf16[72,512]{1,0:T(8,128)(2,1)S(1)}, bf16[72,512]{1,0:T(8,128)(2,1)S(1)}, u32[]{:S(2)}, u32[]{:S(2)}) collective-permute-start(bf16[72,512]{1,0:T(8,128)(2,1)S(1)} %add_convert_fusion.1), channel_id=1, source_target_pairs={{0,8},{1,9},{2,10},{3,11},{4,12},{5,13},{6,14},{7,15},{8,0},{9,1},... | collective-permute-start | bytes 221192 | tf_op jit(solution)/shard_map/ppermute | solution.py:296
  78.4 1.3 %collective-permute-start.13 = (bf16[72,512]{1,0:T(8,128)(2,1)S(1)}, bf16[72,512]{1,0:T(8,128)(2,1)S(1)}, u32[]{:S(2)}, u32[]{:S(2)}) collective-permute-start(bf16[72,512]{1,0:T(8,128)(2,1)S(1)} %add_convert_fusion), channel_id=1, source_target_pairs={{0,1},{1,0},{2,3},{3,2},{4,5},{5,4},{6,7},{7,6},{8,9},{9,8},{10,11... | collective-permute-start | bytes 221192 | tf_op jit(solution)/shard_map/ppermute | solution.py:296

commit v4 on v3

--- a/solution.py
+++ b/solution.py
@@ -11,6 +11,7 @@
 F32 = jnp.float32
 VMEM = pltpu.VMEM
 HBM = pltpu.HBM
+LANES = 128
 
 
 def shape(dims, dtype=BF):
@@ -108,6 +109,8 @@
 
 def padded(block, rows):
     block = block.astype(F32)
+    if rows == block.shape[0]:
+        return block
     return jnp.concatenate([block, jnp.zeros((rows - block.shape[0], block.shape[1]), F32)], axis=0)
 
 
@@ -118,15 +121,26 @@
         load.start()
     for load in loads:
         load.wait()
-    count, channels, _ = state_ref.shape
+    count = state_ref.shape[0]
     rows = out_ref.shape[1]
+    notes = [jnp.zeros((1, LANES), F32) for _ in range(-(-(2 * sends_ref.shape[3] + slots_ref[0].size) // LANES))]
+    peers, reach = sends_ref.shape[3], slots_ref.shape[2]
+    numbers = [(section * peers, sends_ref[section, 0]) for section in range(sends_ref.shape[0])]
+    numbers += [(2 * peers + j * reach, slots_ref[0, j : j + 1]) for j in range(count)]
+    for start, row in numbers:
+        row = row.astype(F32)
+        if row.shape[1] < LANES:
+            row = jnp.concatenate([row, jnp.zeros((1, LANES - row.shape[1]), F32)], axis=1)
+        if start % LANES:
+            row = pltpu.roll(row, start % LANES, 1)
+        notes[start // LANES] += row
     note_ref[...] = jnp.zeros(note_ref.shape, F32)
-    for section in range(sends_ref.shape[0]):
-        note_ref[section : section + 1, : sends_ref.shape[3]] = sends_ref[section, 0].astype(F32)
-    note_ref[4 : 4 + count, : slots_ref.shape[2]] = slots_ref[0].astype(F32)
+    for i, row in enumerate(notes):
+        note_ref[i : i + 1] = row
     for j in range(1, count):
         out_ref[j] = padded(state_ref[j], rows).astype(BF)
-    out_ref[0] = jnp.concatenate([state_ref[0].astype(F32), note_ref[...]], axis=0).astype(BF)
+    top = padded(state_ref[0], rows - 8)
+    out_ref[0] = jnp.concatenate([top, note_ref[...]], axis=0).astype(BF)
 
 
 def own_tangent_kernel(slots_in_ref, sends_in_ref, tangent_in_ref, out_ref, slots_ref, sends_ref, tangent_ref, sems):
@@ -149,38 +163,48 @@
     w_out_t_ref[...] = w_out_ref[...].astype(F32).T.astype(BF)
 
 
-def routes(peers, count, stencil, slots_ref, blocks_ref, notes_ref, tables_ref, route_ref, sem):
+def routes(peers, count, stencil, slots_ref, blocks_ref, notes_ref, tables_ref, route_ref, sem, meanwhile):
     me = lax.axis_index("lat")
+    rows = notes_ref.shape[0] // peers
+    under = blocks_ref.shape[1] - 8
 
     def place(device):
         differs = device ^ me
-        return (differs & 1) * (peers // 2) + (differs >> 1)
+        return (differs & 1) * (peers // 2) + ((differs >> 1) & 3) * (peers // 8) + (differs >> 3)
 
     def read_note(r):
         block = blocks_ref[r * count].astype(F32)
-        notes_ref[r] = block[block.shape[0] - notes_ref.shape[1] :].astype(jnp.int32)
+        notes_ref[pl.ds(r * rows, rows)] = block[under : under + rows].astype(jnp.int32)
 
     repeat(peers, read_note)
-    pltpu.make_async_copy(notes_ref, tables_ref, sem).start()
-    pltpu.make_async_copy(notes_ref, tables_ref, sem).wait()
+    copy = pltpu.make_async_copy(notes_ref, tables_ref, sem)
+    copy.start()
+    meanwhile()
+    copy.wait()
+
+    def note(device, start, index):
+        return tables_ref[place(device) * rows + start // LANES, start % LANES + index]
 
     def fill(t, device, block):
         for k in range(stencil):
-            owner = tables_ref[place(device), 4 + block, k]
-            entry = jnp.maximum(tables_ref[place(owner), 0, device], 0)
+            owner = note(device, 2 * peers, block * stencil + k)
+            entry = jnp.maximum(note(owner, 0, device), 0)
             route_ref[t, k] = place(owner) * count + entry
 
     for k in range(stencil):
         for j in range(count):
             device = slots_ref[1, j, k]
-            fill(k * count + j, device, jnp.maximum(tables_ref[place(device), 1, me], 0))
+            fill(k * count + j, device, jnp.maximum(note(device, peers, me), 0))
     for j in range(count):
         fill(stencil * count + j, me, j)
 
 
 def forward_kernel(peers, count, stencil, slots_ref, blocks_ref, cubic_ref, w_in_ref, w_out_ref, w_in_t_ref, w_out_t_ref, lam_two_ref,
-                   send_ref, adv_one_ref, adv_ref, route_ref, notes_ref, tables_ref, terms_ref, sem, note_sem):
-    routes(peers, count, stencil, slots_ref, blocks_ref, notes_ref, tables_ref, route_ref, note_sem)
+                   send_ref, adv_one_ref, adv_ref, route_ref, notes_ref, tables_ref, terms_ref, pull_ref, sem, note_sem):
+    def pull():
+        pull_ref[...] = dot(w_out_t_ref[...], lam_two_ref[...])
+
+    routes(peers, count, stencil, slots_ref, blocks_ref, notes_ref, tables_ref, route_ref, note_sem, pull)
     everyone = (stencil + 1) * count
     adv = advect(lambda t, k: blocks_ref[route_ref[t, k]], everyone, stencil, cubic_ref)
     wide = adv.shape[1] // (stencil + 1)
@@ -195,7 +219,7 @@
     adv_ref[...] = adv
     lam = lam_two_ref[...]
     slope = gates(dot(w_in_ref[...], adv))[1]
-    ghid = (slope * dot(w_out_t_ref[...], lam)).astype(BF)
+    ghid = (slope * pull_ref[...]).astype(BF)
     ladv = lam.astype(F32) + dot(w_in_t_ref[...], ghid)
     send_terms(ladv, count, stencil, 1, slots_ref, cubic_ref, terms_ref, lambda q: send_ref.at[q], sem)
     pltpu.make_async_copy(terms_ref, terms_ref, sem).wait()
@@ -299,10 +323,11 @@
         return (a.astype(F32) + b.astype(F32)).astype(BF)
 
     def widen(held, step):
-        other = swap(held, step)
-        if step == 1:
-            return jnp.concatenate([held, other], axis=0)
-        return jnp.stack([held, other], axis=1).reshape(-1, *held.shape[1:])
+        return jnp.stack([held, swap(held, step)], axis=1).reshape(-1, *held.shape[1:])
+
+    def cross(near, far):
+        half = near.shape[0] // 2
+        return swap(far[:half], 2), swap(near[half:], 4)
 
     tie = lax.optimization_barrier
 
@@ -315,16 +340,20 @@
             scratch_shapes=scratch,
         )(*(pltpu.with_memory_space_constraint(a, HBM) for a in arrays))
 
-    tall = -(-(channels + 4 + count) // 16) * 16
-    rest = tall - channels
+    tall = -(-(channels + 8) // 16) * 16
+    note_rows = -(-(2 * peers + count * stencil) // LANES)
+    notes = (peers * note_rows, LANES)
     (own,) = load(
         own_kernel, (slots, sends, state), (VMEM((count, tall, columns), BF),),
-        [VMEM(slots.shape, slots.dtype), VMEM(sends.shape, sends.dtype), VMEM(blocks, BF), VMEM((rest, columns), F32), sem((3,))],
+        [VMEM(slots.shape, slots.dtype), VMEM(sends.shape, sends.dtype), VMEM(blocks, BF), VMEM((8, LANES), F32), sem((3,))],
     )
     steps = []
-    while 2 ** len(steps) < peers:
-        steps.insert(0, 2 ** len(steps))
-    states = widen(own[None], steps[0])
+    while 16 * 2 ** len(steps) <= peers:
+        steps.insert(0, 8 * 2 ** len(steps))
+    states = own[None]
+    for step in steps:
+        states = widen(states, step)
+    near, far = swap(states, 2), swap(states, 4)
     own, slots, sends = load(
         own_tangent_kernel, (slots, sends, tangent),
         (VMEM((count, tall, columns), BF), SMEM(slots.shape, slots.dtype), SMEM(sends.shape, sends.dtype)),
@@ -336,18 +365,16 @@
          Placed(VMEM, cubic.shape), Placed(VMEM, (channels, wide))],
         [], [w_in_t, w_out, cubic, cotangent], 0,
     )
-    tangents = widen(own[None], steps[0])
-    states = widen(states, steps[1])
-    for i in range(2, len(steps)):
-        if i < len(steps) - 1:
-            states, tangents = tie((states, tangents))
-        else:
-            states, tangents, w_in, cubic, lam_two = tie((states, tangents, w_in, cubic, lam_two))
-        states = widen(states, steps[i])
-        if i < len(steps) - 1:
-            tangents = widen(tangents, steps[i - 1])
-    states, tangents = tie((states, tangents))
-    tangents = widen(tangents, steps[-2])
+    tangents = own[None]
+    for step in steps:
+        tangents = widen(tangents, step)
+    near, far, tangents = tie((near, far, tangents))
+    states = jnp.concatenate([states, near, far, *cross(near, far)], axis=0)
+    near, far = swap(tangents, 2), swap(tangents, 4)
+    states, near, far, w_in, cubic, lam_two = tie((states, near, far, w_in, cubic, lam_two))
+    states = jnp.concatenate([states, swap(states, 1)], axis=0)
+    states, near, far = tie((states, near, far))
+    tangents = jnp.concatenate([tangents, near, far, *cross(near, far)], axis=0)
     states = states.reshape(-1, tall, columns)
     everyone = (stencil + 1) * count
     send, adv_all, adv_two, route = call(
@@ -355,12 +382,11 @@
         [Placed(HBM, (slot_count, *block)), shape((tall, everyone * columns)), shape((tall, wide)),
          Placed(SMEM, (everyone, stencil), jnp.int32)],
         [slots], [states, cubic, w_in, w_out_pad, w_in_t, w_out_t, lam_two], 7 * mix + 11 * net,
-        [VMEM((peers, rest, columns), jnp.int32), SMEM((peers, rest, columns), jnp.int32),
-         VMEM((count * stencil, *block), BF), sem, sem],
+        [VMEM(notes, jnp.int32), SMEM(notes, jnp.int32), VMEM((count * stencil, *block), BF), VMEM((hid, wide), F32), sem, sem],
     )
     recv_three = exchange(send)
     _, tangents = tie((send, tangents))
-    tangents = widen(tangents, 1).reshape(-1, tall, columns)
+    tangents = jnp.concatenate([tangents, swap(tangents, 1)], axis=0).reshape(-1, tall, columns)
     part_in, part_out, adv_one, hidden_one, slope_one = call(
         between_kernel,
         [shape((channels, hid), F32)] * 2 + [shape((tall, wide))] + [shape((hid, wide))] * 2,
@@ -384,16 +410,15 @@
         [lam_one, hidden_one, ghid_one, adv_one, part_in, part_out], 2 * net,
     )
     mine = add(mine, swap(give, 1))
-    step = 2
-    while step < peers:
-        if 2 * step < peers:
-            near, far, both = swap(mine, step), swap(mine, 2 * step), swap(mine, 3 * step)
-            mine = ((mine.astype(F32) + near.astype(F32)) + (far.astype(F32) + both.astype(F32))).astype(BF)
-            step *= 4
-        else:
-            mine, recv_four, pert = tie((mine, recv_four, pert))
-            mine = add(mine, swap(mine, step))
-            step *= 2
+    step = peers // 2
+    if len(steps) % 2:
+        mine = add(mine, swap(mine, step))
+        step //= 2
+    while step > 1:
+        near, far, both = swap(mine, step // 2), swap(mine, step), swap(mine, step // 2 * 3)
+        mine = ((mine.astype(F32) + near.astype(F32)) + (far.astype(F32) + both.astype(F32))).astype(BF)
+        step //= 4
+    mine, recv_four = tie((mine, recv_four))
     (back,) = call(functools.partial(last_kernel, slot_count), [shape(blocks, F32)], [sends], [recv_four], net)
     other = swap(mine, 1)
     grad_in = jnp.where(side == 0, mine, other).astype(F32).T

time: 80.9 us -> 74.5 us (0.921)
  waiting for transfers between devices: 33.6 us -> 23.5 us
  local copies, waits for them, and re-layouts: 0.15 us -> 3.75 us
    ppermute x14 -> x18, waiting for transfers between devices: 29.1 us -> 19 us  [swap(): return lax.ppermute(values, 'lat', [(i, i ^ step) for i in range(peers)])]
    unnamed x8 -> x16, local copies, waits for them, and re-layouts: 0.02 us -> 3.69 us
    ppermute x14 -> x18, starting transfers between devices: 18.1 us -> 18.8 us  [swap(): return lax.ppermute(values, 'lat', [(i, i ^ step) for i in range(peers)])]
  transfers between devices with their start and end apart: 16 -> 20, of which waited for: 12 -> 11; matrix products, arithmetic and copies ran while one was open for 2% -> 2% of each run, Pallas kernels for 16% -> 16%
where the time goes in v4:
time: 74.5 us; the launch traced here: 73.9 us
  starting transfers between devices  28.5 us (38%)
  waiting for transfers between devices  23.5 us (32%)
  Pallas kernels  15 us (20%)
  local copies, waits for them, and re-layouts  3.75 us (5%)
  other arithmetic  2.19 us (3%)
  between operations  0.93 us (1%)
    ppermute x18, waiting for transfers between devices, swap(): return lax.ppermute(values, 'lat', [(i, i ^ step) for i in range(peers)])  19 us
    ppermute x18, starting transfers between devices, swap(): return lax.ppermute(values, 'lat', [(i, i ^ step) for i in range(peers)])  18.8 us
    pallas_call x7, Pallas kernels, call(): pl.pallas_call(kernel, out_shape=tuple((o.memory_space(o.shape, o.dtype)...  13 us
    all_to_all x2, starting transfers between devices, exchange(): lax.all_to_all(packed, 'lat', split_axis=0, concat_axis=0, tiled=True)  9.69 us
    all_to_all x2, waiting for transfers between devices, exchange(): lax.all_to_all(packed, 'lat', split_axis=0, concat_axis=0, tiled=True)  4.51 us
    unnamed x16, local copies, waits for them, and re-layouts  3.69 us
    pallas_call x2, Pallas kernels, load(): pl.pallas_call(kernel, out_shape=out_shape, in_specs=[pl.BlockSpec(memory...  1.96 us
  transfers between devices with their start and end apart: 20, of which 11 were waited for; matrix products, arithmetic and copies ran while one was open for 2% of the time, Pallas kernels for 16%

profile of v4, /device:TPU:0, one launch (start us, length us, event | category | flops | bytes accessed | tf_op | source)
XLA Modules:
  0.0 73.9 jit_solution(4731500992959172868)
XLA Ops:
  0.6 1.0 %shard_map.112 = bf16[4,80,128]{2,1,0:T(8,128)(2,1)S(1)} custom-call(s32[2,4,4]{2,1,0:T(4,128)} %slots_in_ref.3, s32[2,1,1,16]{3,2,1,0:T(1,128)} %bitcast.36, bf16[4,72,128]{2,1,0:T(8,128)(2,1)} %state_in_ref.1), custom_call_target="tpu_custom_call" | custom-call | tf_op jit(solution)/shard_map/pallas_call | solution.py:335
  1.7 4.1 %collective-permute-start = (bf16[1,4,80,128]{3,2,1,0:T(8,128)(2,1)S(1)}, bf16[1,4,80,128]{3,2,1,0:T(8,128)(2,1)S(1)}, u32[]{:S(2)}, u32[]{:S(2)}) collective-permute-start(bf16[1,4,80,128]{3,2,1,0:T(8,128)(2,1)S(1)} %bitcast.24), channel_id=1, source_target_pairs={{0,8},{1,9},{2,10},{3,11},{4,12},{5,13},{6,14},{7,15},{8,0},{9,1},... | collective-permute-start | bytes 245768 | tf_op jit(solution)/shard_map/ppermute | solution.py:320
  5.8 0.9 %shard_map.111 = (bf16[4,80,128]{2,1,0:T(8,128)(2,1)S(1)}, s32[2,4,4]{2,1,0:T(4,128)S(4)}, s32[2,1,1,16]{3,2,1,0:T(1,128)S(4)}) custom-call(s32[2,4,4]{2,1,0:T(4,128)} %slots_in_ref.3, s32[2,1,1,16]{3,2,1,0:T(1,128)} %bitcast.37, bf16[4,72,128]{2,1,0:T(8,128)(2,1)} %tangent_in_ref.1), custom_call_target="tpu_custom_call" | custom-call | tf_op jit(solution)/shard_map/pallas_call | solution.py:335
  6.7 0.1 collective-permute-start.3
  6.8 0.9 %copy-done = bf16[512,72]{0,1:T(8,128)(2,1)S(1)} copy-done((bf16[512,72]{0,1:T(8,128)(2,1)S(1)}, bf16[512,72]{0,1:T(8,128)(2,1)}, u32[]{:S(2)}) %copy-start) | copy-done | bytes 73752
  7.7 0.9 %copy-done.2 = bf16[4,128,128]{2,1,0:T(8,128)(2,1)S(1)} copy-done((bf16[4,128,128]{2,1,0:T(8,128)(2,1)S(1)}, bf16[4,128,128]{2,1,0:T(8,128)(2,1)}, u32[]{:S(2)}) %copy-start.2) | copy-done | bytes 131096
  8.6 0.9 %copy-done.3 = bf16[72,512]{1,0:T(8,128)(2,1)S(1)} copy-done((bf16[72,512]{1,0:T(8,128)(2,1)S(1)}, bf16[72,512]{1,0:T(8,128)(2,1)}, u32[]{:S(2)}) %copy-start.3) | copy-done | bytes 73752
  9.5 0.9 %copy-done.4 = bf16[4,72,128]{2,1,0:T(8,128)(2,1)S(1)} copy-done((bf16[4,72,128]{2,1,0:T(8,128)(2,1)S(1)}, bf16[4,72,128]{2,1,0:T(8,128)(2,1)}, u32[]{:S(2)}) %copy-start.4) | copy-done | bytes 73752
  10.4 0.1 shard_map.113
  10.5 1.9 %collective-permute-start.1 = (bf16[2,4,80,128]{3,2,1,0:T(8,128)(2,1)S(1)}, bf16[2,4,80,128]{3,2,1,0:T(8,128)(2,1)S(1)}, u32[]{:S(2)}, u32[]{:S(2)}) collective-permute-start(bf16[2,4,80,128]{3,2,1,0:T(8,128)(2,1)S(1)} %maximum_bitcast_fusion), channel_id=1, source_target_pairs={{0,2},{1,3},{2,0},{3,1},{4,6},{5,7},{6,4},{7,5},{8,10},{9,11},{10,... | collective-permute-start | bytes 491528 | tf_op jit(solution)/shard_map/ppermute | solution.py:320
  12.4 1.8 %collective-permute-start.2 = (bf16[2,4,80,128]{3,2,1,0:T(8,128)(2,1)S(1)}, bf16[2,4,80,128]{3,2,1,0:T(8,128)(2,1)S(1)}, u32[]{:S(2)}, u32[]{:S(2)}) collective-permute-start(bf16[2,4,80,128]{3,2,1,0:T(8,128)(2,1)S(1)} %maximum_bitcast_fusion), channel_id=1, source_target_pairs={{0,4},{1,5},{2,6},{3,7},{4,0},{5,1},{6,2},{7,3},{8,12},{9,13},{10,... | collective-permute-start | bytes 491528 | tf_op jit(solution)/shard_map/ppermute | solution.py:320
  14.3 2.0 %collective-permute-done.1 = bf16[2,4,80,128]{3,2,1,0:T(8,128)(2,1)S(1)} collective-permute-done((bf16[2,4,80,128]{3,2,1,0:T(8,128)(2,1)S(1)}, bf16[2,4,80,128]{3,2,1,0:T(8,128)(2,1)S(1)}, u32[]{:S(2)}, u32[]{:S(2)}) %collective-permute-start.1) | collective-permute-done | bytes 163872 | tf_op jit(solution)/shard_map/ppermute | solution.py:320
  16.3 1.8 %collective-permute-done.2 = bf16[2,4,80,128]{3,2,1,0:T(8,128)(2,1)S(1)} collective-permute-done((bf16[2,4,80,128]{3,2,1,0:T(8,128)(2,1)S(1)}, bf16[2,4,80,128]{3,2,1,0:T(8,128)(2,1)S(1)}, u32[]{:S(2)}, u32[]{:S(2)}) %collective-permute-start.2) | collective-permute-done | bytes 163872 | tf_op jit(solution)/shard_map/ppermute | solution.py:320
  18.1 0.6 collective-permute-start.6
  18.7 1.7 %collective-permute-start.7 = (bf16[2,4,80,128]{3,2,1,0:T(8,128)(2,1)S(1)}, bf16[2,4,80,128]{3,2,1,0:T(8,128)(2,1)S(1)}, u32[]{:S(2)}, u32[]{:S(2)}) collective-permute-start(bf16[2,4,80,128]{3,2,1,0:T(8,128)(2,1)S(1)} %maximum_bitcast_fusion.1), channel_id=1, source_target_pairs={{0,4},{1,5},{2,6},{3,7},{4,0},{5,1},{6,2},{7,3},{8,12},{9,13},{10,... | collective-permute-start | bytes 491528 | tf_op jit(solution)/shard_map/ppermute | solution.py:320
  20.4 1.5 %collective-permute-start.4 = (bf16[1,4,80,128]{3,2,1,0:T(8,128)(2,1)S(1)}, bf16[1,4,80,128]{3,2,1,0:T(8,128)(2,1)S(1)}, u32[]{:S(2)}, u32[]{:S(2)}) collective-permute-start(bf16[1,4,80,128]{3,2,1,0:T(8,128)(2,1)S(1)} %slice.12), channel_id=1, source_target_pairs={{0,2},{1,3},{2,0},{3,1},{4,6},{5,7},{6,4},{7,5},{8,10},{9,11},{10,... | collective-permute-start | bytes 245768 | tf_op jit(solution)/shard_map/ppermute | solution.py:320
  21.9 0.3 collective-permute-start.5
  22.3 2.7 %collective-permute-done.4 = bf16[1,4,80,128]{3,2,1,0:T(8,128)(2,1)S(1)} collective-permute-done((bf16[1,4,80,128]{3,2,1,0:T(8,128)(2,1)S(1)}, bf16[1,4,80,128]{3,2,1,0:T(8,128)(2,1)S(1)}, u32[]{:S(2)}, u32[]{:S(2)}) %collective-permute-start.4) | collective-permute-done | bytes 81952 | tf_op jit(solution)/shard_map/ppermute | solution.py:320
  24.9 1.4 %collective-permute-done.5 = bf16[1,4,80,128]{3,2,1,0:T(8,128)(2,1)S(1)} collective-permute-done((bf16[1,4,80,128]{3,2,1,0:T(8,128)(2,1)S(1)}, bf16[1,4,80,128]{3,2,1,0:T(8,128)(2,1)S(1)}, u32[]{:S(2)}, u32[]{:S(2)}) %collective-permute-start.5) | collective-permute-done | bytes 81952 | tf_op jit(solution)/shard_map/ppermute | solution.py:320
  26.4 0.1 collective-permute-start.8
  26.5 2.1 %collective-permute-done.8 = bf16[8,4,80,128]{3,2,1,0:T(8,128)(2,1)S(1)} collective-permute-done((bf16[8,4,80,128]{3,2,1,0:T(8,128)(2,1)S(1)}, bf16[8,4,80,128]{3,2,1,0:T(8,128)(2,1)S(1)}, u32[]{:S(2)}, u32[]{:S(2)}) %collective-permute-start.8) | collective-permute-done | bytes 655392 | tf_op jit(solution)/shard_map/ppermute | solution.py:320
  28.6 0.1 pad_maximum_fusion
  28.7 0.6 collective-permute-start.9
  29.4 1.1 %collective-permute-start.10 = (bf16[1,4,80,128]{3,2,1,0:T(8,128)(2,1)S(1)}, bf16[1,4,80,128]{3,2,1,0:T(8,128)(2,1)S(1)}, u32[]{:S(2)}, u32[]{:S(2)}) collective-permute-start(bf16[1,4,80,128]{3,2,1,0:T(8,128)(2,1)S(1)} %slice.15), channel_id=1, source_target_pairs={{0,4},{1,5},{2,6},{3,7},{4,0},{5,1},{6,2},{7,3},{8,12},{9,13},{10,... | collective-permute-start | bytes 245768 | tf_op jit(solution)/shard_map/ppermute | solution.py:320
  30.6 5.3 %shard_map.114 = (bf16[16,72,128]{2,1,0:T(8,128)(2,1)}, bf16[80,2560]{1,0:T(8,128)(2,1)S(1)}, bf16[80,512]{1,0:T(8,128)(2,1)S(1)}, s32[20,4]{1,0:T(8,128)S(4)}) custom-call(s32[2,4,4]{2,1,0:T(4,128)S(4)} %get-tuple-element.43.slots_ref, bf16[64,80,128]{2,1,0:T(8,128)(2,1)S(1)} %bitcast.22, bf16[512,128]{1,0:T(8,128)(2,1)S(1)} %get-tuple-element.55.cubic_ref, ...), custom_call_target="tpu_custom_call" | custom-call | flops 679477248 | bytes 2613568 | tf_op jit(solution)/shard_map/pallas_call | solution.py:33
  35.9 0.1 collective-permute-start.11
  36.0 6.2 %all-to-all-start = ((bf16[16,72,128]{2,1,0:T(8,128)(2,1)}), bf16[16,72,128]{2,1,0:T(8,128)(2,1)S(1)}, u32[]{:S(2)}, u32[]{:S(2)}) async-start(bf16[16,72,128]{2,1,0:T(8,128)(2,1)} %get-tuple-element.60), calls=%async_computation | async-start | bytes 589824 | tf_op jit(solution)/shard_map/all_to_all | solution.py:317
  42.2 1.2 %shard_map.116 = (f32[72,512]{1,0:T(8,128)S(1)}, f32[72,512]{1,0:T(8,128)S(1)}, bf16[80,512]{1,0:T(8,128)(2,1)S(1)}, bf16[512,512]{1,0:T(8,128)(2,1)S(1)}, bf16[512,512]{1,0:T(8,128)(2,1)S(1)}) custom-call(bf16[72,512]{1,0:T(8,128)(2,1)S(1)} %get-tuple-element.59.lam_two_ref, bf16[512,80]{1,0:T(8,128)(2,1)S(1)} %get-tuple-element.56.w_in_ref, ...), custom_call_target="tpu_custom_call" | custom-call | flops 188743680 | bytes 2146304 | tf_op jit(solution)/shard_map/pallas_call | solution.py:33
  43.4 1.2 %pad_maximum_fusion.1 = bf16[16,4,80,128]{3,2,1,0:T(8,128)(2,1)S(1)} fusion(bf16[8,4,80,128]{3,2,1,0:T(8,128)(2,1)} %collective-permute-done.11, bf16[8,4,80,128]{3,2,1,0:T(8,128)(2,1)S(1)} %constant_dynamic-update-slice_fusion.5), kind=kLoop, calls=%fused_computation.1 | loop fusion | flops 655360 | bytes 2621440 | tf_op jit(solution)/shard_map/concatenate | solution.py:389
  44.6 3.7 %shard_map.115 = bf16[4,72,128]{2,1,0:T(8,128)(2,1)} custom-call(s32[20,4]{1,0:T(8,128)S(4)} %get-tuple-element.61.route_ref, bf16[64,80,128]{2,1,0:T(8,128)(2,1)S(1)} %bitcast.23, bf16[512,128]{1,0:T(8,128)(2,1)S(1)} %get-tuple-element.55.cubic_ref, bf16[512,80]{1,0:T(8,128)(2,1)S(1)} %get-tuple-element.56.w_in_ref, ...), custom_call_target="tpu_custom_call" | custom-call | flops 754974720 | bytes 2170880 | tf_op jit(solution)/shard_map/pallas_call | solution.py:33
  48.2 4.5 %all-to-all-done.recv_ref = bf16[16,72,128]{2,1,0:T(8,128)(2,1)S(1)} async-done(((bf16[16,72,128]{2,1,0:T(8,128)(2,1)}), bf16[16,72,128]{2,1,0:T(8,128)(2,1)S(1)}, u32[]{:S(2)}, u32[]{:S(2)}) %all-to-all-start) | async-done | bytes 294944 | tf_op jit(solution)/shard_map/all_to_all | solution.py:317
  52.7 1.4 %shard_map.117 = (bf16[16,72,128]{2,1,0:T(8,128)(2,1)}, bf16[72,512]{1,0:T(8,128)(2,1)S(1)}, bf16[512,512]{1,0:T(8,128)(2,1)S(1)}) custom-call(s32[2,4,4]{2,1,0:T(4,128)S(4)} %get-tuple-element.43.slots_ref, s32[2,1,1,16]{3,2,1,0:T(1,128)S(4)} %get-tuple-element.68.sends_ref, bf16[16,72,128]{2,1,0:T(8,128)(2,1)S(1)} %all-to-all-done.recv_ref, ...), custom_call_target="tpu_custom_call" | custom-call | flops 113246208 | bytes 1990656 | tf_op jit(solution)/shard_map/pallas_call | solution.py:33
  54.2 0.5 shard_map.118
  54.7 0.1 collective-permute-start.12
  54.7 1.3 %collective-permute-done.12 = bf16[72,512]{1,0:T(8,128)(2,1)S(1)} collective-permute-done((bf16[72,512]{1,0:T(8,128)(2,1)S(1)}, bf16[72,512]{1,0:T(8,128)(2,1)S(1)}, u32[]{:S(2)}, u32[]{:S(2)}) %collective-permute-start.12) | collective-permute-done | bytes 73760 | tf_op jit(solution)/shard_map/ppermute | solution.py:320
  56.0 1.3 %collective-permute-start.13 = (bf16[72,512]{1,0:T(8,128)(2,1)S(1)}, bf16[72,512]{1,0:T(8,128)(2,1)S(1)}, u32[]{:S(2)}, u32[]{:S(2)}) collective-permute-start(bf16[72,512]{1,0:T(8,128)(2,1)S(1)} %add_convert_fusion.2), channel_id=1, source_target_pairs={{0,8},{1,9},{2,10},{3,11},{4,12},{5,13},{6,14},{7,15},{8,0},{9,1},... | collective-permute-start | bytes 221192 | tf_op jit(solution)/shard_map/ppermute | solution.py:320
  57.3 3.5 %all-to-all-start.1 = ((bf16[16,72,128]{2,1,0:T(8,128)(2,1)}), bf16[16,72,128]{2,1,0:T(8,128)(2,1)S(1)}, u32[]{:S(2)}, u32[]{:S(2)}) async-start(bf16[16,72,128]{2,1,0:T(8,128)(2,1)} %get-tuple-element.79), calls=%async_computation.1 | async-start | bytes 589824 | tf_op jit(solution)/shard_map/all_to_all | solution.py:317
  60.8 2.0 %collective-permute-done.13 = bf16[72,512]{1,0:T(8,128)(2,1)S(1)} collective-permute-done((bf16[72,512]{1,0:T(8,128)(2,1)S(1)}, bf16[72,512]{1,0:T(8,128)(2,1)S(1)}, u32[]{:S(2)}, u32[]{:S(2)}) %collective-permute-start.13) | collective-permute-done | bytes 73760 | tf_op jit(solution)/shard_map/ppermute | solution.py:320
  62.9 0.8 %collective-permute-start.16 = (bf16[72,512]{1,0:T(8,128)(2,1)S(1)}, bf16[72,512]{1,0:T(8,128)(2,1)S(1)}, u32[]{:S(2)}, u32[]{:S(2)}) collective-permute-start(bf16[72,512]{1,0:T(8,128)(2,1)S(1)} %add_convert_fusion.1), channel_id=1, source_target_pairs={{0,6},{1,7},{2,4},{3,5},{4,2},{5,3},{6,0},{7,1},{8,14},{9,15},{10,... | collective-permute-start | bytes 221192 | tf_op jit(solution)/shard_map/ppermute | solution.py:320
  63.7 1.3 %collective-permute-start.15 = (bf16[72,512]{1,0:T(8,128)(2,1)S(1)}, bf16[72,512]{1,0:T(8,128)(2,1)S(1)}, u32[]{:S(2)}, u32[]{:S(2)}) collective-permute-start(bf16[72,512]{1,0:T(8,128)(2,1)S(1)} %add_convert_fusion.1), channel_id=1, source_target_pairs={{0,4},{1,5},{2,6},{3,7},{4,0},{5,1},{6,2},{7,3},{8,12},{9,13},{10,... | collective-permute-start | bytes 221192 | tf_op jit(solution)/shard_map/ppermute | solution.py:320
  64.9 1.5 %collective-permute-start.14 = (bf16[72,512]{1,0:T(8,128)(2,1)S(1)}, bf16[72,512]{1,0:T(8,128)(2,1)S(1)}, u32[]{:S(2)}, u32[]{:S(2)}) collective-permute-start(bf16[72,512]{1,0:T(8,128)(2,1)S(1)} %add_convert_fusion.1), channel_id=1, source_target_pairs={{0,2},{1,3},{2,0},{3,1},{4,6},{5,7},{6,4},{7,5},{8,10},{9,11},{10,... | collective-permute-start | bytes 221192 | tf_op jit(solution)/shard_map/ppermute | solution.py:320
  66.5 4.8 %collective-permute-done.16 = bf16[72,512]{1,0:T(8,128)(2,1)S(1)} collective-permute-done((bf16[72,512]{1,0:T(8,128)(2,1)S(1)}, bf16[72,512]{1,0:T(8,128)(2,1)S(1)}, u32[]{:S(2)}, u32[]{:S(2)}) %collective-permute-start.16) | collective-permute-done | bytes 73760 | tf_op jit(solution)/shard_map/ppermute | solution.py:320
  71.2 0.5 collective-permute-done.15
  71.8 0.0 all-to-all-done.1.recv_ref
  71.8 0.1 collective-permute-start.17
  71.9 0.8 %shard_map.119 = f32[4,72,128]{2,1,0:T(8,128)} custom-call(s32[2,1,1,16]{3,2,1,0:T(1,128)S(4)} %get-tuple-element.68.sends_ref, bf16[16,72,128]{2,1,0:T(8,128)(2,1)S(1)} %all-to-all-done.1.recv_ref), custom_call_target="tpu_custom_call" | custom-call | flops 37748736 | bytes 442368 | tf_op jit(solution)/shard_map/pallas_call | solution.py:33
  72.7 0.4 collective-permute-done.17
  73.2 0.7 select_convert_fusion
  (32 shorter events, 0.4 us)
Async XLA Ops:
  1.7 8.8 %collective-permute-start = (bf16[1,4,80,128]{3,2,1,0:T(8,128)(2,1)S(1)}, bf16[1,4,80,128]{3,2,1,0:T(8,128)(2,1)S(1)}, u32[]{:S(2)}, u32[]{:S(2)}) collective-permute-start(bf16[1,4,80,128]{3,2,1,0:T(8,128)(2,1)S(1)} %bitcast.24), channel_id=1, source_target_pairs={{0,8},{1,9},{2,10},{3,11},{4,12},{5,13},{6,14},{7,15},{8,0},{9,1},... | collective-permute-start | bytes 245768 | tf_op jit(solution)/shard_map/ppermute | solution.py:320
  6.7 7.5 %collective-permute-start.3 = (bf16[1,4,80,128]{3,2,1,0:T(8,128)(2,1)S(1)}, bf16[1,4,80,128]{3,2,1,0:T(8,128)(2,1)S(1)}, u32[]{:S(2)}, u32[]{:S(2)}) collective-permute-start(bf16[1,4,80,128]{3,2,1,0:T(8,128)(2,1)S(1)} %bitcast.31), channel_id=1, source_target_pairs={{0,8},{1,9},{2,10},{3,11},{4,12},{5,13},{6,14},{7,15},{8,0},{9,1},... | collective-permute-start | bytes 245768 | tf_op jit(solution)/shard_map/ppermute | solution.py:320
  6.8 0.9 %copy-start = (bf16[512,72]{0,1:T(8,128)(2,1)S(1)}, bf16[512,72]{0,1:T(8,128)(2,1)}, u32[]{:S(2)}) copy-start(bf16[512,72]{0,1:T(8,128)(2,1)} %param.12) | copy-start | bytes 221188
  7.7 0.9 %copy-start.2 = (bf16[4,128,128]{2,1,0:T(8,128)(2,1)S(1)}, bf16[4,128,128]{2,1,0:T(8,128)(2,1)}, u32[]{:S(2)}) copy-start(bf16[4,128,128]{2,1,0:T(8,128)(2,1)} %param.11) | copy-start | bytes 393220
  8.6 0.9 %copy-start.3 = (bf16[72,512]{1,0:T(8,128)(2,1)S(1)}, bf16[72,512]{1,0:T(8,128)(2,1)}, u32[]{:S(2)}) copy-start(bf16[72,512]{1,0:T(8,128)(2,1)} %w_out_ref.1) | copy-start | bytes 221188
  9.5 0.9 %copy-start.4 = (bf16[4,72,128]{2,1,0:T(8,128)(2,1)S(1)}, bf16[4,72,128]{2,1,0:T(8,128)(2,1)}, u32[]{:S(2)}) copy-start(bf16[4,72,128]{2,1,0:T(8,128)(2,1)} %cot_ref.1) | copy-start | bytes 221188
  10.5 5.7 %collective-permute-start.1 = (bf16[2,4,80,128]{3,2,1,0:T(8,128)(2,1)S(1)}, bf16[2,4,80,128]{3,2,1,0:T(8,128)(2,1)S(1)}, u32[]{:S(2)}, u32[]{:S(2)}) collective-permute-start(bf16[2,4,80,128]{3,2,1,0:T(8,128)(2,1)S(1)} %maximum_bitcast_fusion), channel_id=1, source_target_pairs={{0,2},{1,3},{2,0},{3,1},{4,6},{5,7},{6,4},{7,5},{8,10},{9,11},{10,... | collective-permute-start | bytes 491528 | tf_op jit(solution)/shard_map/ppermute | solution.py:320
  12.4 5.6 %collective-permute-start.2 = (bf16[2,4,80,128]{3,2,1,0:T(8,128)(2,1)S(1)}, bf16[2,4,80,128]{3,2,1,0:T(8,128)(2,1)S(1)}, u32[]{:S(2)}, u32[]{:S(2)}) collective-permute-start(bf16[2,4,80,128]{3,2,1,0:T(8,128)(2,1)S(1)} %maximum_bitcast_fusion), channel_id=1, source_target_pairs={{0,4},{1,5},{2,6},{3,7},{4,0},{5,1},{6,2},{7,3},{8,12},{9,13},{10,... | collective-permute-start | bytes 491528 | tf_op jit(solution)/shard_map/ppermute | solution.py:320
  18.1 8.3 %collective-permute-start.6 = (bf16[2,4,80,128]{3,2,1,0:T(8,128)(2,1)S(1)}, bf16[2,4,80,128]{3,2,1,0:T(8,128)(2,1)S(1)}, u32[]{:S(2)}, u32[]{:S(2)}) collective-permute-start(bf16[2,4,80,128]{3,2,1,0:T(8,128)(2,1)S(1)} %maximum_bitcast_fusion.1), channel_id=1, source_target_pairs={{0,2},{1,3},{2,0},{3,1},{4,6},{5,7},{6,4},{7,5},{8,10},{9,11},{10,... | collective-permute-start | bytes 491528 | tf_op jit(solution)/shard_map/ppermute | solution.py:320
  18.7 7.7 %collective-permute-start.7 = (bf16[2,4,80,128]{3,2,1,0:T(8,128)(2,1)S(1)}, bf16[2,4,80,128]{3,2,1,0:T(8,128)(2,1)S(1)}, u32[]{:S(2)}, u32[]{:S(2)}) collective-permute-start(bf16[2,4,80,128]{3,2,1,0:T(8,128)(2,1)S(1)} %maximum_bitcast_fusion.1), channel_id=1, source_target_pairs={{0,4},{1,5},{2,6},{3,7},{4,0},{5,1},{6,2},{7,3},{8,12},{9,13},{10,... | collective-permute-start | bytes 491528 | tf_op jit(solution)/shard_map/ppermute | solution.py:320
  20.4 4.5 %collective-permute-start.4 = (bf16[1,4,80,128]{3,2,1,0:T(8,128)(2,1)S(1)}, bf16[1,4,80,128]{3,2,1,0:T(8,128)(2,1)S(1)}, u32[]{:S(2)}, u32[]{:S(2)}) collective-permute-start(bf16[1,4,80,128]{3,2,1,0:T(8,128)(2,1)S(1)} %slice.12), channel_id=1, source_target_pairs={{0,2},{1,3},{2,0},{3,1},{4,6},{5,7},{6,4},{7,5},{8,10},{9,11},{10,... | collective-permute-start | bytes 245768 | tf_op jit(solution)/shard_map/ppermute | solution.py:320
  21.9 4.4 %collective-permute-start.5 = (bf16[1,4,80,128]{3,2,1,0:T(8,128)(2,1)S(1)}, bf16[1,4,80,128]{3,2,1,0:T(8,128)(2,1)S(1)}, u32[]{:S(2)}, u32[]{:S(2)}) collective-permute-start(bf16[1,4,80,128]{3,2,1,0:T(8,128)(2,1)S(1)} %slice.13), channel_id=1, source_target_pairs={{0,4},{1,5},{2,6},{3,7},{4,0},{5,1},{6,2},{7,3},{8,12},{9,13},{10,... | collective-permute-start | bytes 245768 | tf_op jit(solution)/shard_map/ppermute | solution.py:320
  26.4 2.2 %collective-permute-start.8 = (bf16[8,4,80,128]{3,2,1,0:T(8,128)(2,1)S(1)}, bf16[8,4,80,128]{3,2,1,0:T(8,128)(2,1)S(1)}, u32[]{:S(2)}, u32[]{:S(2)}) collective-permute-start(bf16[8,4,80,128]{3,2,1,0:T(8,128)(2,1)S(1)} %constant_dynamic-update-slice_fusion), channel_id=1, source_target_pairs={{0,1},{1,0},{2,3},{3,2},{4,5},{5,4},{6,7},{7,6},{8,9},{9,8},{10,11... | collective-permute-start | bytes 1966088 | tf_op jit(solution)/shard_map/ppermute | solution.py:320
  28.7 7.1 %collective-permute-start.9 = (bf16[1,4,80,128]{3,2,1,0:T(8,128)(2,1)S(1)}, bf16[1,4,80,128]{3,2,1,0:T(8,128)(2,1)S(1)}, u32[]{:S(2)}, u32[]{:S(2)}) collective-permute-start(bf16[1,4,80,128]{3,2,1,0:T(8,128)(2,1)S(1)} %slice.14), channel_id=1, source_target_pairs={{0,2},{1,3},{2,0},{3,1},{4,6},{5,7},{6,4},{7,5},{8,10},{9,11},{10,... | collective-permute-start | bytes 245768 | tf_op jit(solution)/shard_map/ppermute | solution.py:320
  29.4 6.5 %collective-permute-start.10 = (bf16[1,4,80,128]{3,2,1,0:T(8,128)(2,1)S(1)}, bf16[1,4,80,128]{3,2,1,0:T(8,128)(2,1)S(1)}, u32[]{:S(2)}, u32[]{:S(2)}) collective-permute-start(bf16[1,4,80,128]{3,2,1,0:T(8,128)(2,1)S(1)} %slice.15), channel_id=1, source_target_pairs={{0,4},{1,5},{2,6},{3,7},{4,0},{5,1},{6,2},{7,3},{8,12},{9,13},{10,... | collective-permute-start | bytes 245768 | tf_op jit(solution)/shard_map/ppermute | solution.py:320
  35.9 7.4 %collective-permute-start.11 = (bf16[8,4,80,128]{3,2,1,0:T(8,128)(2,1)S(1)}, bf16[8,4,80,128]{3,2,1,0:T(8,128)(2,1)}, u32[]{:S(2)}, u32[]{:S(2)}) collective-permute-start(bf16[8,4,80,128]{3,2,1,0:T(8,128)(2,1)S(1)} %constant_dynamic-update-slice_fusion.5), channel_id=1, source_target_pairs={{0,1},{1,0},{2,3},{3,2},{4,5},{5,4},{6,7},{7,6},{8,9},{9,8},{10,11... | collective-permute-start | bytes 1966088 | tf_op jit(solution)/shard_map/ppermute | solution.py:320
  36.0 16.7 %all-to-all-start = ((bf16[16,72,128]{2,1,0:T(8,128)(2,1)}), bf16[16,72,128]{2,1,0:T(8,128)(2,1)S(1)}, u32[]{:S(2)}, u32[]{:S(2)}) async-start(bf16[16,72,128]{2,1,0:T(8,128)(2,1)} %get-tuple-element.60), calls=%async_computation | async-start | bytes 589824 | tf_op jit(solution)/shard_map/all_to_all | solution.py:317
  44.6 8.2 %copy-start.1 = (bf16[512,72]{0,1:T(8,128)(2,1)S(1)}, bf16[512,72]{0,1:T(8,128)(2,1)}, u32[]{:S(2)}) copy-start(bf16[512,72]{0,1:T(8,128)(2,1)} %param.12) | copy-start | bytes 221188
  54.7 1.3 %collective-permute-start.12 = (bf16[72,512]{1,0:T(8,128)(2,1)S(1)}, bf16[72,512]{1,0:T(8,128)(2,1)S(1)}, u32[]{:S(2)}, u32[]{:S(2)}) collective-permute-start(bf16[72,512]{1,0:T(8,128)(2,1)S(1)} %get-tuple-element.78), channel_id=1, source_target_pairs={{0,1},{1,0},{2,3},{3,2},{4,5},{5,4},{6,7},{7,6},{8,9},{9,8},{10,11... | collective-permute-start | bytes 221192 | tf_op jit(solution)/shard_map/ppermute | solution.py:320
  56.0 6.9 %collective-permute-start.13 = (bf16[72,512]{1,0:T(8,128)(2,1)S(1)}, bf16[72,512]{1,0:T(8,128)(2,1)S(1)}, u32[]{:S(2)}, u32[]{:S(2)}) collective-permute-start(bf16[72,512]{1,0:T(8,128)(2,1)S(1)} %add_convert_fusion.2), channel_id=1, source_target_pairs={{0,8},{1,9},{2,10},{3,11},{4,12},{5,13},{6,14},{7,15},{8,0},{9,1},... | collective-permute-start | bytes 221192 | tf_op jit(solution)/shard_map/ppermute | solution.py:320
  57.3 14.6 %all-to-all-start.1 = ((bf16[16,72,128]{2,1,0:T(8,128)(2,1)}), bf16[16,72,128]{2,1,0:T(8,128)(2,1)S(1)}, u32[]{:S(2)}, u32[]{:S(2)}) async-start(bf16[16,72,128]{2,1,0:T(8,128)(2,1)} %get-tuple-element.79), calls=%async_computation.1 | async-start | bytes 589824 | tf_op jit(solution)/shard_map/all_to_all | solution.py:317
  62.9 8.3 %collective-permute-start.16 = (bf16[72,512]{1,0:T(8,128)(2,1)S(1)}, bf16[72,512]{1,0:T(8,128)(2,1)S(1)}, u32[]{:S(2)}, u32[]{:S(2)}) collective-permute-start(bf16[72,512]{1,0:T(8,128)(2,1)S(1)} %add_convert_fusion.1), channel_id=1, source_target_pairs={{0,6},{1,7},{2,4},{3,5},{4,2},{5,3},{6,0},{7,1},{8,14},{9,15},{10,... | collective-permute-start | bytes 221192 | tf_op jit(solution)/shard_map/ppermute | solution.py:320
  63.7 8.1 %collective-permute-start.15 = (bf16[72,512]{1,0:T(8,128)(2,1)S(1)}, bf16[72,512]{1,0:T(8,128)(2,1)S(1)}, u32[]{:S(2)}, u32[]{:S(2)}) collective-permute-start(bf16[72,512]{1,0:T(8,128)(2,1)S(1)} %add_convert_fusion.1), channel_id=1, source_target_pairs={{0,4},{1,5},{2,6},{3,7},{4,0},{5,1},{6,2},{7,3},{8,12},{9,13},{10,... | collective-permute-start | bytes 221192 | tf_op jit(solution)/shard_map/ppermute | solution.py:320
  64.9 6.8 %collective-permute-start.14 = (bf16[72,512]{1,0:T(8,128)(2,1)S(1)}, bf16[72,512]{1,0:T(8,128)(2,1)S(1)}, u32[]{:S(2)}, u32[]{:S(2)}) collective-permute-start(bf16[72,512]{1,0:T(8,128)(2,1)S(1)} %add_convert_fusion.1), channel_id=1, source_target_pairs={{0,2},{1,3},{2,0},{3,1},{4,6},{5,7},{6,4},{7,5},{8,10},{9,11},{10,... | collective-permute-start | bytes 221192 | tf_op jit(solution)/shard_map/ppermute | solution.py:320
  71.8 1.3 %collective-permute-start.17 = (bf16[72,512]{1,0:T(8,128)(2,1)S(1)}, bf16[72,512]{1,0:T(8,128)(2,1)S(1)}, u32[]{:S(2)}, u32[]{:S(2)}) collective-permute-start(bf16[72,512]{1,0:T(8,128)(2,1)S(1)} %add_convert_fusion), channel_id=1, source_target_pairs={{0,1},{1,0},{2,3},{3,2},{4,5},{5,4},{6,7},{7,6},{8,9},{9,8},{10,11... | collective-permute-start | bytes 221192 | tf_op jit(solution)/shard_map/ppermute | solution.py:320

commit v5 on v4

--- a/solution.py
+++ b/solution.py
@@ -154,8 +154,14 @@
         out_ref[j] = padded(tangent_ref[j], out_ref.shape[1]).astype(BF)
 
 
-def prepare_kernel(w_in_t_ref, w_out_ref, cubic_in_ref, cot_ref, w_in_ref, w_out_pad_ref, w_out_t_ref, cubic_ref, lam_ref):
-    cubic_ref[...] = cubic_in_ref[...]
+def prepare_kernel(w_in_t_hbm, w_out_hbm, cubic_hbm, cot_hbm, w_in_ref, w_out_pad_ref, w_out_t_ref, cubic_ref, lam_ref,
+                   w_in_t_ref, w_out_ref, cot_ref, sems):
+    pairs = ((w_in_t_hbm, w_in_t_ref), (w_out_hbm, w_out_ref), (cot_hbm, cot_ref), (cubic_hbm, cubic_ref))
+    loads = [pltpu.make_async_copy(a, b, sems.at[i]) for i, (a, b) in enumerate(pairs)]
+    for load in loads:
+        load.start()
+    for load in loads:
+        load.wait()
     lam_ref[...] = side_by_side(cot_ref)
     rows = w_out_pad_ref.shape[0]
     w_in_ref[...] = padded(w_in_t_ref[...], rows).T.astype(BF)
@@ -264,31 +270,28 @@
 
 
 def third_kernel(count, stencil, slots, slots_ref, sends_ref, recv_ref, cubic_ref, w_in_t_ref, w_out_t_ref, slope_ref,
-                 send_ref, lam_ref, ghid_ref, total_ref, terms_ref, sem):
+                 hidden_ref, adv_ref, part_in_ref, part_out_ref, send_ref, keep_ref, give_ref, total_ref, terms_ref, sem):
     collect(sends_ref, 1, slots, lambda q: recv_ref[q], total_ref)
     lam = side_by_side(total_ref).astype(BF)
-    lam_ref[...] = lam
     ghid = (slope_ref[...].astype(F32) * dot(w_out_t_ref[...], lam)).astype(BF)
-    ghid_ref[...] = ghid
     ladv = lam.astype(F32) + dot(w_in_t_ref[...], ghid)
     send_terms(ladv, count, stencil, 0, slots_ref, cubic_ref, terms_ref, lambda q: send_ref.at[q], sem)
-    pltpu.make_async_copy(terms_ref, terms_ref, sem).wait()
-
-
-def grad_pair_kernel(side_ref, lam_ref, hidden_ref, ghid_ref, adv_ref, in_ref, out_ref, keep_ref, give_ref):
-    grad_in = dot_nt(adv_ref[...], ghid_ref[...])
-    grad_in = (in_ref[...] + grad_in[: in_ref.shape[0]]).astype(BF)
-    grad_out = (out_ref[...] + dot_nt(lam_ref[...], hidden_ref[...])).astype(BF)
-
-    @pl.when(side_ref[0] == 0)
+    grad_in = dot_nt(adv_ref[...], ghid)
+    grad_in = (part_in_ref[...] + grad_in[: part_in_ref.shape[0]]).astype(BF)
+    grad_out = (part_out_ref[...] + dot_nt(lam, hidden_ref[...])).astype(BF)
+    side = lax.axis_index("lat") & 1
+
+    @pl.when(side == 0)
     def _():
         keep_ref[...] = grad_in
         give_ref[...] = grad_out
 
-    @pl.when(side_ref[0] != 0)
+    @pl.when(side != 0)
     def _():
         keep_ref[...] = grad_out
         give_ref[...] = grad_in
+
+    pltpu.make_async_copy(terms_ref, terms_ref, sem).wait()
 
 
 def last_kernel(slots, sends_ref, recv_ref, back_ref):
@@ -336,7 +339,7 @@
             kernel,
             out_shape=out_shape,
             in_specs=[pl.BlockSpec(memory_space=HBM)] * len(arrays),
-            out_specs=tuple(pl.BlockSpec(memory_space=place) for place in (VMEM, SMEM, SMEM)[: len(out_shape)]),
+            out_specs=tuple(pl.BlockSpec(memory_space=o.memory_space) for o in out_shape),
             scratch_shapes=scratch,
         )(*(pltpu.with_memory_space_constraint(a, HBM) for a in arrays))
 
@@ -359,11 +362,10 @@
         (VMEM((count, tall, columns), BF), SMEM(slots.shape, slots.dtype), SMEM(sends.shape, sends.dtype)),
         [VMEM(blocks, BF), sem((3,))],
     )
-    w_in, w_out_pad, w_out_t, cubic, lam_two = call(
-        prepare_kernel,
-        [shape((hid, tall)), shape((tall, hid)), shape((hid, channels)),
-         Placed(VMEM, cubic.shape), Placed(VMEM, (channels, wide))],
-        [], [w_in_t, w_out, cubic, cotangent], 0,
+    w_in, w_out_pad, w_out_t, cubic, lam_two = load(
+        prepare_kernel, (w_in_t, w_out, cubic, cotangent),
+        tuple(VMEM(dims, BF) for dims in ((hid, tall), (tall, hid), (hid, channels), cubic.shape, (channels, wide))),
+        [VMEM(w_in_t.shape, BF), VMEM(w_out.shape, BF), VMEM(blocks, BF), sem((4,))],
     )
     tangents = own[None]
     for step in steps:
@@ -371,9 +373,9 @@
     near, far, tangents = tie((near, far, tangents))
     states = jnp.concatenate([states, near, far, *cross(near, far)], axis=0)
     near, far = swap(tangents, 2), swap(tangents, 4)
-    states, near, far, w_in, cubic, lam_two = tie((states, near, far, w_in, cubic, lam_two))
+    states, w_in, cubic, lam_two = tie((states, w_in, cubic, lam_two))
     states = jnp.concatenate([states, swap(states, 1)], axis=0)
-    states, near, far = tie((states, near, far))
+    _, near, far = tie((states, near, far))
     tangents = jnp.concatenate([tangents, near, far, *cross(near, far)], axis=0)
     states = states.reshape(-1, tall, columns)
     everyone = (stencil + 1) * count
@@ -396,19 +398,14 @@
         functools.partial(tangent_kernel, count, stencil),
         [shape(blocks)], [route], [tangents, cubic, w_in, w_out_pad, adv_all, adv_two], 5 * mix + 15 * net,
     )
-    recv_three, pert = tie((recv_three, pert))
-    send, lam_one, ghid_one = call(
+    send, mine, give = call(
         functools.partial(third_kernel, *sizes),
-        [Placed(HBM, (slot_count, *block)), shape((channels, wide)), shape((hid, wide))],
-        [slots, sends], [recv_three, cubic, w_in_t, w_out_t, slope_one], mix + 2 * net,
+        [Placed(HBM, (slot_count, *block)), shape((channels, hid)), shape((channels, hid))],
+        [slots, sends],
+        [recv_three, cubic, w_in_t, w_out_t, slope_one, hidden_one, adv_one, part_in, part_out], mix + 4 * net,
         [VMEM(blocks, F32), VMEM((count * stencil, *block), BF), sem],
     )
     recv_four = exchange(send)
-    mine, give = call(
-        grad_pair_kernel,
-        [shape((channels, hid))] * 2, [side.astype(jnp.int32).reshape(1)],
-        [lam_one, hidden_one, ghid_one, adv_one, part_in, part_out], 2 * net,
-    )
     mine = add(mine, swap(give, 1))
     step = peers // 2
     if len(steps) % 2:
@@ -418,7 +415,7 @@
         near, far, both = swap(mine, step // 2), swap(mine, step), swap(mine, step // 2 * 3)
         mine = ((mine.astype(F32) + near.astype(F32)) + (far.astype(F32) + both.astype(F32))).astype(BF)
         step //= 4
-    mine, recv_four = tie((mine, recv_four))
+    mine, recv_four, pert = tie((mine, recv_four, pert))
     (back,) = call(functools.partial(last_kernel, slot_count), [shape(blocks, F32)], [sends], [recv_four], net)
     other = swap(mine, 1)
     grad_in = jnp.where(side == 0, mine, other).astype(F32).T

time: 74.5 us -> 72 us (0.966)
  starting transfers between devices: 28.5 us -> 32.8 us
  waiting for transfers between devices: 23.5 us -> 19.8 us
  local copies, waits for them, and re-layouts: 3.75 us -> 0.32 us
    ppermute x18, starting transfers between devices: 18.8 us -> 23.7 us  [swap(): return lax.ppermute(values, 'lat', [(i, i ^ step) for i in range(peers)])]
    all_to_all x2, waiting for transfers between devices: 4.51 us -> 0.49 us  [exchange(): lax.all_to_all(packed, 'lat', split_axis=0, concat_axis=0, tiled=True)]
    unnamed x16 -> x9, local copies, waits for them, and re-layouts: 3.69 us -> 0.18 us
    pallas_call x2 -> x3, Pallas kernels: 1.96 us -> 3.15 us  [load(): pl.pallas_call(kernel, out_shape=out_shape, in_specs=[pl.BlockSpec(memory...]
    pallas_call x7 -> x5, Pallas kernels: 13 us -> 12.4 us  [call(): pl.pallas_call(kernel, out_shape=tuple((o.memory_space(o.shape, o.dtype)...]
  transfers between devices with their start and end apart: 20 -> 20, of which waited for: 11 -> 13; matrix products, arithmetic and copies ran while one was open for 2% -> 2% of each run, Pallas kernels for 16% -> 20%
where the time goes in v5:
time: 72 us; the launch traced here: 71.5 us
  starting transfers between devices  32.8 us (46%)
  waiting for transfers between devices  19.8 us (28%)
  Pallas kernels  15.6 us (22%)
  other arithmetic  2.07 us (3%)
  between operations  0.88 us (1%)
    ppermute x18, starting transfers between devices, swap(): return lax.ppermute(values, 'lat', [(i, i ^ step) for i in range(peers)])  23.7 us
    ppermute x18, waiting for transfers between devices, swap(): return lax.ppermute(values, 'lat', [(i, i ^ step) for i in range(peers)])  19.3 us
    pallas_call x5, Pallas kernels, call(): pl.pallas_call(kernel, out_shape=tuple((o.memory_space(o.shape, o.dtype)...  12.4 us
    all_to_all x2, starting transfers between devices, exchange(): lax.all_to_all(packed, 'lat', split_axis=0, concat_axis=0, tiled=True)  9.13 us
    pallas_call x3, Pallas kernels, load(): pl.pallas_call(kernel, out_shape=out_shape, in_specs=[pl.BlockSpec(memory...  3.15 us
  transfers between devices with their start and end apart: 20, of which 13 were waited for; matrix products, arithmetic and copies ran while one was open for 2% of the time, Pallas kernels for 20%

profile of v5, /device:TPU:0, one launch (start us, length us, event | category | flops | bytes accessed | tf_op | source)
XLA Modules:
  0.0 71.5 jit_solution(10716896622887780732)
XLA Ops:
  0.6 1.0 %shard_map.112 = bf16[4,80,128]{2,1,0:T(8,128)(2,1)S(1)} custom-call(s32[2,4,4]{2,1,0:T(4,128)} %slots_in_ref.3, s32[2,1,1,16]{3,2,1,0:T(1,128)} %bitcast.35, bf16[4,72,128]{2,1,0:T(8,128)(2,1)} %state_in_ref.1), custom_call_target="tpu_custom_call" | custom-call | tf_op jit(solution)/shard_map/pallas_call | solution.py:338
  1.7 4.1 %collective-permute-start = (bf16[1,4,80,128]{3,2,1,0:T(8,128)(2,1)S(1)}, bf16[1,4,80,128]{3,2,1,0:T(8,128)(2,1)S(1)}, u32[]{:S(2)}, u32[]{:S(2)}) collective-permute-start(bf16[1,4,80,128]{3,2,1,0:T(8,128)(2,1)S(1)} %bitcast.22), channel_id=1, source_target_pairs={{0,8},{1,9},{2,10},{3,11},{4,12},{5,13},{6,14},{7,15},{8,0},{9,1},... | collective-permute-start | bytes 245768 | tf_op jit(solution)/shard_map/ppermute | solution.py:323
  5.8 0.9 %shard_map.111 = (bf16[4,80,128]{2,1,0:T(8,128)(2,1)S(1)}, s32[2,4,4]{2,1,0:T(4,128)S(4)}, s32[2,1,1,16]{3,2,1,0:T(1,128)S(4)}) custom-call(s32[2,4,4]{2,1,0:T(4,128)} %slots_in_ref.3, s32[2,1,1,16]{3,2,1,0:T(1,128)} %bitcast.36, bf16[4,72,128]{2,1,0:T(8,128)(2,1)} %tangent_in_ref.1), custom_call_target="tpu_custom_call" | custom-call | tf_op jit(solution)/shard_map/pallas_call | solution.py:338
  6.7 0.1 collective-permute-start.3
  6.8 1.2 %shard_map.113 = (bf16[512,80]{1,0:T(8,128)(2,1)S(1)}, bf16[80,512]{1,0:T(8,128)(2,1)S(1)}, bf16[512,72]{1,0:T(8,128)(2,1)S(1)}, bf16[512,128]{1,0:T(8,128)(2,1)S(1)}, bf16[72,512]{1,0:T(8,128)(2,1)S(1)}) custom-call(bf16[72,512]{1,0:T(8,128)(2,1)} %bitcast.26, bf16[72,512]{1,0:T(8,128)(2,1)} %w_out_hbm.1, bf16[512,128]{1,0:T(8,128)(2,1)} %bitcast.33, ...), custom_call_target="tpu_custom_call" | custom-call | tf_op jit(solution)/shard_map/pallas_call | solution.py:338
  8.0 2.1 %collective-permute-done = bf16[1,4,80,128]{3,2,1,0:T(8,128)(2,1)S(1)} collective-permute-done((bf16[1,4,80,128]{3,2,1,0:T(8,128)(2,1)S(1)}, bf16[1,4,80,128]{3,2,1,0:T(8,128)(2,1)S(1)}, u32[]{:S(2)}, u32[]{:S(2)}) %collective-permute-start) | collective-permute-done | bytes 81952 | tf_op jit(solution)/shard_map/ppermute | solution.py:323
  10.1 1.9 %collective-permute-start.1 = (bf16[2,4,80,128]{3,2,1,0:T(8,128)(2,1)S(1)}, bf16[2,4,80,128]{3,2,1,0:T(8,128)(2,1)S(1)}, u32[]{:S(2)}, u32[]{:S(2)}) collective-permute-start(bf16[2,4,80,128]{3,2,1,0:T(8,128)(2,1)S(1)} %maximum_bitcast_fusion), channel_id=1, source_target_pairs={{0,2},{1,3},{2,0},{3,1},{4,6},{5,7},{6,4},{7,5},{8,10},{9,11},{10,... | collective-permute-start | bytes 491528 | tf_op jit(solution)/shard_map/ppermute | solution.py:323
  12.0 2.2 %collective-permute-start.2 = (bf16[2,4,80,128]{3,2,1,0:T(8,128)(2,1)S(1)}, bf16[2,4,80,128]{3,2,1,0:T(8,128)(2,1)S(1)}, u32[]{:S(2)}, u32[]{:S(2)}) collective-permute-start(bf16[2,4,80,128]{3,2,1,0:T(8,128)(2,1)S(1)} %maximum_bitcast_fusion), channel_id=1, source_target_pairs={{0,4},{1,5},{2,6},{3,7},{4,0},{5,1},{6,2},{7,3},{8,12},{9,13},{10,... | collective-permute-start | bytes 491528 | tf_op jit(solution)/shard_map/ppermute | solution.py:323
  14.2 0.0 collective-permute-done.3
  14.3 1.2 %collective-permute-done.1 = bf16[2,4,80,128]{3,2,1,0:T(8,128)(2,1)S(1)} collective-permute-done((bf16[2,4,80,128]{3,2,1,0:T(8,128)(2,1)S(1)}, bf16[2,4,80,128]{3,2,1,0:T(8,128)(2,1)S(1)}, u32[]{:S(2)}, u32[]{:S(2)}) %collective-permute-start.1) | collective-permute-done | bytes 163872 | tf_op jit(solution)/shard_map/ppermute | solution.py:323
  15.5 2.6 %collective-permute-done.2 = bf16[2,4,80,128]{3,2,1,0:T(8,128)(2,1)S(1)} collective-permute-done((bf16[2,4,80,128]{3,2,1,0:T(8,128)(2,1)S(1)}, bf16[2,4,80,128]{3,2,1,0:T(8,128)(2,1)S(1)}, u32[]{:S(2)}, u32[]{:S(2)}) %collective-permute-start.2) | collective-permute-done | bytes 163872 | tf_op jit(solution)/shard_map/ppermute | solution.py:323
  18.1 0.7 collective-permute-start.4
  18.8 1.7 %collective-permute-start.5 = (bf16[1,4,80,128]{3,2,1,0:T(8,128)(2,1)S(1)}, bf16[1,4,80,128]{3,2,1,0:T(8,128)(2,1)S(1)}, u32[]{:S(2)}, u32[]{:S(2)}) collective-permute-start(bf16[1,4,80,128]{3,2,1,0:T(8,128)(2,1)S(1)} %slice.13), channel_id=1, source_target_pairs={{0,4},{1,5},{2,6},{3,7},{4,0},{5,1},{6,2},{7,3},{8,12},{9,13},{10,... | collective-permute-start | bytes 245768 | tf_op jit(solution)/shard_map/ppermute | solution.py:323
  20.5 2.1 %collective-permute-done.4 = bf16[1,4,80,128]{3,2,1,0:T(8,128)(2,1)S(1)} collective-permute-done((bf16[1,4,80,128]{3,2,1,0:T(8,128)(2,1)S(1)}, bf16[1,4,80,128]{3,2,1,0:T(8,128)(2,1)S(1)}, u32[]{:S(2)}, u32[]{:S(2)}) %collective-permute-start.4) | collective-permute-done | bytes 81952 | tf_op jit(solution)/shard_map/ppermute | solution.py:323
  22.6 0.6 collective-permute-done.5
  23.2 0.0 copy-start
  23.3 0.1 collective-permute-start.6
  23.3 1.5 %collective-permute-start.12 = (bf16[2,4,80,128]{3,2,1,0:T(8,128)(2,1)S(1)}, bf16[2,4,80,128]{3,2,1,0:T(8,128)(2,1)S(1)}, u32[]{:S(2)}, u32[]{:S(2)}) collective-permute-start(bf16[2,4,80,128]{3,2,1,0:T(8,128)(2,1)S(1)} %maximum_bitcast_fusion.1), channel_id=1, source_target_pairs={{0,2},{1,3},{2,0},{3,1},{4,6},{5,7},{6,4},{7,5},{8,10},{9,11},{10,... | collective-permute-start | bytes 491528 | tf_op jit(solution)/shard_map/ppermute | solution.py:323
  24.8 1.7 %collective-permute-start.13 = (bf16[2,4,80,128]{3,2,1,0:T(8,128)(2,1)S(1)}, bf16[2,4,80,128]{3,2,1,0:T(8,128)(2,1)S(1)}, u32[]{:S(2)}, u32[]{:S(2)}) collective-permute-start(bf16[2,4,80,128]{3,2,1,0:T(8,128)(2,1)S(1)} %maximum_bitcast_fusion.1), channel_id=1, source_target_pairs={{0,4},{1,5},{2,6},{3,7},{4,0},{5,1},{6,2},{7,3},{8,12},{9,13},{10,... | collective-permute-start | bytes 491528 | tf_op jit(solution)/shard_map/ppermute | solution.py:323
  26.6 0.1 constant_dynamic-update-slice_fusion.5
  26.7 5.3 %shard_map.114 = (bf16[16,72,128]{2,1,0:T(8,128)(2,1)}, bf16[80,2560]{1,0:T(8,128)(2,1)S(1)}, bf16[80,512]{1,0:T(8,128)(2,1)S(1)}, s32[20,4]{1,0:T(8,128)S(4)}) custom-call(s32[2,4,4]{2,1,0:T(4,128)S(4)} %get-tuple-element.37.slots_ref, bf16[64,80,128]{2,1,0:T(8,128)(2,1)S(1)} %bitcast.25, bf16[512,128]{1,0:T(8,128)(2,1)S(1)} %get-tuple-element.46.cubic_ref, ...), custom_call_target="tpu_custom_call" | custom-call | flops 679477248 | bytes 2613568 | tf_op jit(solution)/shard_map/pallas_call | solution.py:33
  32.0 5.6 %all-to-all-start = ((bf16[16,72,128]{2,1,0:T(8,128)(2,1)}), bf16[16,72,128]{2,1,0:T(8,128)(2,1)S(1)}, u32[]{:S(2)}, u32[]{:S(2)}) async-start(bf16[16,72,128]{2,1,0:T(8,128)(2,1)} %get-tuple-element.51), calls=%async_computation | async-start | bytes 589824 | tf_op jit(solution)/shard_map/all_to_all | solution.py:320
  37.6 0.0 collective-permute-done.13
  37.6 2.0 %collective-permute-start.14 = (bf16[1,4,80,128]{3,2,1,0:T(8,128)(2,1)S(1)}, bf16[1,4,80,128]{3,2,1,0:T(8,128)(2,1)S(1)}, u32[]{:S(2)}, u32[]{:S(2)}) collective-permute-start(bf16[1,4,80,128]{3,2,1,0:T(8,128)(2,1)S(1)} %slice.14), channel_id=1, source_target_pairs={{0,2},{1,3},{2,0},{3,1},{4,6},{5,7},{6,4},{7,5},{8,10},{9,11},{10,... | collective-permute-start | bytes 245768 | tf_op jit(solution)/shard_map/ppermute | solution.py:323
  39.6 1.5 %collective-permute-start.15 = (bf16[1,4,80,128]{3,2,1,0:T(8,128)(2,1)S(1)}, bf16[1,4,80,128]{3,2,1,0:T(8,128)(2,1)S(1)}, u32[]{:S(2)}, u32[]{:S(2)}) collective-permute-start(bf16[1,4,80,128]{3,2,1,0:T(8,128)(2,1)S(1)} %slice.15), channel_id=1, source_target_pairs={{0,4},{1,5},{2,6},{3,7},{4,0},{5,1},{6,2},{7,3},{8,12},{9,13},{10,... | collective-permute-start | bytes 245768 | tf_op jit(solution)/shard_map/ppermute | solution.py:323
  41.2 3.3 %collective-permute-done.14 = bf16[1,4,80,128]{3,2,1,0:T(8,128)(2,1)S(1)} collective-permute-done((bf16[1,4,80,128]{3,2,1,0:T(8,128)(2,1)S(1)}, bf16[1,4,80,128]{3,2,1,0:T(8,128)(2,1)S(1)}, u32[]{:S(2)}, u32[]{:S(2)}) %collective-permute-start.14) | collective-permute-done | bytes 81952 | tf_op jit(solution)/shard_map/ppermute | solution.py:323
  44.5 2.4 %collective-permute-done.15 = bf16[1,4,80,128]{3,2,1,0:T(8,128)(2,1)S(1)} collective-permute-done((bf16[1,4,80,128]{3,2,1,0:T(8,128)(2,1)S(1)}, bf16[1,4,80,128]{3,2,1,0:T(8,128)(2,1)S(1)}, u32[]{:S(2)}, u32[]{:S(2)}) %collective-permute-start.15) | collective-permute-done | bytes 81952 | tf_op jit(solution)/shard_map/ppermute | solution.py:323
  46.9 0.1 collective-permute-start.16
  47.0 1.2 %shard_map.115 = (f32[72,512]{1,0:T(8,128)S(1)}, f32[72,512]{1,0:T(8,128)S(1)}, bf16[80,512]{1,0:T(8,128)(2,1)S(1)}, bf16[512,512]{1,0:T(8,128)(2,1)S(1)}, bf16[512,512]{1,0:T(8,128)(2,1)S(1)}) custom-call(bf16[72,512]{1,0:T(8,128)(2,1)S(1)} %get-tuple-element.50.lam_two_ref, bf16[512,80]{1,0:T(8,128)(2,1)S(1)} %get-tuple-element.47.w_in_ref, ...), custom_call_target="tpu_custom_call" | custom-call | flops 188743680 | bytes 2146304 | tf_op jit(solution)/shard_map/pallas_call | solution.py:33
  48.2 0.5 all-to-all-done.recv_ref
  48.7 1.5 %shard_map.116 = (bf16[16,72,128]{2,1,0:T(8,128)(2,1)}, bf16[72,512]{1,0:T(8,128)(2,1)S(1)}, bf16[72,512]{1,0:T(8,128)(2,1)S(1)}) custom-call(s32[2,4,4]{2,1,0:T(4,128)S(4)} %get-tuple-element.37.slots_ref, s32[2,1,1,16]{3,2,1,0:T(1,128)S(4)} %get-tuple-element.38.sends_ref, bf16[16,72,128]{2,1,0:T(8,128)(2,1)S(1)} %all-to-all-done.recv_ref, ...), custom_call_target="tpu_custom_call" | custom-call | flops 188743680 | bytes 2441216 | tf_op jit(solution)/shard_map/pallas_call | solution.py:33
  50.1 0.1 collective-permute-start.7
  50.2 1.2 %collective-permute-done.7 = bf16[72,512]{1,0:T(8,128)(2,1)S(1)} collective-permute-done((bf16[72,512]{1,0:T(8,128)(2,1)S(1)}, bf16[72,512]{1,0:T(8,128)(2,1)S(1)}, u32[]{:S(2)}, u32[]{:S(2)}) %collective-permute-start.7) | collective-permute-done | bytes 73760 | tf_op jit(solution)/shard_map/ppermute | solution.py:323
  51.5 2.5 %collective-permute-start.8 = (bf16[72,512]{1,0:T(8,128)(2,1)S(1)}, bf16[72,512]{1,0:T(8,128)(2,1)S(1)}, u32[]{:S(2)}, u32[]{:S(2)}) collective-permute-start(bf16[72,512]{1,0:T(8,128)(2,1)S(1)} %add_convert_fusion.2), channel_id=1, source_target_pairs={{0,8},{1,9},{2,10},{3,11},{4,12},{5,13},{6,14},{7,15},{8,0},{9,1},... | collective-permute-start | bytes 221192 | tf_op jit(solution)/shard_map/ppermute | solution.py:323
  54.0 3.5 %all-to-all-start.1 = ((bf16[16,72,128]{2,1,0:T(8,128)(2,1)}), bf16[16,72,128]{2,1,0:T(8,128)(2,1)S(1)}, u32[]{:S(2)}, u32[]{:S(2)}) async-start(bf16[16,72,128]{2,1,0:T(8,128)(2,1)} %get-tuple-element.61), calls=%async_computation.1 | async-start | bytes 589824 | tf_op jit(solution)/shard_map/all_to_all | solution.py:320
  57.5 0.8 %collective-permute-done.8 = bf16[72,512]{1,0:T(8,128)(2,1)S(1)} collective-permute-done((bf16[72,512]{1,0:T(8,128)(2,1)S(1)}, bf16[72,512]{1,0:T(8,128)(2,1)S(1)}, u32[]{:S(2)}, u32[]{:S(2)}) %collective-permute-start.8) | collective-permute-done | bytes 73760 | tf_op jit(solution)/shard_map/ppermute | solution.py:323
  58.4 1.1 %collective-permute-start.10 = (bf16[72,512]{1,0:T(8,128)(2,1)S(1)}, bf16[72,512]{1,0:T(8,128)(2,1)S(1)}, u32[]{:S(2)}, u32[]{:S(2)}) collective-permute-start(bf16[72,512]{1,0:T(8,128)(2,1)S(1)} %add_convert_fusion.1), channel_id=1, source_target_pairs={{0,4},{1,5},{2,6},{3,7},{4,0},{5,1},{6,2},{7,3},{8,12},{9,13},{10,... | collective-permute-start | bytes 221192 | tf_op jit(solution)/shard_map/ppermute | solution.py:323
  59.5 1.9 %collective-permute-start.11 = (bf16[72,512]{1,0:T(8,128)(2,1)S(1)}, bf16[72,512]{1,0:T(8,128)(2,1)S(1)}, u32[]{:S(2)}, u32[]{:S(2)}) collective-permute-start(bf16[72,512]{1,0:T(8,128)(2,1)S(1)} %add_convert_fusion.1), channel_id=1, source_target_pairs={{0,6},{1,7},{2,4},{3,5},{4,2},{5,3},{6,0},{7,1},{8,14},{9,15},{10,... | collective-permute-start | bytes 221192 | tf_op jit(solution)/shard_map/ppermute | solution.py:323
  61.3 0.6 collective-permute-start.9
  61.9 0.0 collective-permute-done.16
  62.0 1.2 %pad_maximum_fusion = bf16[16,4,80,128]{3,2,1,0:T(8,128)(2,1)S(1)} fusion(bf16[8,4,80,128]{3,2,1,0:T(8,128)(2,1)} %collective-permute-done.16, bf16[8,4,80,128]{3,2,1,0:T(8,128)(2,1)S(1)} %constant_dynamic-update-slice_fusion.7), kind=kLoop, calls=%fused_computation | loop fusion | flops 655360 | bytes 2621440 | tf_op jit(solution)/shard_map/concatenate | solution.py:391
  63.2 3.7 %shard_map.117 = bf16[4,72,128]{2,1,0:T(8,128)(2,1)} custom-call(s32[20,4]{1,0:T(8,128)S(4)} %get-tuple-element.62.route_ref, bf16[64,80,128]{2,1,0:T(8,128)(2,1)S(1)} %bitcast.21, bf16[512,128]{1,0:T(8,128)(2,1)S(1)} %get-tuple-element.46.cubic_ref, bf16[512,80]{1,0:T(8,128)(2,1)S(1)} %get-tuple-element.47.w_in_ref, ...), custom_call_target="tpu_custom_call" | custom-call | flops 754974720 | bytes 2170880 | tf_op jit(solution)/shard_map/pallas_call | solution.py:33
  66.8 0.4 collective-permute-done.10
  67.2 2.2 %collective-permute-done.11 = bf16[72,512]{1,0:T(8,128)(2,1)S(1)} collective-permute-done((bf16[72,512]{1,0:T(8,128)(2,1)S(1)}, bf16[72,512]{1,0:T(8,128)(2,1)S(1)}, u32[]{:S(2)}, u32[]{:S(2)}) %collective-permute-start.11) | collective-permute-done | bytes 73760 | tf_op jit(solution)/shard_map/ppermute | solution.py:323
  69.4 0.1 collective-permute-start.17
  69.5 0.8 %shard_map.118 = f32[4,72,128]{2,1,0:T(8,128)} custom-call(s32[2,1,1,16]{3,2,1,0:T(1,128)S(4)} %get-tuple-element.38.sends_ref, bf16[16,72,128]{2,1,0:T(8,128)(2,1)S(1)} %all-to-all-done.1.recv_ref), custom_call_target="tpu_custom_call" | custom-call | flops 37748736 | bytes 442368 | tf_op jit(solution)/shard_map/pallas_call | solution.py:33
  70.4 0.4 collective-permute-done.17
  70.8 0.7 %select_convert_fusion = (f32[72,512]{1,0:T(8,128)}, f32[512,72]{0,1:T(8,128)}) fusion(bf16[72,512]{1,0:T(8,128)(2,1)S(1)} %collective-permute-done.17, bf16[72,512]{1,0:T(8,128)(2,1)S(1)} %add_convert_fusion, pred[]{:T(512)S(6)} %eq.6), kind=kLoop, calls=%fused_computation.7 | loop fusion | flops 147456 | bytes 442369 | tf_op jit(solution)/shard_map/convert_element_type | solution.py:422
  (24 shorter events, 0.4 us)
Async XLA Ops:
  1.7 8.4 %collective-permute-start = (bf16[1,4,80,128]{3,2,1,0:T(8,128)(2,1)S(1)}, bf16[1,4,80,128]{3,2,1,0:T(8,128)(2,1)S(1)}, u32[]{:S(2)}, u32[]{:S(2)}) collective-permute-start(bf16[1,4,80,128]{3,2,1,0:T(8,128)(2,1)S(1)} %bitcast.22), channel_id=1, source_target_pairs={{0,8},{1,9},{2,10},{3,11},{4,12},{5,13},{6,14},{7,15},{8,0},{9,1},... | collective-permute-start | bytes 245768 | tf_op jit(solution)/shard_map/ppermute | solution.py:323
  6.7 7.5 %collective-permute-start.3 = (bf16[1,4,80,128]{3,2,1,0:T(8,128)(2,1)S(1)}, bf16[1,4,80,128]{3,2,1,0:T(8,128)(2,1)S(1)}, u32[]{:S(2)}, u32[]{:S(2)}) collective-permute-start(bf16[1,4,80,128]{3,2,1,0:T(8,128)(2,1)S(1)} %bitcast.29), channel_id=1, source_target_pairs={{0,8},{1,9},{2,10},{3,11},{4,12},{5,13},{6,14},{7,15},{8,0},{9,1},... | collective-permute-start | bytes 245768 | tf_op jit(solution)/shard_map/ppermute | solution.py:323
  10.1 5.4 %collective-permute-start.1 = (bf16[2,4,80,128]{3,2,1,0:T(8,128)(2,1)S(1)}, bf16[2,4,80,128]{3,2,1,0:T(8,128)(2,1)S(1)}, u32[]{:S(2)}, u32[]{:S(2)}) collective-permute-start(bf16[2,4,80,128]{3,2,1,0:T(8,128)(2,1)S(1)} %maximum_bitcast_fusion), channel_id=1, source_target_pairs={{0,2},{1,3},{2,0},{3,1},{4,6},{5,7},{6,4},{7,5},{8,10},{9,11},{10,... | collective-permute-start | bytes 491528 | tf_op jit(solution)/shard_map/ppermute | solution.py:323
  12.0 6.0 %collective-permute-start.2 = (bf16[2,4,80,128]{3,2,1,0:T(8,128)(2,1)S(1)}, bf16[2,4,80,128]{3,2,1,0:T(8,128)(2,1)S(1)}, u32[]{:S(2)}, u32[]{:S(2)}) collective-permute-start(bf16[2,4,80,128]{3,2,1,0:T(8,128)(2,1)S(1)} %maximum_bitcast_fusion), channel_id=1, source_target_pairs={{0,4},{1,5},{2,6},{3,7},{4,0},{5,1},{6,2},{7,3},{8,12},{9,13},{10,... | collective-permute-start | bytes 491528 | tf_op jit(solution)/shard_map/ppermute | solution.py:323
  18.1 4.5 %collective-permute-start.4 = (bf16[1,4,80,128]{3,2,1,0:T(8,128)(2,1)S(1)}, bf16[1,4,80,128]{3,2,1,0:T(8,128)(2,1)S(1)}, u32[]{:S(2)}, u32[]{:S(2)}) collective-permute-start(bf16[1,4,80,128]{3,2,1,0:T(8,128)(2,1)S(1)} %slice.12), channel_id=1, source_target_pairs={{0,2},{1,3},{2,0},{3,1},{4,6},{5,7},{6,4},{7,5},{8,10},{9,11},{10,... | collective-permute-start | bytes 245768 | tf_op jit(solution)/shard_map/ppermute | solution.py:323
  18.8 4.4 %collective-permute-start.5 = (bf16[1,4,80,128]{3,2,1,0:T(8,128)(2,1)S(1)}, bf16[1,4,80,128]{3,2,1,0:T(8,128)(2,1)S(1)}, u32[]{:S(2)}, u32[]{:S(2)}) collective-permute-start(bf16[1,4,80,128]{3,2,1,0:T(8,128)(2,1)S(1)} %slice.13), channel_id=1, source_target_pairs={{0,4},{1,5},{2,6},{3,7},{4,0},{5,1},{6,2},{7,3},{8,12},{9,13},{10,... | collective-permute-start | bytes 245768 | tf_op jit(solution)/shard_map/ppermute | solution.py:323
  23.2 3.5 %copy-start = (bf16[512,72]{0,1:T(8,128)(2,1)S(1)}, bf16[512,72]{0,1:T(8,128)(2,1)}, u32[]{:S(2)}) copy-start(bf16[512,72]{0,1:T(8,128)(2,1)} %param.12) | copy-start | bytes 221188
  23.3 3.3 %collective-permute-start.6 = (bf16[8,4,80,128]{3,2,1,0:T(8,128)(2,1)S(1)}, bf16[8,4,80,128]{3,2,1,0:T(8,128)(2,1)S(1)}, u32[]{:S(2)}, u32[]{:S(2)}) collective-permute-start(bf16[8,4,80,128]{3,2,1,0:T(8,128)(2,1)S(1)} %constant_dynamic-update-slice_fusion), channel_id=1, source_target_pairs={{0,1},{1,0},{2,3},{3,2},{4,5},{5,4},{6,7},{7,6},{8,9},{9,8},{10,11... | collective-permute-start | bytes 1966088 | tf_op jit(solution)/shard_map/ppermute | solution.py:323
  23.3 14.3 %collective-permute-start.12 = (bf16[2,4,80,128]{3,2,1,0:T(8,128)(2,1)S(1)}, bf16[2,4,80,128]{3,2,1,0:T(8,128)(2,1)S(1)}, u32[]{:S(2)}, u32[]{:S(2)}) collective-permute-start(bf16[2,4,80,128]{3,2,1,0:T(8,128)(2,1)S(1)} %maximum_bitcast_fusion.1), channel_id=1, source_target_pairs={{0,2},{1,3},{2,0},{3,1},{4,6},{5,7},{6,4},{7,5},{8,10},{9,11},{10,... | collective-permute-start | bytes 491528 | tf_op jit(solution)/shard_map/ppermute | solution.py:323
  24.8 12.8 %collective-permute-start.13 = (bf16[2,4,80,128]{3,2,1,0:T(8,128)(2,1)S(1)}, bf16[2,4,80,128]{3,2,1,0:T(8,128)(2,1)S(1)}, u32[]{:S(2)}, u32[]{:S(2)}) collective-permute-start(bf16[2,4,80,128]{3,2,1,0:T(8,128)(2,1)S(1)} %maximum_bitcast_fusion.1), channel_id=1, source_target_pairs={{0,4},{1,5},{2,6},{3,7},{4,0},{5,1},{6,2},{7,3},{8,12},{9,13},{10,... | collective-permute-start | bytes 491528 | tf_op jit(solution)/shard_map/ppermute | solution.py:323
  32.0 16.7 %all-to-all-start = ((bf16[16,72,128]{2,1,0:T(8,128)(2,1)}), bf16[16,72,128]{2,1,0:T(8,128)(2,1)S(1)}, u32[]{:S(2)}, u32[]{:S(2)}) async-start(bf16[16,72,128]{2,1,0:T(8,128)(2,1)} %get-tuple-element.51), calls=%async_computation | async-start | bytes 589824 | tf_op jit(solution)/shard_map/all_to_all | solution.py:320
  37.6 6.8 %collective-permute-start.14 = (bf16[1,4,80,128]{3,2,1,0:T(8,128)(2,1)S(1)}, bf16[1,4,80,128]{3,2,1,0:T(8,128)(2,1)S(1)}, u32[]{:S(2)}, u32[]{:S(2)}) collective-permute-start(bf16[1,4,80,128]{3,2,1,0:T(8,128)(2,1)S(1)} %slice.14), channel_id=1, source_target_pairs={{0,2},{1,3},{2,0},{3,1},{4,6},{5,7},{6,4},{7,5},{8,10},{9,11},{10,... | collective-permute-start | bytes 245768 | tf_op jit(solution)/shard_map/ppermute | solution.py:323
  39.6 7.2 %collective-permute-start.15 = (bf16[1,4,80,128]{3,2,1,0:T(8,128)(2,1)S(1)}, bf16[1,4,80,128]{3,2,1,0:T(8,128)(2,1)S(1)}, u32[]{:S(2)}, u32[]{:S(2)}) collective-permute-start(bf16[1,4,80,128]{3,2,1,0:T(8,128)(2,1)S(1)} %slice.15), channel_id=1, source_target_pairs={{0,4},{1,5},{2,6},{3,7},{4,0},{5,1},{6,2},{7,3},{8,12},{9,13},{10,... | collective-permute-start | bytes 245768 | tf_op jit(solution)/shard_map/ppermute | solution.py:323
  46.9 15.0 %collective-permute-start.16 = (bf16[8,4,80,128]{3,2,1,0:T(8,128)(2,1)S(1)}, bf16[8,4,80,128]{3,2,1,0:T(8,128)(2,1)}, u32[]{:S(2)}, u32[]{:S(2)}) collective-permute-start(bf16[8,4,80,128]{3,2,1,0:T(8,128)(2,1)S(1)} %constant_dynamic-update-slice_fusion.7), channel_id=1, source_target_pairs={{0,1},{1,0},{2,3},{3,2},{4,5},{5,4},{6,7},{7,6},{8,9},{9,8},{10,11... | collective-permute-start | bytes 1966088 | tf_op jit(solution)/shard_map/ppermute | solution.py:323
  50.1 1.3 %collective-permute-start.7 = (bf16[72,512]{1,0:T(8,128)(2,1)S(1)}, bf16[72,512]{1,0:T(8,128)(2,1)S(1)}, u32[]{:S(2)}, u32[]{:S(2)}) collective-permute-start(bf16[72,512]{1,0:T(8,128)(2,1)S(1)} %get-tuple-element.60), channel_id=1, source_target_pairs={{0,1},{1,0},{2,3},{3,2},{4,5},{5,4},{6,7},{7,6},{8,9},{9,8},{10,11... | collective-permute-start | bytes 221192 | tf_op jit(solution)/shard_map/ppermute | solution.py:323
  51.5 6.9 %collective-permute-start.8 = (bf16[72,512]{1,0:T(8,128)(2,1)S(1)}, bf16[72,512]{1,0:T(8,128)(2,1)S(1)}, u32[]{:S(2)}, u32[]{:S(2)}) collective-permute-start(bf16[72,512]{1,0:T(8,128)(2,1)S(1)} %add_convert_fusion.2), channel_id=1, source_target_pairs={{0,8},{1,9},{2,10},{3,11},{4,12},{5,13},{6,14},{7,15},{8,0},{9,1},... | collective-permute-start | bytes 221192 | tf_op jit(solution)/shard_map/ppermute | solution.py:323
  54.0 15.4 %all-to-all-start.1 = ((bf16[16,72,128]{2,1,0:T(8,128)(2,1)}), bf16[16,72,128]{2,1,0:T(8,128)(2,1)S(1)}, u32[]{:S(2)}, u32[]{:S(2)}) async-start(bf16[16,72,128]{2,1,0:T(8,128)(2,1)} %get-tuple-element.61), calls=%async_computation.1 | async-start | bytes 589824 | tf_op jit(solution)/shard_map/all_to_all | solution.py:320
  58.4 8.8 %collective-permute-start.10 = (bf16[72,512]{1,0:T(8,128)(2,1)S(1)}, bf16[72,512]{1,0:T(8,128)(2,1)S(1)}, u32[]{:S(2)}, u32[]{:S(2)}) collective-permute-start(bf16[72,512]{1,0:T(8,128)(2,1)S(1)} %add_convert_fusion.1), channel_id=1, source_target_pairs={{0,4},{1,5},{2,6},{3,7},{4,0},{5,1},{6,2},{7,3},{8,12},{9,13},{10,... | collective-permute-start | bytes 221192 | tf_op jit(solution)/shard_map/ppermute | solution.py:323
  59.5 9.9 %collective-permute-start.11 = (bf16[72,512]{1,0:T(8,128)(2,1)S(1)}, bf16[72,512]{1,0:T(8,128)(2,1)S(1)}, u32[]{:S(2)}, u32[]{:S(2)}) collective-permute-start(bf16[72,512]{1,0:T(8,128)(2,1)S(1)} %add_convert_fusion.1), channel_id=1, source_target_pairs={{0,6},{1,7},{2,4},{3,5},{4,2},{5,3},{6,0},{7,1},{8,14},{9,15},{10,... | collective-permute-start | bytes 221192 | tf_op jit(solution)/shard_map/ppermute | solution.py:323
  61.3 8.1 %collective-permute-start.9 = (bf16[72,512]{1,0:T(8,128)(2,1)S(1)}, bf16[72,512]{1,0:T(8,128)(2,1)S(1)}, u32[]{:S(2)}, u32[]{:S(2)}) collective-permute-start(bf16[72,512]{1,0:T(8,128)(2,1)S(1)} %add_convert_fusion.1), channel_id=1, source_target_pairs={{0,2},{1,3},{2,0},{3,1},{4,6},{5,7},{6,4},{7,5},{8,10},{9,11},{10,... | collective-permute-start | bytes 221192 | tf_op jit(solution)/shard_map/ppermute | solution.py:323
  69.4 1.3 %collective-permute-start.17 = (bf16[72,512]{1,0:T(8,128)(2,1)S(1)}, bf16[72,512]{1,0:T(8,128)(2,1)S(1)}, u32[]{:S(2)}, u32[]{:S(2)}) collective-permute-start(bf16[72,512]{1,0:T(8,128)(2,1)S(1)} %add_convert_fusion), channel_id=1, source_target_pairs={{0,1},{1,0},{2,3},{3,2},{4,5},{5,4},{6,7},{7,6},{8,9},{9,8},{10,11... | collective-permute-start | bytes 221192 | tf_op jit(solution)/shard_map/ppermute | solution.py:323

commit v6 on v5

--- a/solution.py
+++ b/solution.py
@@ -388,7 +388,8 @@
     )
     recv_three = exchange(send)
     _, tangents = tie((send, tangents))
-    tangents = jnp.concatenate([tangents, swap(tangents, 1)], axis=0).reshape(-1, tall, columns)
+    tangents = jnp.concatenate([tangents, swap(tangents[: peers // 4], 1), swap(tangents[peers // 4 :], 1)], axis=0)
+    tangents = tangents.reshape(-1, tall, columns)
     part_in, part_out, adv_one, hidden_one, slope_one = call(
         between_kernel,
         [shape((channels, hid), F32)] * 2 + [shape((tall, wide))] + [shape((hid, wide))] * 2,

time: 72 us -> 70.6 us (0.981)
  local copies, waits for them, and re-layouts: 0.32 us -> 2.21 us
  waiting for transfers between devices: 19.8 us -> 18.4 us
  other arithmetic: 2.07 us -> 1.02 us
  starting transfers between devices: 32.8 us -> 31.9 us
    ppermute x18 -> x19, waiting for transfers between devices: 19.3 us -> 16.6 us  [swap(): return lax.ppermute(values, 'lat', [(i, i ^ step) for i in range(peers)])]
    unnamed x9 -> x13, local copies, waits for them, and re-layouts: 0.18 us -> 2.02 us
    all_to_all x2, waiting for transfers between devices: 0.49 us -> 1.76 us  [exchange(): lax.all_to_all(packed, 'lat', split_axis=0, concat_axis=0, tiled=True)]
    concatenate x1, other arithmetic: 1.2 us -> 0.15 us  [shards(): jnp.concatenate([tangents, swap(tangents[:peers // 4], 1), swap(tangents[...]
    ppermute x18 -> x19, starting transfers between devices: 23.7 us -> 22.8 us  [swap(): return lax.ppermute(values, 'lat', [(i, i ^ step) for i in range(peers)])]
  transfers between devices with their start and end apart: 20 -> 21, of which waited for: 13 -> 13; matrix products, arithmetic and copies ran while one was open for 2% -> 3% of each run, Pallas kernels for 20% -> 19%
where the time goes in v6:
time: 70.6 us; the launch traced here: 70.1 us
  starting transfers between devices  31.9 us (45%)
  waiting for transfers between devices  18.4 us (26%)
  Pallas kernels  15.6 us (22%)
  local copies, waits for them, and re-layouts  2.21 us (3%)
  other arithmetic  1.02 us (1%)
  between operations  0.91 us (1%)
    ppermute x19, starting transfers between devices, swap(): return lax.ppermute(values, 'lat', [(i, i ^ step) for i in range(peers)])  22.8 us
    ppermute x19, waiting for transfers between devices, swap(): return lax.ppermute(values, 'lat', [(i, i ^ step) for i in range(peers)])  16.6 us
    pallas_call x5, Pallas kernels, call(): pl.pallas_call(kernel, out_shape=tuple((o.memory_space(o.shape, o.dtype)...  12.5 us
    all_to_all x2, starting transfers between devices, exchange(): lax.all_to_all(packed, 'lat', split_axis=0, concat_axis=0, tiled=True)  9.12 us
    pallas_call x3, Pallas kernels, load(): pl.pallas_call(kernel, out_shape=out_shape, in_specs=[pl.BlockSpec(memory...  3.15 us
    unnamed x13, local copies, waits for them, and re-layouts  2.02 us
    all_to_all x2, waiting for transfers between devices, exchange(): lax.all_to_all(packed, 'lat', split_axis=0, concat_axis=0, tiled=True)  1.76 us
  transfers between devices with their start and end apart: 21, of which 13 were waited for; matrix products, arithmetic and copies ran while one was open for 3% of the time, Pallas kernels for 19%

profile of v6, /device:TPU:0, one launch (start us, length us, event | category | flops | bytes accessed | tf_op | source)
XLA Modules:
  0.0 70.1 jit_solution(13676878639453200211)
XLA Ops:
  0.6 1.0 %shard_map.112 = bf16[4,80,128]{2,1,0:T(8,128)(2,1)S(1)} custom-call(s32[2,4,4]{2,1,0:T(4,128)} %slots_in_ref.3, s32[2,1,1,16]{3,2,1,0:T(1,128)} %bitcast.35, bf16[4,72,128]{2,1,0:T(8,128)(2,1)} %state_in_ref.1), custom_call_target="tpu_custom_call" | custom-call | tf_op jit(solution)/shard_map/pallas_call | solution.py:338
  1.7 4.1 %collective-permute-start = (bf16[1,4,80,128]{3,2,1,0:T(8,128)(2,1)S(1)}, bf16[1,4,80,128]{3,2,1,0:T(8,128)(2,1)S(1)}, u32[]{:S(2)}, u32[]{:S(2)}) collective-permute-start(bf16[1,4,80,128]{3,2,1,0:T(8,128)(2,1)S(1)} %bitcast.22), channel_id=1, source_target_pairs={{0,8},{1,9},{2,10},{3,11},{4,12},{5,13},{6,14},{7,15},{8,0},{9,1},... | collective-permute-start | bytes 245768 | tf_op jit(solution)/shard_map/ppermute | solution.py:323
  5.8 0.9 %shard_map.111 = (bf16[4,80,128]{2,1,0:T(8,128)(2,1)S(1)}, s32[2,4,4]{2,1,0:T(4,128)S(4)}, s32[2,1,1,16]{3,2,1,0:T(1,128)S(4)}) custom-call(s32[2,4,4]{2,1,0:T(4,128)} %slots_in_ref.3, s32[2,1,1,16]{3,2,1,0:T(1,128)} %bitcast.36, bf16[4,72,128]{2,1,0:T(8,128)(2,1)} %tangent_in_ref.1), custom_call_target="tpu_custom_call" | custom-call | tf_op jit(solution)/shard_map/pallas_call | solution.py:338
  6.7 0.1 collective-permute-start.3
  6.8 1.2 %shard_map.113 = (bf16[512,80]{1,0:T(8,128)(2,1)S(1)}, bf16[80,512]{1,0:T(8,128)(2,1)S(1)}, bf16[512,72]{1,0:T(8,128)(2,1)S(1)}, bf16[512,128]{1,0:T(8,128)(2,1)S(1)}, bf16[72,512]{1,0:T(8,128)(2,1)S(1)}) custom-call(bf16[72,512]{1,0:T(8,128)(2,1)} %bitcast.26, bf16[72,512]{1,0:T(8,128)(2,1)} %w_out_hbm.1, bf16[512,128]{1,0:T(8,128)(2,1)} %bitcast.33, ...), custom_call_target="tpu_custom_call" | custom-call | tf_op jit(solution)/shard_map/pallas_call | solution.py:338
  8.0 2.1 %collective-permute-done = bf16[1,4,80,128]{3,2,1,0:T(8,128)(2,1)S(1)} collective-permute-done((bf16[1,4,80,128]{3,2,1,0:T(8,128)(2,1)S(1)}, bf16[1,4,80,128]{3,2,1,0:T(8,128)(2,1)S(1)}, u32[]{:S(2)}, u32[]{:S(2)}) %collective-permute-start) | collective-permute-done | bytes 81952 | tf_op jit(solution)/shard_map/ppermute | solution.py:323
  10.1 1.9 %collective-permute-start.1 = (bf16[2,4,80,128]{3,2,1,0:T(8,128)(2,1)S(1)}, bf16[2,4,80,128]{3,2,1,0:T(8,128)(2,1)S(1)}, u32[]{:S(2)}, u32[]{:S(2)}) collective-permute-start(bf16[2,4,80,128]{3,2,1,0:T(8,128)(2,1)S(1)} %maximum_bitcast_fusion), channel_id=1, source_target_pairs={{0,2},{1,3},{2,0},{3,1},{4,6},{5,7},{6,4},{7,5},{8,10},{9,11},{10,... | collective-permute-start | bytes 491528 | tf_op jit(solution)/shard_map/ppermute | solution.py:323
  12.0 2.2 %collective-permute-start.2 = (bf16[2,4,80,128]{3,2,1,0:T(8,128)(2,1)S(1)}, bf16[2,4,80,128]{3,2,1,0:T(8,128)(2,1)S(1)}, u32[]{:S(2)}, u32[]{:S(2)}) collective-permute-start(bf16[2,4,80,128]{3,2,1,0:T(8,128)(2,1)S(1)} %maximum_bitcast_fusion), channel_id=1, source_target_pairs={{0,4},{1,5},{2,6},{3,7},{4,0},{5,1},{6,2},{7,3},{8,12},{9,13},{10,... | collective-permute-start | bytes 491528 | tf_op jit(solution)/shard_map/ppermute | solution.py:323
  14.3 1.2 %collective-permute-done.1 = bf16[2,4,80,128]{3,2,1,0:T(8,128)(2,1)S(1)} collective-permute-done((bf16[2,4,80,128]{3,2,1,0:T(8,128)(2,1)S(1)}, bf16[2,4,80,128]{3,2,1,0:T(8,128)(2,1)S(1)}, u32[]{:S(2)}, u32[]{:S(2)}) %collective-permute-start.1) | collective-permute-done | bytes 163872 | tf_op jit(solution)/shard_map/ppermute | solution.py:323
  15.5 2.6 %collective-permute-done.2 = bf16[2,4,80,128]{3,2,1,0:T(8,128)(2,1)S(1)} collective-permute-done((bf16[2,4,80,128]{3,2,1,0:T(8,128)(2,1)S(1)}, bf16[2,4,80,128]{3,2,1,0:T(8,128)(2,1)S(1)}, u32[]{:S(2)}, u32[]{:S(2)}) %collective-permute-start.2) | collective-permute-done | bytes 163872 | tf_op jit(solution)/shard_map/ppermute | solution.py:323
  18.1 0.7 collective-permute-start.4
  18.8 1.7 %collective-permute-start.5 = (bf16[1,4,80,128]{3,2,1,0:T(8,128)(2,1)S(1)}, bf16[1,4,80,128]{3,2,1,0:T(8,128)(2,1)S(1)}, u32[]{:S(2)}, u32[]{:S(2)}) collective-permute-start(bf16[1,4,80,128]{3,2,1,0:T(8,128)(2,1)S(1)} %slice.19), channel_id=1, source_target_pairs={{0,4},{1,5},{2,6},{3,7},{4,0},{5,1},{6,2},{7,3},{8,12},{9,13},{10,... | collective-permute-start | bytes 245768 | tf_op jit(solution)/shard_map/ppermute | solution.py:323
  20.5 2.1 %collective-permute-done.4 = bf16[1,4,80,128]{3,2,1,0:T(8,128)(2,1)S(1)} collective-permute-done((bf16[1,4,80,128]{3,2,1,0:T(8,128)(2,1)S(1)}, bf16[1,4,80,128]{3,2,1,0:T(8,128)(2,1)S(1)}, u32[]{:S(2)}, u32[]{:S(2)}) %collective-permute-start.4) | collective-permute-done | bytes 81952 | tf_op jit(solution)/shard_map/ppermute | solution.py:323
  22.6 0.6 collective-permute-done.5
  23.2 0.0 copy-start
  23.3 0.1 collective-permute-start.6
  23.3 1.5 %collective-permute-start.12 = (bf16[2,4,80,128]{3,2,1,0:T(8,128)(2,1)S(1)}, bf16[2,4,80,128]{3,2,1,0:T(8,128)(2,1)S(1)}, u32[]{:S(2)}, u32[]{:S(2)}) collective-permute-start(bf16[2,4,80,128]{3,2,1,0:T(8,128)(2,1)S(1)} %maximum_bitcast_fusion.1), channel_id=1, source_target_pairs={{0,2},{1,3},{2,0},{3,1},{4,6},{5,7},{6,4},{7,5},{8,10},{9,11},{10,... | collective-permute-start | bytes 491528 | tf_op jit(solution)/shard_map/ppermute | solution.py:323
  24.8 1.7 %collective-permute-start.13 = (bf16[2,4,80,128]{3,2,1,0:T(8,128)(2,1)S(1)}, bf16[2,4,80,128]{3,2,1,0:T(8,128)(2,1)S(1)}, u32[]{:S(2)}, u32[]{:S(2)}) collective-permute-start(bf16[2,4,80,128]{3,2,1,0:T(8,128)(2,1)S(1)} %maximum_bitcast_fusion.1), channel_id=1, source_target_pairs={{0,4},{1,5},{2,6},{3,7},{4,0},{5,1},{6,2},{7,3},{8,12},{9,13},{10,... | collective-permute-start | bytes 491528 | tf_op jit(solution)/shard_map/ppermute | solution.py:323
  26.6 0.1 constant_dynamic-update-slice_fusion.5
  26.7 5.3 %shard_map.114 = (bf16[16,72,128]{2,1,0:T(8,128)(2,1)}, bf16[80,2560]{1,0:T(8,128)(2,1)S(1)}, bf16[80,512]{1,0:T(8,128)(2,1)S(1)}, s32[20,4]{1,0:T(8,128)S(4)}) custom-call(s32[2,4,4]{2,1,0:T(4,128)S(4)} %get-tuple-element.37.slots_ref, bf16[64,80,128]{2,1,0:T(8,128)(2,1)S(1)} %bitcast.25, bf16[512,128]{1,0:T(8,128)(2,1)S(1)} %get-tuple-element.46.cubic_ref, ...), custom_call_target="tpu_custom_call" | custom-call | flops 679477248 | bytes 2613568 | tf_op jit(solution)/shard_map/pallas_call | solution.py:33
  32.0 5.6 %all-to-all-start = ((bf16[16,72,128]{2,1,0:T(8,128)(2,1)}), bf16[16,72,128]{2,1,0:T(8,128)(2,1)S(1)}, u32[]{:S(2)}, u32[]{:S(2)}) async-start(bf16[16,72,128]{2,1,0:T(8,128)(2,1)} %get-tuple-element.51), calls=%async_computation | async-start | bytes 589824 | tf_op jit(solution)/shard_map/all_to_all | solution.py:320
  37.7 2.0 %collective-permute-start.14 = (bf16[1,4,80,128]{3,2,1,0:T(8,128)(2,1)S(1)}, bf16[1,4,80,128]{3,2,1,0:T(8,128)(2,1)S(1)}, u32[]{:S(2)}, u32[]{:S(2)}) collective-permute-start(bf16[1,4,80,128]{3,2,1,0:T(8,128)(2,1)S(1)} %slice.20), channel_id=1, source_target_pairs={{0,2},{1,3},{2,0},{3,1},{4,6},{5,7},{6,4},{7,5},{8,10},{9,11},{10,... | collective-permute-start | bytes 245768 | tf_op jit(solution)/shard_map/ppermute | solution.py:323
  39.7 1.5 %collective-permute-start.15 = (bf16[1,4,80,128]{3,2,1,0:T(8,128)(2,1)S(1)}, bf16[1,4,80,128]{3,2,1,0:T(8,128)(2,1)S(1)}, u32[]{:S(2)}, u32[]{:S(2)}) collective-permute-start(bf16[1,4,80,128]{3,2,1,0:T(8,128)(2,1)S(1)} %slice.21), channel_id=1, source_target_pairs={{0,4},{1,5},{2,6},{3,7},{4,0},{5,1},{6,2},{7,3},{8,12},{9,13},{10,... | collective-permute-start | bytes 245768 | tf_op jit(solution)/shard_map/ppermute | solution.py:323
  41.1 1.2 %shard_map.115 = (f32[72,512]{1,0:T(8,128)S(1)}, f32[72,512]{1,0:T(8,128)S(1)}, bf16[80,512]{1,0:T(8,128)(2,1)S(1)}, bf16[512,512]{1,0:T(8,128)(2,1)S(1)}, bf16[512,512]{1,0:T(8,128)(2,1)S(1)}) custom-call(bf16[72,512]{1,0:T(8,128)(2,1)S(1)} %get-tuple-element.50.lam_two_ref, bf16[512,80]{1,0:T(8,128)(2,1)S(1)} %get-tuple-element.47.w_in_ref, ...), custom_call_target="tpu_custom_call" | custom-call | flops 188743680 | bytes 2146304 | tf_op jit(solution)/shard_map/pallas_call | solution.py:33
  42.3 0.9 %constant_dynamic-update-slice_fusion.10 = bf16[8,4,80,128]{3,2,1,0:T(8,128)(2,1)S(1)} fusion(bf16[8,4,80,128]{3,2,1,0:T(8,128)(2,1)S(1)} %get-tuple-element.75, bf16[2,4,80,128]{3,2,1,0:T(8,128)(2,1)} %copy-done.1), kind=kLoop, calls=%fused_computation.18 | loop fusion | bytes 327680
  43.3 0.9 %constant_dynamic-update-slice_fusion.9 = bf16[8,4,80,128]{3,2,1,0:T(8,128)(2,1)S(1)} fusion(bf16[8,4,80,128]{3,2,1,0:T(8,128)(2,1)S(1)} %constant_dynamic-update-slice_fusion.10, bf16[2,4,80,128]{3,2,1,0:T(8,128)(2,1)} %copy-done.2), kind=kLoop, calls=%fused_computation.17 | loop fusion | bytes 327680
  44.2 0.3 collective-permute-done.14
  44.5 2.4 %collective-permute-done.15 = bf16[1,4,80,128]{3,2,1,0:T(8,128)(2,1)S(1)} collective-permute-done((bf16[1,4,80,128]{3,2,1,0:T(8,128)(2,1)S(1)}, bf16[1,4,80,128]{3,2,1,0:T(8,128)(2,1)S(1)}, u32[]{:S(2)}, u32[]{:S(2)}) %collective-permute-start.15) | collective-permute-done | bytes 81952 | tf_op jit(solution)/shard_map/ppermute | solution.py:323
  46.9 1.8 %all-to-all-done.recv_ref = bf16[16,72,128]{2,1,0:T(8,128)(2,1)S(1)} async-done(((bf16[16,72,128]{2,1,0:T(8,128)(2,1)}), bf16[16,72,128]{2,1,0:T(8,128)(2,1)S(1)}, u32[]{:S(2)}, u32[]{:S(2)}) %all-to-all-start) | async-done | bytes 294944 | tf_op jit(solution)/shard_map/all_to_all | solution.py:320
  48.7 1.5 %shard_map.116 = (bf16[16,72,128]{2,1,0:T(8,128)(2,1)}, bf16[72,512]{1,0:T(8,128)(2,1)S(1)}, bf16[72,512]{1,0:T(8,128)(2,1)S(1)}) custom-call(s32[2,4,4]{2,1,0:T(4,128)S(4)} %get-tuple-element.37.slots_ref, s32[2,1,1,16]{3,2,1,0:T(1,128)S(4)} %get-tuple-element.38.sends_ref, bf16[16,72,128]{2,1,0:T(8,128)(2,1)S(1)} %all-to-all-done.recv_ref, ...), custom_call_target="tpu_custom_call" | custom-call | flops 188743680 | bytes 2441216 | tf_op jit(solution)/shard_map/pallas_call | solution.py:33
  50.1 0.1 collective-permute-start.7
  50.3 0.6 collective-permute-start.16
  50.8 0.1 collective-permute-start.17
  50.9 0.6 collective-permute-done.7
  51.5 1.1 %collective-permute-start.8 = (bf16[72,512]{1,0:T(8,128)(2,1)S(1)}, bf16[72,512]{1,0:T(8,128)(2,1)S(1)}, u32[]{:S(2)}, u32[]{:S(2)}) collective-permute-start(bf16[72,512]{1,0:T(8,128)(2,1)S(1)} %add_convert_fusion.2), channel_id=1, source_target_pairs={{0,8},{1,9},{2,10},{3,11},{4,12},{5,13},{6,14},{7,15},{8,0},{9,1},... | collective-permute-start | bytes 221192 | tf_op jit(solution)/shard_map/ppermute | solution.py:323
  52.6 3.5 %all-to-all-start.1 = ((bf16[16,72,128]{2,1,0:T(8,128)(2,1)}), bf16[16,72,128]{2,1,0:T(8,128)(2,1)S(1)}, u32[]{:S(2)}, u32[]{:S(2)}) async-start(bf16[16,72,128]{2,1,0:T(8,128)(2,1)} %get-tuple-element.61), calls=%async_computation.1 | async-start | bytes 589824 | tf_op jit(solution)/shard_map/all_to_all | solution.py:320
  56.1 1.9 %collective-permute-done.8 = bf16[72,512]{1,0:T(8,128)(2,1)S(1)} collective-permute-done((bf16[72,512]{1,0:T(8,128)(2,1)S(1)}, bf16[72,512]{1,0:T(8,128)(2,1)S(1)}, u32[]{:S(2)}, u32[]{:S(2)}) %collective-permute-start.8) | collective-permute-done | bytes 73760 | tf_op jit(solution)/shard_map/ppermute | solution.py:323
  58.1 0.1 collective-permute-start.10
  58.1 1.8 %collective-permute-start.11 = (bf16[72,512]{1,0:T(8,128)(2,1)S(1)}, bf16[72,512]{1,0:T(8,128)(2,1)S(1)}, u32[]{:S(2)}, u32[]{:S(2)}) collective-permute-start(bf16[72,512]{1,0:T(8,128)(2,1)S(1)} %add_convert_fusion.1), channel_id=1, source_target_pairs={{0,6},{1,7},{2,4},{3,5},{4,2},{5,3},{6,0},{7,1},{8,14},{9,15},{10,... | collective-permute-start | bytes 221192 | tf_op jit(solution)/shard_map/ppermute | solution.py:323
  60.0 1.6 %collective-permute-start.9 = (bf16[72,512]{1,0:T(8,128)(2,1)S(1)}, bf16[72,512]{1,0:T(8,128)(2,1)S(1)}, u32[]{:S(2)}, u32[]{:S(2)}) collective-permute-start(bf16[72,512]{1,0:T(8,128)(2,1)S(1)} %add_convert_fusion.1), channel_id=1, source_target_pairs={{0,2},{1,3},{2,0},{3,1},{4,6},{5,7},{6,4},{7,5},{8,10},{9,11},{10,... | collective-permute-start | bytes 221192 | tf_op jit(solution)/shard_map/ppermute | solution.py:323
  61.6 0.1 pad_maximum_fusion
  61.8 3.7 %shard_map.117 = bf16[4,72,128]{2,1,0:T(8,128)(2,1)} custom-call(s32[20,4]{1,0:T(8,128)S(4)} %get-tuple-element.62.route_ref, bf16[64,80,128]{2,1,0:T(8,128)(2,1)S(1)} %bitcast.21, bf16[512,128]{1,0:T(8,128)(2,1)S(1)} %get-tuple-element.46.cubic_ref, bf16[512,80]{1,0:T(8,128)(2,1)S(1)} %get-tuple-element.47.w_in_ref, ...), custom_call_target="tpu_custom_call" | custom-call | flops 754974720 | bytes 2170880 | tf_op jit(solution)/shard_map/pallas_call | solution.py:33
  65.5 0.3 collective-permute-done.10
  65.8 2.2 %collective-permute-done.11 = bf16[72,512]{1,0:T(8,128)(2,1)S(1)} collective-permute-done((bf16[72,512]{1,0:T(8,128)(2,1)S(1)}, bf16[72,512]{1,0:T(8,128)(2,1)S(1)}, u32[]{:S(2)}, u32[]{:S(2)}) %collective-permute-start.11) | collective-permute-done | bytes 73760 | tf_op jit(solution)/shard_map/ppermute | solution.py:323
  68.0 0.1 collective-permute-start.18
  68.1 0.8 %shard_map.118 = f32[4,72,128]{2,1,0:T(8,128)} custom-call(s32[2,1,1,16]{3,2,1,0:T(1,128)S(4)} %get-tuple-element.38.sends_ref, bf16[16,72,128]{2,1,0:T(8,128)(2,1)S(1)} %all-to-all-done.1.recv_ref), custom_call_target="tpu_custom_call" | custom-call | flops 37748736 | bytes 442368 | tf_op jit(solution)/shard_map/pallas_call | solution.py:33
  69.0 0.4 collective-permute-done.18
  69.4 0.7 %select_convert_fusion = (f32[72,512]{1,0:T(8,128)}, f32[512,72]{0,1:T(8,128)}) fusion(bf16[72,512]{1,0:T(8,128)(2,1)S(1)} %collective-permute-done.18, bf16[72,512]{1,0:T(8,128)(2,1)S(1)} %add_convert_fusion, pred[]{:T(512)S(6)} %eq.6), kind=kLoop, calls=%fused_computation.7 | loop fusion | flops 147456 | bytes 442369 | tf_op jit(solution)/shard_map/convert_element_type | solution.py:423
  (31 shorter events, 0.4 us)
Async XLA Ops:
  1.7 8.4 %collective-permute-start = (bf16[1,4,80,128]{3,2,1,0:T(8,128)(2,1)S(1)}, bf16[1,4,80,128]{3,2,1,0:T(8,128)(2,1)S(1)}, u32[]{:S(2)}, u32[]{:S(2)}) collective-permute-start(bf16[1,4,80,128]{3,2,1,0:T(8,128)(2,1)S(1)} %bitcast.22), channel_id=1, source_target_pairs={{0,8},{1,9},{2,10},{3,11},{4,12},{5,13},{6,14},{7,15},{8,0},{9,1},... | collective-permute-start | bytes 245768 | tf_op jit(solution)/shard_map/ppermute | solution.py:323
  6.7 7.5 %collective-permute-start.3 = (bf16[1,4,80,128]{3,2,1,0:T(8,128)(2,1)S(1)}, bf16[1,4,80,128]{3,2,1,0:T(8,128)(2,1)S(1)}, u32[]{:S(2)}, u32[]{:S(2)}) collective-permute-start(bf16[1,4,80,128]{3,2,1,0:T(8,128)(2,1)S(1)} %bitcast.29), channel_id=1, source_target_pairs={{0,8},{1,9},{2,10},{3,11},{4,12},{5,13},{6,14},{7,15},{8,0},{9,1},... | collective-permute-start | bytes 245768 | tf_op jit(solution)/shard_map/ppermute | solution.py:323
  10.1 5.4 %collective-permute-start.1 = (bf16[2,4,80,128]{3,2,1,0:T(8,128)(2,1)S(1)}, bf16[2,4,80,128]{3,2,1,0:T(8,128)(2,1)S(1)}, u32[]{:S(2)}, u32[]{:S(2)}) collective-permute-start(bf16[2,4,80,128]{3,2,1,0:T(8,128)(2,1)S(1)} %maximum_bitcast_fusion), channel_id=1, source_target_pairs={{0,2},{1,3},{2,0},{3,1},{4,6},{5,7},{6,4},{7,5},{8,10},{9,11},{10,... | collective-permute-start | bytes 491528 | tf_op jit(solution)/shard_map/ppermute | solution.py:323
  12.0 6.0 %collective-permute-start.2 = (bf16[2,4,80,128]{3,2,1,0:T(8,128)(2,1)S(1)}, bf16[2,4,80,128]{3,2,1,0:T(8,128)(2,1)S(1)}, u32[]{:S(2)}, u32[]{:S(2)}) collective-permute-start(bf16[2,4,80,128]{3,2,1,0:T(8,128)(2,1)S(1)} %maximum_bitcast_fusion), channel_id=1, source_target_pairs={{0,4},{1,5},{2,6},{3,7},{4,0},{5,1},{6,2},{7,3},{8,12},{9,13},{10,... | collective-permute-start | bytes 491528 | tf_op jit(solution)/shard_map/ppermute | solution.py:323
  18.1 4.5 %collective-permute-start.4 = (bf16[1,4,80,128]{3,2,1,0:T(8,128)(2,1)S(1)}, bf16[1,4,80,128]{3,2,1,0:T(8,128)(2,1)S(1)}, u32[]{:S(2)}, u32[]{:S(2)}) collective-permute-start(bf16[1,4,80,128]{3,2,1,0:T(8,128)(2,1)S(1)} %slice.18), channel_id=1, source_target_pairs={{0,2},{1,3},{2,0},{3,1},{4,6},{5,7},{6,4},{7,5},{8,10},{9,11},{10,... | collective-permute-start | bytes 245768 | tf_op jit(solution)/shard_map/ppermute | solution.py:323
  18.8 4.4 %collective-permute-start.5 = (bf16[1,4,80,128]{3,2,1,0:T(8,128)(2,1)S(1)}, bf16[1,4,80,128]{3,2,1,0:T(8,128)(2,1)S(1)}, u32[]{:S(2)}, u32[]{:S(2)}) collective-permute-start(bf16[1,4,80,128]{3,2,1,0:T(8,128)(2,1)S(1)} %slice.19), channel_id=1, source_target_pairs={{0,4},{1,5},{2,6},{3,7},{4,0},{5,1},{6,2},{7,3},{8,12},{9,13},{10,... | collective-permute-start | bytes 245768 | tf_op jit(solution)/shard_map/ppermute | solution.py:323
  23.2 3.5 %copy-start = (bf16[512,72]{0,1:T(8,128)(2,1)S(1)}, bf16[512,72]{0,1:T(8,128)(2,1)}, u32[]{:S(2)}) copy-start(bf16[512,72]{0,1:T(8,128)(2,1)} %param.12) | copy-start | bytes 221188
  23.3 3.3 %collective-permute-start.6 = (bf16[8,4,80,128]{3,2,1,0:T(8,128)(2,1)S(1)}, bf16[8,4,80,128]{3,2,1,0:T(8,128)(2,1)S(1)}, u32[]{:S(2)}, u32[]{:S(2)}) collective-permute-start(bf16[8,4,80,128]{3,2,1,0:T(8,128)(2,1)S(1)} %constant_dynamic-update-slice_fusion), channel_id=1, source_target_pairs={{0,1},{1,0},{2,3},{3,2},{4,5},{5,4},{6,7},{7,6},{8,9},{9,8},{10,11... | collective-permute-start | bytes 1966088 | tf_op jit(solution)/shard_map/ppermute | solution.py:323
  23.3 14.3 %collective-permute-start.12 = (bf16[2,4,80,128]{3,2,1,0:T(8,128)(2,1)S(1)}, bf16[2,4,80,128]{3,2,1,0:T(8,128)(2,1)S(1)}, u32[]{:S(2)}, u32[]{:S(2)}) collective-permute-start(bf16[2,4,80,128]{3,2,1,0:T(8,128)(2,1)S(1)} %maximum_bitcast_fusion.1), channel_id=1, source_target_pairs={{0,2},{1,3},{2,0},{3,1},{4,6},{5,7},{6,4},{7,5},{8,10},{9,11},{10,... | collective-permute-start | bytes 491528 | tf_op jit(solution)/shard_map/ppermute | solution.py:323
  24.8 12.8 %collective-permute-start.13 = (bf16[2,4,80,128]{3,2,1,0:T(8,128)(2,1)S(1)}, bf16[2,4,80,128]{3,2,1,0:T(8,128)(2,1)S(1)}, u32[]{:S(2)}, u32[]{:S(2)}) collective-permute-start(bf16[2,4,80,128]{3,2,1,0:T(8,128)(2,1)S(1)} %maximum_bitcast_fusion.1), channel_id=1, source_target_pairs={{0,4},{1,5},{2,6},{3,7},{4,0},{5,1},{6,2},{7,3},{8,12},{9,13},{10,... | collective-permute-start | bytes 491528 | tf_op jit(solution)/shard_map/ppermute | solution.py:323
  32.0 16.6 %all-to-all-start = ((bf16[16,72,128]{2,1,0:T(8,128)(2,1)}), bf16[16,72,128]{2,1,0:T(8,128)(2,1)S(1)}, u32[]{:S(2)}, u32[]{:S(2)}) async-start(bf16[16,72,128]{2,1,0:T(8,128)(2,1)} %get-tuple-element.51), calls=%async_computation | async-start | bytes 589824 | tf_op jit(solution)/shard_map/all_to_all | solution.py:320
  37.6 3.5 %copy-start.1 = (bf16[2,4,80,128]{3,2,1,0:T(8,128)(2,1)}, bf16[2,4,80,128]{3,2,1,0:T(8,128)(2,1)S(1)}, u32[]{:S(2)}) copy-start(bf16[2,4,80,128]{3,2,1,0:T(8,128)(2,1)S(1)} %collective-permute-done.12) | copy-start | bytes 491524
  37.7 3.5 %copy-start.2 = (bf16[2,4,80,128]{3,2,1,0:T(8,128)(2,1)}, bf16[2,4,80,128]{3,2,1,0:T(8,128)(2,1)S(1)}, u32[]{:S(2)}) copy-start(bf16[2,4,80,128]{3,2,1,0:T(8,128)(2,1)S(1)} %collective-permute-done.13) | copy-start | bytes 491524
  37.7 6.8 %collective-permute-start.14 = (bf16[1,4,80,128]{3,2,1,0:T(8,128)(2,1)S(1)}, bf16[1,4,80,128]{3,2,1,0:T(8,128)(2,1)S(1)}, u32[]{:S(2)}, u32[]{:S(2)}) collective-permute-start(bf16[1,4,80,128]{3,2,1,0:T(8,128)(2,1)S(1)} %slice.20), channel_id=1, source_target_pairs={{0,2},{1,3},{2,0},{3,1},{4,6},{5,7},{6,4},{7,5},{8,10},{9,11},{10,... | collective-permute-start | bytes 245768 | tf_op jit(solution)/shard_map/ppermute | solution.py:323
  39.7 7.2 %collective-permute-start.15 = (bf16[1,4,80,128]{3,2,1,0:T(8,128)(2,1)S(1)}, bf16[1,4,80,128]{3,2,1,0:T(8,128)(2,1)S(1)}, u32[]{:S(2)}, u32[]{:S(2)}) collective-permute-start(bf16[1,4,80,128]{3,2,1,0:T(8,128)(2,1)S(1)} %slice.21), channel_id=1, source_target_pairs={{0,4},{1,5},{2,6},{3,7},{4,0},{5,1},{6,2},{7,3},{8,12},{9,13},{10,... | collective-permute-start | bytes 245768 | tf_op jit(solution)/shard_map/ppermute | solution.py:323
  50.1 1.3 %collective-permute-start.7 = (bf16[72,512]{1,0:T(8,128)(2,1)S(1)}, bf16[72,512]{1,0:T(8,128)(2,1)S(1)}, u32[]{:S(2)}, u32[]{:S(2)}) collective-permute-start(bf16[72,512]{1,0:T(8,128)(2,1)S(1)} %get-tuple-element.60), channel_id=1, source_target_pairs={{0,1},{1,0},{2,3},{3,2},{4,5},{5,4},{6,7},{7,6},{8,9},{9,8},{10,11... | collective-permute-start | bytes 221192 | tf_op jit(solution)/shard_map/ppermute | solution.py:323
  50.3 11.3 %collective-permute-start.16 = (bf16[4,4,80,128]{3,2,1,0:T(8,128)(2,1)S(1)}, bf16[4,4,80,128]{3,2,1,0:T(8,128)(2,1)S(1)}, u32[]{:S(2)}, u32[]{:S(2)}) collective-permute-start(bf16[4,4,80,128]{3,2,1,0:T(8,128)(2,1)S(1)} %get-tuple-element.70), channel_id=1, source_target_pairs={{0,1},{1,0},{2,3},{3,2},{4,5},{5,4},{6,7},{7,6},{8,9},{9,8},{10,11... | collective-permute-start | bytes 983048 | tf_op jit(solution)/shard_map/ppermute | solution.py:323
  50.8 10.8 %collective-permute-start.17 = (bf16[4,4,80,128]{3,2,1,0:T(8,128)(2,1)S(1)}, bf16[4,4,80,128]{3,2,1,0:T(8,128)(2,1)S(1)}, u32[]{:S(2)}, u32[]{:S(2)}) collective-permute-start(bf16[4,4,80,128]{3,2,1,0:T(8,128)(2,1)S(1)} %get-tuple-element.71), channel_id=1, source_target_pairs={{0,1},{1,0},{2,3},{3,2},{4,5},{5,4},{6,7},{7,6},{8,9},{9,8},{10,11... | collective-permute-start | bytes 983048 | tf_op jit(solution)/shard_map/ppermute | solution.py:323
  51.5 6.5 %collective-permute-start.8 = (bf16[72,512]{1,0:T(8,128)(2,1)S(1)}, bf16[72,512]{1,0:T(8,128)(2,1)S(1)}, u32[]{:S(2)}, u32[]{:S(2)}) collective-permute-start(bf16[72,512]{1,0:T(8,128)(2,1)S(1)} %add_convert_fusion.2), channel_id=1, source_target_pairs={{0,8},{1,9},{2,10},{3,11},{4,12},{5,13},{6,14},{7,15},{8,0},{9,1},... | collective-permute-start | bytes 221192 | tf_op jit(solution)/shard_map/ppermute | solution.py:323
  52.6 15.4 %all-to-all-start.1 = ((bf16[16,72,128]{2,1,0:T(8,128)(2,1)}), bf16[16,72,128]{2,1,0:T(8,128)(2,1)S(1)}, u32[]{:S(2)}, u32[]{:S(2)}) async-start(bf16[16,72,128]{2,1,0:T(8,128)(2,1)} %get-tuple-element.61), calls=%async_computation.1 | async-start | bytes 589824 | tf_op jit(solution)/shard_map/all_to_all | solution.py:320
  58.1 7.7 %collective-permute-start.10 = (bf16[72,512]{1,0:T(8,128)(2,1)S(1)}, bf16[72,512]{1,0:T(8,128)(2,1)S(1)}, u32[]{:S(2)}, u32[]{:S(2)}) collective-permute-start(bf16[72,512]{1,0:T(8,128)(2,1)S(1)} %add_convert_fusion.1), channel_id=1, source_target_pairs={{0,4},{1,5},{2,6},{3,7},{4,0},{5,1},{6,2},{7,3},{8,12},{9,13},{10,... | collective-permute-start | bytes 221192 | tf_op jit(solution)/shard_map/ppermute | solution.py:323
  58.1 9.8 %collective-permute-start.11 = (bf16[72,512]{1,0:T(8,128)(2,1)S(1)}, bf16[72,512]{1,0:T(8,128)(2,1)S(1)}, u32[]{:S(2)}, u32[]{:S(2)}) collective-permute-start(bf16[72,512]{1,0:T(8,128)(2,1)S(1)} %add_convert_fusion.1), channel_id=1, source_target_pairs={{0,6},{1,7},{2,4},{3,5},{4,2},{5,3},{6,0},{7,1},{8,14},{9,15},{10,... | collective-permute-start | bytes 221192 | tf_op jit(solution)/shard_map/ppermute | solution.py:323
  60.0 8.0 %collective-permute-start.9 = (bf16[72,512]{1,0:T(8,128)(2,1)S(1)}, bf16[72,512]{1,0:T(8,128)(2,1)S(1)}, u32[]{:S(2)}, u32[]{:S(2)}) collective-permute-start(bf16[72,512]{1,0:T(8,128)(2,1)S(1)} %add_convert_fusion.1), channel_id=1, source_target_pairs={{0,2},{1,3},{2,0},{3,1},{4,6},{5,7},{6,4},{7,5},{8,10},{9,11},{10,... | collective-permute-start | bytes 221192 | tf_op jit(solution)/shard_map/ppermute | solution.py:323
  68.0 1.3 %collective-permute-start.18 = (bf16[72,512]{1,0:T(8,128)(2,1)S(1)}, bf16[72,512]{1,0:T(8,128)(2,1)S(1)}, u32[]{:S(2)}, u32[]{:S(2)}) collective-permute-start(bf16[72,512]{1,0:T(8,128)(2,1)S(1)} %add_convert_fusion), channel_id=1, source_target_pairs={{0,1},{1,0},{2,3},{3,2},{4,5},{5,4},{6,7},{7,6},{8,9},{9,8},{10,11... | collective-permute-start | bytes 221192 | tf_op jit(solution)/shard_map/ppermute | solution.py:323
